TPU v7x, 128 devices: a whole 4x4x4 slice. The times are simulated.
128 devices in a mesh: row: 16 (over x, y), col: 8 (over z, core).
Axes of the slice: x: 4, y: 4, z: 4, core: 2. Of those that a mesh axis runs over, the one named last changes fastest.
Arguments:
- amp_store: bfloat16 [32768, 1024], P(('row', 'col')), may hold values from -6 to 6
- store_map: int32 [32768], P(('row', 'col')), may hold values from 0 to 32767, as said below
- integrals: bfloat16 [32768, 32768], P('row', 'col'), may hold values from -0.09375 to 0.09375
- occ_irrep: int32 [100], replicated, may hold values from 0 to 7
- virt_irrep: int32 [800], replicated, may hold values from 0 to 7
- occ_orbs: int32 [2, 1024], replicated, may hold values from 0 to 99
- k_orbs: int32 [2, 32768], P(None, 'col'), may hold values from 0 to 799
- m_orbs: int32 [2, 32768], P(None, 'row'), may hold values from 0 to 799
Outputs:
- ladder: bfloat16 [32768, 1024], P('row', 'col')
Inputs may be any that keep to these rules, and one draw needn't show every extreme that they name: store_map is a permutation. Grid position k belongs to the block of device (r, c) with c = k // 4096 and r = (k % 4096) // 256; the stored rows of device s = r' * 8 + c' (its shard of amp_store) send exactly 2 rows to every device's block, and within block (r, c) those rows fill positions s * 2 to s * 2 + 1.
All inputs are finite; a program needn't handle non-finite values.
Results may differ from a plain program's by a relative error of at most 0.001.
Values may be sent and summed in bfloat16 or wider, within the bound.
No kernel may reach another device: no remote copies, remote signals or barrier semaphores. Data moves between devices by JAX's collectives and lax.ppermute only.
A program may use at most 192 MiB of HBM per device.

v0:
```python
import jax
import jax.numpy as jnp
from jax import lax
from jax.sharding import PartitionSpec as P


def pair_irrep(labels, orbitals):
    return jnp.bitwise_xor(labels[orbitals[0]], labels[orbitals[1]])


def redistribute(buffer):
    return lax.all_to_all(buffer, ("row", "col"), split_axis=0, concat_axis=0, tiled=True)


def body(amp_store, store_map, integrals, occ_irrep, virt_irrep, occ_orbs, k_orbs, m_orbs):
    row_count = lax.axis_size("row")
    col_count = lax.axis_size("col")
    dev_count = row_count * col_count
    stored = amp_store.shape[0]
    slot_count = stored // dev_count
    kblock = k_orbs.shape[1]
    my_row = lax.axis_index("row")
    my_col = lax.axis_index("col")
    myself = my_row * col_count + my_col
    occ_sym = pair_irrep(occ_irrep, occ_orbs)
    k_sym = pair_irrep(virt_irrep, k_orbs)
    m_sym = pair_irrep(virt_irrep, m_orbs)
    naught = jnp.zeros((), amp_store.dtype)
    owner_col = store_map // kblock
    owner_row = store_map % kblock // stored
    within = store_map % stored - myself * slot_count
    place = (owner_row * col_count + owner_col) * slot_count + within
    ordered = jnp.zeros_like(amp_store).at[place].set(amp_store)
    grid_rows = redistribute(ordered)
    own_sym = lax.dynamic_slice_in_dim(k_sym, my_row * stored, stored)
    masked = jnp.where(own_sym[:, None] == occ_sym[None, :], grid_rows, naught)
    screened = jnp.where(m_sym[:, None] == k_sym[None, :], integrals, naught)
    partial_sum = jnp.dot(
        screened,
        lax.all_gather(masked, "row", axis=0, tiled=True),
        preferred_element_type=jnp.float32,
    )
    return lax.psum_scatter(partial_sum, "col", scatter_dimension=1, tiled=True).astype(
        jnp.bfloat16
    )


def solution(mesh):
    in_specs = (
        P(("row", "col"), None),
        P(("row", "col")),
        P("row", "col"),
        P(),
        P(),
        P(),
        P(None, "col"),
        P(None, "row"),
    )
    out_specs = P("row", "col")
    return jax.shard_map(body, mesh=mesh, in_specs=in_specs, out_specs=out_specs, check_vma=False)
```

profile of v0, /device:TPU:1, one launch (start us, length us, event | category | flops | bytes accessed | tf_op | source)
XLA Modules:
  0.0 227.8 jit_solution(790989512550864099)
XLA Ops:
  6.5 0.0 copy-start
  6.5 0.7 compare_select_fusion.9
  7.3 2.3 %scatter_custom_fusion = bf16[256,1024]{1,0:T(8,128)(2,1)S(1)} fusion(s32[256]{0:T(256)S(1)} %compare_select_fusion.9, bf16[256,1024]{1,0:T(8,128)(2,1)} %param.8, bf16[]{:T(256)} %constant.62.clone.1), kind=kCustom, calls=%fused_computation.13 | custom fusion | bytes 524800 | tf_op jit(solution)/shard_map/scatter | solution.py:33
  9.6 1.0 all_to_all.8
  10.6 11.5 %all-to-all-start = ((bf16[128,2,1024]{2,1,0:T(2,128)(2,1)}), bf16[128,2,1024]{2,1,0:T(2,128)(2,1)S(1)}, u32[]{:S(2)}, u32[]{:S(2)}) async-start(bf16[128,2,1024]{2,1,0:T(2,128)(2,1)} %all_to_all.8), calls=%async_computation | async-start | bytes 1048576 | tf_op jit(solution)/shard_map/all_to_all | solution.py:12
  22.1 0.0 all-gather.2.cloned.1.call-start
  22.1 0.8 compare_select_fusion.7
  22.9 0.9 compare_select_fusion.3
  23.8 5.9 %gather_fusion.5 = s32[1024]{0:T(1024)S(1)} fusion(s32[100]{0:T(128)} %param.11, s32[1024]{0:T(1024)S(1)} %broadcast_clamp_fusion.4), kind=kCustom, calls=%fused_computation.5 | custom fusion | bytes 12288 | tf_op jit(solution)/shard_map/gather | solution.py:8
  29.7 5.9 %gather_fusion.4 = s32[1024]{0:T(1024)S(1)} fusion(s32[100]{0:T(128)} %param.11, s32[1024]{0:T(1024)S(1)} %broadcast_clamp_fusion.5), kind=kCustom, calls=%fused_computation.4 | custom fusion | bytes 12288 | tf_op jit(solution)/shard_map/gather | solution.py:8
  35.5 0.0 copy-done
  35.5 0.0 copy-start.1
  35.6 16.7 %gather_fusion.3 = s32[4096]{0:T(1024)S(1)} fusion(s32[800]{0:T(1024)S(1)} %copy-done, s32[4096]{0:T(1024)S(1)} %broadcast_clamp_fusion), kind=kCustom, calls=%fused_computation.3 | custom fusion | bytes 49152 | tf_op jit(solution)/shard_map/gather | solution.py:8
  52.3 16.7 %gather_fusion.2 = s32[4096]{0:T(1024)S(1)} fusion(s32[800]{0:T(1024)S(1)} %copy-done, s32[4096]{0:T(1024)S(1)} %broadcast_clamp_fusion.1), kind=kCustom, calls=%fused_computation.2 | custom fusion | bytes 49152 | tf_op jit(solution)/shard_map/gather | solution.py:8
  69.0 0.1 dynamic_slice.3
  69.1 0.0 all-to-all-done
  69.1 0.2 all_to_all.10
  69.3 1.0 compare_select_fusion.2
  70.3 0.0 all-gather.2.cloned.1.call-update
  70.3 0.0 reduce-scatter.2.cloned.1.call-start
  70.3 0.0 copy-done.1
  70.4 8.6 %gather_fusion.1 = s32[2048]{0:T(1024)S(1)} fusion(s32[800]{0:T(1024)S(1)} %copy-done, s32[2048]{0:T(1024)S(1)} %broadcast_clamp_fusion.2), kind=kCustom, calls=%fused_computation.1 | custom fusion | bytes 24576 | tf_op jit(solution)/shard_map/gather | solution.py:8
  79.0 8.6 %gather_fusion = s32[2048]{0:T(1024)S(1)} fusion(s32[800]{0:T(1024)S(1)} %copy-done, s32[2048]{0:T(1024)S(1)} %broadcast_clamp_fusion.3), kind=kCustom, calls=%fused_computation | custom fusion | bytes 24576 | tf_op jit(solution)/shard_map/gather | solution.py:8
  87.6 54.9 %all-gather.2.cloned.1.call-done = bf16[4096,1024]{1,0:T(8,128)(2,1)} async-done(((bf16[256,1024]{1,0:T(8,128)(2,1)}), bf16[4096,1024]{1,0:T(8,128)(2,1)}) %all-gather.2.cloned.1.call-update) | async-done | bytes 8388624 | tf_op jit(solution)/shard_map/all_gather | solution.py:40
  142.5 24.6 %fusion = f32[2048,1024]{1,0:T(8,128)} fusion(bf16[4096,1024]{1,0:T(8,128)(2,1)} %all-gather.2.cloned.1.call-done, bf16[2048,4096]{1,0:T(8,128)(2,1)} %param.10, s32[4096]{0:T(1024)S(1)} %xor.22, s32[2048]{0:T(1024)S(1)} %xor.21), kind=kOutput, calls=%fused_computation.8 | convolution fusion | flops 17196646400 | bytes 33579008 | tf_op jit(solution)/shard_map/dot_general | solution.py:38
  167.1 0.0 reduce-scatter.2.cloned.1.call-update
  167.1 51.8 %reduce-scatter.2.cloned.1.call-done = f32[2048,128]{1,0:T(8,128)} async-done(((f32[2048,1024]{1,0:T(8,128)}), f32[2048,128]{1,0:T(8,128)}) %reduce-scatter.2.cloned.1.call-update) | async-done | bytes 1048592 | tf_op jit(solution)/shard_map/reduce_scatter | solution.py:43
  218.9 2.1 convert_element_type.3
  (10 shorter events, 0.1 us)
Async XLA Ops:
  6.5 29.0 %copy-start = (s32[800]{0:T(1024)S(1)}, s32[800]{0:T(1024)}, u32[]{:S(2)}) copy-start(s32[800]{0:T(1024)} %param.12) | copy-start | bytes 9604
  10.6 58.5 %all-to-all-start = ((bf16[128,2,1024]{2,1,0:T(2,128)(2,1)}), bf16[128,2,1024]{2,1,0:T(2,128)(2,1)S(1)}, u32[]{:S(2)}, u32[]{:S(2)}) async-start(bf16[128,2,1024]{2,1,0:T(2,128)(2,1)} %all_to_all.8), calls=%async_computation | async-start | bytes 1048576 | tf_op jit(solution)/shard_map/all_to_all | solution.py:12
  22.1 120.5 %all-gather.2.cloned.1.call-start = ((), (), s32[]{:S(2)}) async-start(), calls=%async_computation.2 | async-start | bytes 8912896 | tf_op jit(solution)/shard_map/all_gather | solution.py:40
  35.5 34.8 %copy-start.1 = (s32[2,2048]{1,0:T(2,128)S(1)}, s32[2,2048]{1,0:T(2,128)}, u32[]{:S(2)}) copy-start(s32[2,2048]{1,0:T(2,128)} %param.15) | copy-start | bytes 49156
  70.3 148.7 %reduce-scatter.2.cloned.1.call-start = ((), (), s32[]{:S(2)}) async-start(), calls=%async_computation.3 | async-start | bytes 9437184 | tf_op jit(solution)/shard_map/reduce_scatter | solution.py:43
Sparse Core Ops, SparseCore 0:
  70.4 72.0 all-gather.1
  167.2 51.6 reduce-scatter.1
where the time goes:
time: 228 us
  waiting for transfers between devices  107 us (47%)
  local copies, waits for them, and re-layouts  65.8 us (29%)
  matrix products  24.6 us (11%)
  between operations  13.6 us (6%)
  starting transfers between devices  11.6 us (5%)
  other arithmetic  5.5 us (2%)
    gather x6, local copies, waits for them, and re-layouts, pair_irrep(): return jnp.bitwise_xor(labels[orbitals[0]], labels[orbitals[1]])  62.2 us
    all_gather x1, waiting for transfers between devices, body(): lax.all_gather(masked, 'row', axis=0, tiled=True)  54.9 us
    reduce_scatter x1, waiting for transfers between devices, body(): lax.psum_scatter(partial_sum, 'col', scatter_dimension=1, tiled=True)  51.8 us
    dot_general x1, matrix products, body(): jnp.dot(screened, lax.all_gather(masked, 'row', axis=0, tiled=True), pref...  24.6 us
    all_to_all x1, starting transfers between devices, redistribute(): lax.all_to_all(buffer, ('row', 'col'), split_axis=0, concat_axis=0, tiled...  11.5 us
  transfers between devices with their start and end apart: 3, of which 2 were waited for; matrix products, arithmetic and copies ran while one was open for 28% of the time, Pallas kernels for 0%

commit v1 on v0

v1 whole, which is shorter than its diff:
```python
import functools

import jax
import jax.numpy as jnp
from jax import lax
from jax.experimental import pallas as pl
from jax.experimental.pallas import tpu as pltpu
from jax.sharding import PartitionSpec as P

BF16 = jnp.bfloat16
F32 = jnp.float32
I32 = jnp.int32
LANES = 128
CAP = 32
TM = 256
VMEM_LIMIT = 48 * 1024 * 1024


def pack_labels(labels):
    word = labels[0:1, :]
    for i in range(1, labels.shape[0]):
        word = word | (labels[i : i + 1, :] << (4 * i))
    return jnp.broadcast_to(word, (8, LANES))


def look_up(packed, orbitals):
    orbitals = jnp.broadcast_to(orbitals, (8, LANES))
    word = jnp.take_along_axis(packed, orbitals & (LANES - 1), axis=1)
    return (word >> ((orbitals >> 7) << 2)) & 7


def pair_symbols(packed, orbs_ref, start):
    lanes = slice(start, start + LANES)
    return look_up(packed, orbs_ref[0:1, lanes]) ^ look_up(packed, orbs_ref[1:2, lanes])


def as_column(symbols):
    row = jnp.broadcast_to(symbols[0:1, :].astype(F32), (LANES, LANES))
    return jnp.transpose(row)


def symbols_kernel(
    occ_ref, virt_ref, occ_orbs, k_orbs, m_orbs, own_orbs, occ_out, rank_out, k_out, m_out, own_out, most_out
):
    occ = pack_labels(occ_ref[0:1, :])
    virt = pack_labels(virt_ref[0:7, :])
    first = lax.broadcasted_iota(I32, (LANES, LANES), 0)
    second = lax.broadcasted_iota(I32, (LANES, LANES), 1)
    most = jnp.zeros((1, LANES), I32)
    for start in range(0, occ_orbs.shape[1], LANES):
        sym = pair_symbols(occ, occ_orbs, start)
        occ_out[:, start : start + LANES] = sym
        same = as_column(sym) == jnp.broadcast_to(sym[0:1, :].astype(F32), (LANES, LANES))
        earlier = jnp.where(same & (first < second), 1.0, 0.0)
        rank = jnp.sum(earlier, axis=0, keepdims=True).astype(I32)
        most = jnp.maximum(most, rank)
        rank_out[:, start : start + LANES] = jnp.broadcast_to(rank, (8, LANES))
    most_out[0, 0] = jnp.max(most)
    for start in range(0, k_orbs.shape[1], LANES):
        sym = pair_symbols(virt, k_orbs, start).astype(F32)
        k_out[:, start : start + LANES] = jnp.concatenate([sym, sym], axis=0).astype(BF16)
    for start in range(0, m_orbs.shape[1], LANES):
        m_out[start : start + LANES, :] = as_column(pair_symbols(virt, m_orbs, start)).astype(BF16)
    for start in range(0, own_orbs.shape[1], LANES):
        own_out[start : start + LANES, :] = as_column(pair_symbols(virt, own_orbs, start)).astype(I32)


def compact_kernel(copies, pass_ref, rows_ref, own_ref, occ_ref, rank_ref, out_ref):
    n, pairs = rows_ref.shape
    cols = pairs // LANES
    i = lax.broadcasted_iota(I32, (n, n), 0)
    j = lax.broadcasted_iota(I32, (n, n), 1)
    wanted = ((i >> 1) & 7) * 32 + (i >> 4) * 2 + (i & 1)
    order = jnp.where(j == wanted, 1.0, 0.0).astype(BF16)
    rows = jnp.dot(order, rows_ref[...], preferred_element_type=F32)
    base = pass_ref[0] * CAP
    slot = lax.broadcasted_iota(I32, (CAP, LANES), 0) + base
    own = own_ref[...]
    for c in range(cols):
        lanes = slice(c * LANES, (c + 1) * LANES)
        keep = own == jnp.broadcast_to(occ_ref[0:1, lanes], (n, LANES))
        kept = jnp.where(keep, rows[:, lanes], 0.0).astype(BF16)
        pick = jnp.where(slot == jnp.broadcast_to(rank_ref[0:1, lanes], (CAP, LANES)), 1.0, 0.0).astype(BF16)
        part = lax.dot_general(kept, pick, (((1,), (1,)), ((), ())), preferred_element_type=F32).astype(BF16)
        for r in range(copies):
            out_ref[r, :, c * CAP : (c + 1) * CAP] = part


def product_kernel(core_ref, amp_ref, int_ref, k_ref, m_ref, keep_ref, send_ref, kept):
    depth, width = amp_ref.shape
    block = depth // 16

    @pl.when(pl.program_id(0) == 0)
    def _():
        for r in range(16):
            for source in range(16):
                kept[r * block + source * 16 : r * block + source * 16 + 16, :] = amp_ref[
                    source * block + r * 16 : source * block + r * 16 + 16, :
                ]

    m_sym = m_ref[...]
    chunk = 1024
    total = jnp.zeros((m_ref.shape[0], width), F32)
    for at in range(0, depth, chunk):
        parts = []
        for lane in range(at, at + chunk, LANES):
            lanes = slice(lane, lane + LANES)
            same = m_sym == jnp.broadcast_to(k_ref[0:1, lanes], m_sym.shape)
            parts.append(jnp.where(same, int_ref[:, lanes], jnp.zeros((), BF16)))
        screened = jnp.concatenate(parts, axis=1)
        total += jnp.dot(screened, kept[at : at + chunk, :], preferred_element_type=F32)
    turned = jnp.transpose(total)
    even = core_ref[0] == 0
    for z in range(4):
        low = turned[z * 2 * CAP : z * 2 * CAP + CAP, :]
        high = turned[z * 2 * CAP + CAP : z * 2 * CAP + 2 * CAP, :]
        keep_ref[z] = jnp.where(even, low, high)
        send_ref[z] = jnp.where(even, high, low)


def share_kernel(z_ref, keep_ref, got_ref, *out_refs):
    for step, out_ref in enumerate(out_refs):
        z = (z_ref[0] + step) % 4
        out_ref[...] = keep_ref[z] + got_ref[z]


def expand_kernel(at_ref, a_ref, b_ref, c_ref, d_ref, m_ref, occ_ref, rank_ref, out_ref):
    lanes = pl.ds(pl.multiple_of(at_ref[0] * LANES, LANES), LANES)
    total = (a_ref[...] + b_ref[...] + c_ref[...] + d_ref[...]).astype(BF16)
    slot = lax.broadcasted_iota(I32, (CAP, LANES), 0) + at_ref[1] * CAP
    pick = jnp.where(slot == jnp.broadcast_to(rank_ref[0:1, lanes], (CAP, LANES)), 1.0, 0.0).astype(BF16)
    wide = lax.dot_general(total, pick, (((0,), (0,)), ((), ())), preferred_element_type=F32)
    same = m_ref[...].astype(F32) == jnp.broadcast_to(occ_ref[0:1, lanes].astype(F32), wide.shape)
    out_ref[...] = jnp.where(same, wide, 0.0).astype(BF16)


def params():
    return pltpu.CompilerParams(vmem_limit_bytes=VMEM_LIMIT)


def whole():
    return pl.BlockSpec(memory_space=pltpu.VMEM)


def scalars():
    return pl.BlockSpec(memory_space=pltpu.SMEM)


def body(amp_store, store_map, integrals, occ_irrep, virt_irrep, occ_orbs, k_orbs, m_orbs):
    rows = lax.axis_size("row")
    cols = lax.axis_size("col")
    stored, pairs = amp_store.shape
    kblock = k_orbs.shape[1]
    m_dev = m_orbs.shape[1]
    my_row = lax.axis_index("row")
    my_col = lax.axis_index("col")
    shape = jax.ShapeDtypeStruct

    place = (store_map // kblock) * (rows * 2) + ((store_map % kblock) // stored) * 2 + store_map % 2
    order = (jnp.arange(stored, dtype=I32)[:, None] == place[None, :]).astype(BF16)
    ordered = jnp.dot(order, amp_store, preferred_element_type=F32).astype(BF16)
    column_rows = lax.all_to_all(ordered, "col", split_axis=0, concat_axis=0, tiled=True)

    own_orbs = lax.dynamic_slice_in_dim(k_orbs.reshape(2, rows, stored), my_row * 16, 16, axis=2).reshape(2, stored)
    occ_lab = jnp.pad(occ_irrep, (0, LANES - occ_irrep.shape[0])).reshape(1, LANES)
    virt_lab = jnp.pad(virt_irrep, (0, 8 * LANES - virt_irrep.shape[0])).reshape(8, LANES)
    occ_sym, rank, k_sym, m_sym, own_sym, most = pl.pallas_call(
        symbols_kernel,
        out_shape=(
            shape((8, pairs), I32),
            shape((8, pairs), I32),
            shape((16, kblock), BF16),
            shape((m_dev, LANES), BF16),
            shape((stored, LANES), I32),
            shape((1, 1), I32),
        ),
        in_specs=[whole()] * 6,
        out_specs=(whole(),) * 5 + (scalars(),),
        compiler_params=params(),
        name="symbols",
    )(occ_lab, virt_lab, occ_orbs, k_orbs, m_orbs, own_orbs)

    def one_pass(step):
        width = cols * CAP
        compact = pl.pallas_call(
            functools.partial(compact_kernel, rows),
            out_shape=shape((rows, stored, width), BF16),
            in_specs=[scalars()] + [whole()] * 4,
            out_specs=whole(),
            compiler_params=params(),
            name="compact",
        )(step.reshape(1), column_rows, own_sym, occ_sym, rank)
        gathered = lax.all_to_all(
            compact.reshape(rows * stored, width), "row", split_axis=0, concat_axis=0, tiled=True
        )
        keep, send = pl.pallas_call(
            product_kernel,
            grid=(m_dev // TM,),
            out_shape=(shape((4, CAP, m_dev), F32),) * 2,
            in_specs=[
                scalars(),
                pl.BlockSpec((kblock, width), lambda i: (0, 0)),
                pl.BlockSpec((TM, kblock), lambda i: (i, 0)),
                pl.BlockSpec((16, kblock), lambda i: (0, 0)),
                pl.BlockSpec((TM, LANES), lambda i: (i, 0)),
            ],
            out_specs=(pl.BlockSpec((4, CAP, TM), lambda i: (0, 0, i)),) * 2,
            scratch_shapes=[pltpu.VMEM((kblock, width), BF16)],
            compiler_params=params(),
            name="product",
        )((my_col % 2).reshape(1), gathered, integrals, k_sym, m_sym)
        got = lax.ppermute(send, "col", [(i, i ^ 1) for i in range(cols)])
        shares = pl.pallas_call(
            share_kernel,
            out_shape=(shape((CAP, m_dev), F32),) * 4,
            in_specs=[scalars(), whole(), whole()],
            out_specs=(whole(),) * 4,
            compiler_params=params(),
            name="share",
        )((my_col // 2).reshape(1), keep, got)
        sums = [shares[0]]
        for distance in range(1, 4):
            hops = [(i, (i + 2 * distance) % cols) for i in range(cols)]
            sums.append(lax.ppermute(shares[distance], "col", hops))
        return pl.pallas_call(
            expand_kernel,
            out_shape=shape((m_dev, LANES), BF16),
            in_specs=[scalars()] + [whole()] * 7,
            out_specs=whole(),
            compiler_params=params(),
            name="expand",
        )(jnp.stack([my_col, step]), *sums, m_sym, occ_sym, rank)

    passes = most[0, 0] // CAP + 1
    first = one_pass(jnp.zeros((), I32))
    return lax.while_loop(
        lambda state: state[0] < passes,
        lambda state: (state[0] + 1, state[1] + one_pass(state[0])),
        (jnp.ones((), I32), first),
    )[1]


def solution(mesh):
    in_specs = (
        P(("row", "col"), None),
        P(("row", "col")),
        P("row", "col"),
        P(),
        P(),
        P(),
        P(None, "col"),
        P(None, "row"),
    )
    out_specs = P("row", "col")
    return jax.shard_map(body, mesh=mesh, in_specs=in_specs, out_specs=out_specs, check_vma=False)
```

time: 228 us -> 93.9 us (0.41)
  local copies, waits for them, and re-layouts: 65.8 us -> 2.7 us
  waiting for transfers between devices: 107 us -> 46.2 us
  matrix products: 24.6 us -> 1.1 us
  Pallas kernels: 0 us -> 18.7 us
  between operations: 13.6 us -> 2.74 us
  starting transfers between devices: 11.6 us -> 21.1 us
  other arithmetic: 5.5 us -> 0.83 us
    gather x6 -> x0, local copies, waits for them, and re-layouts: 62.2 us -> none  [pair_irrep(): return jnp.bitwise_xor(labels[orbitals[0]], labels[orbitals[1]])]
    all_gather x1 -> x0, waiting for transfers between devices: 54.9 us -> none  [body(): lax.all_gather(masked, 'row', axis=0, tiled=True)]
    reduce_scatter x1 -> x0, waiting for transfers between devices: 51.8 us -> none  [body(): lax.psum_scatter(partial_sum, 'col', scatter_dimension=1, tiled=True)]
    all_to_all x1 -> x2, waiting for transfers between devices: 0.01 us -> 34.5 us  [the longest x1 26.4 us: one_pass(): lax.all_to_all(compact.reshape(rows * stored, width), 'row', split_axis=0...]
    dot_general x1, matrix products: 24.6 us -> 1.1 us  [body(): ordered = jnp.dot(order, amp_store, preferred_element_type=F32).astype(BF16)]
    pallas_call x0 -> x5, Pallas kernels: none -> 18.7 us  [the longest x1 11.8 us: one_pass(): pl.pallas_call(product_kernel, grid=(m_dev // TM,), out_shape=(shape((4,...]
    ppermute x0 -> x4, waiting for transfers between devices: none -> 11.8 us  [the longest x3 9.29 us: one_pass(): sums.append(lax.ppermute(shares[distance], 'col', hops))]
    ppermute x0 -> x4, starting transfers between devices: none -> 7.52 us  [the longest x1 4.67 us: one_pass(): got = lax.ppermute(send, 'col', [(i, i ^ 1) for i in range(cols)])]
  transfers between devices with their start and end apart: 3 -> 6, of which waited for: 2 -> 6; matrix products, arithmetic and copies ran while one was open for 28% -> 0% of each run, Pallas kernels for 0% -> 1%
where the time goes in v1:
time: 93.9 us; the launch traced here: 93.4 us
  waiting for transfers between devices  46.2 us (49%)
  starting transfers between devices  21.1 us (22%)
  Pallas kernels  18.7 us (20%)
  between operations  2.74 us (3%)
  local copies, waits for them, and re-layouts  2.7 us (3%)
  matrix products  1.1 us (1%)
    all_to_all x1, waiting for transfers between devices, one_pass(): lax.all_to_all(compact.reshape(rows * stored, width), 'row', split_axis=0...  26.4 us
    pallas_call x1, Pallas kernels, one_pass(): pl.pallas_call(product_kernel, grid=(m_dev // TM,), out_shape=(shape((4,...  11.8 us
    ppermute x3, waiting for transfers between devices, one_pass(): sums.append(lax.ppermute(shares[distance], 'col', hops))  9.29 us
    all_to_all x1, waiting for transfers between devices, body(): lax.all_to_all(ordered, 'col', split_axis=0, concat_axis=0, tiled=True)  8.02 us
    all_to_all x1, starting transfers between devices, body(): lax.all_to_all(ordered, 'col', split_axis=0, concat_axis=0, tiled=True)  6.81 us
    all_to_all x1, starting transfers between devices, one_pass(): lax.all_to_all(compact.reshape(rows * stored, width), 'row', split_axis=0...  6.77 us
    ppermute x1, starting transfers between devices, one_pass(): got = lax.ppermute(send, 'col', [(i, i ^ 1) for i in range(cols)])  4.67 us
    pallas_call x1, Pallas kernels, one_pass(): pl.pallas_call(functools.partial(compact_kernel, rows), out_shape=shape((...  3.31 us
  transfers between devices with their start and end apart: 6, of which 6 were waited for; matrix products, arithmetic and copies ran while one was open for 0% of the time, Pallas kernels for 1%

profile of v1, /device:TPU:1, one launch (start us, length us, event | category | flops | bytes accessed | tf_op | source)
XLA Modules:
  0.0 93.4 jit_solution(14235182871714878414)
XLA Ops:
  0.0 0.8 fusion.1
  0.8 0.3 copy-done
  1.1 1.1 %convolution_convert_fusion = bf16[256,1024]{1,0:T(8,128)(2,1)} fusion(bf16[256,1024]{1,0:T(8,128)(2,1)S(1)} %copy-done, s32[256]{0:T(256)S(1)} %fusion.1), kind=kOutput, calls=%fused_computation.1 | convolution fusion | flops 134545408 | bytes 1049600 | tf_op jit(solution)/shard_map/dot_general | solution.py:161
  2.2 6.8 %all-to-all-start.1 = ((bf16[8,32,1024]{2,1,0:T(8,128)(2,1)}), bf16[8,32,1024]{2,1,0:T(8,128)(2,1)S(1)}, u32[]{:S(2)}, u32[]{:S(2)}) async-start(bf16[8,32,1024]{2,1,0:T(8,128)(2,1)} %bitcast.8), calls=%async_computation.1 | async-start | bytes 1048576 | tf_op jit(solution)/shard_map/all_to_all | solution.py:162
  9.0 0.0 copy-done.3
  9.0 0.1 constant_dynamic-slice_fusion
  9.1 0.1 reshape.45.own_orbs
  9.2 1.2 %symbols.1 = (s32[8,1024]{1,0:T(8,128)S(1)}, s32[8,1024]{1,0:T(8,128)S(1)}, bf16[16,4096]{1,0:T(8,128)(2,1)S(1)}, bf16[2048,128]{1,0:T(8,128)(2,1)S(1)}, s32[256,128]{1,0:T(8,128)S(1)}, /*index=5*/s32[1,1]{1,0:T(1,128)}) custom-call(s32[1,128]{1,0:T(1,128)S(1)} %pad_bitcast_fusion.1.occ_ref, s32[8,128]{1,0:T(8,128)S(1)} %pad_bitcast_fusion.virt_ref, ...), custom_call_target="tpu_custom_call" | custom-call | tf_op jit(solution)/shard_map/symbols/pallas_call | solution.py:167
  10.4 0.0 copy-start.12
  10.4 0.0 copy-start.15
  10.4 0.0 copy-start.18
  10.4 0.0 copy-start.6
  10.4 8.0 %all-to-all-done.1 = bf16[8,32,1024]{2,1,0:T(8,128)(2,1)S(1)} async-done(((bf16[8,32,1024]{2,1,0:T(8,128)(2,1)}), bf16[8,32,1024]{2,1,0:T(8,128)(2,1)S(1)}, u32[]{:S(2)}, u32[]{:S(2)}) %all-to-all-start.1) | async-done | bytes 524320 | tf_op jit(solution)/shard_map/all_to_all | solution.py:162
  18.5 3.3 %compact.6 = bf16[16,256,256]{2,1,0:T(8,128)(2,1)} custom-call(s32[1]{0:T(128)} %constant.117.clone.1.pass_ref, bf16[256,1024]{1,0:T(8,128)(2,1)S(1)} %bitcast.34, s32[256,128]{1,0:T(8,128)S(1)} %get-tuple-element.473.own_ref, s32[8,1024]{1,0:T(8,128)S(1)} %get-tuple-element.474.occ_ref, s32[8,1024]{1,0:T(8,128)S(1)} %get-tuple-element.475.rank_ref), custom_call_target="tpu_custom_call" | custom-call | tf_op jit(solution)/shard_map/compact/pallas_call | solution.py:185
  21.8 0.0 copy-done.8
  21.8 6.8 %all-to-all-start.2 = ((bf16[16,256,256]{2,1,0:T(8,128)(2,1)}), bf16[16,256,256]{2,1,0:T(8,128)(2,1)S(1)}, u32[]{:S(2)}, u32[]{:S(2)}) async-start(bf16[16,256,256]{2,1,0:T(8,128)(2,1)} %compact.6), calls=%async_computation.2 | async-start | bytes 4194304 | tf_op jit(solution)/shard_map/all_to_all | solution.py:193
  28.6 26.4 %all-to-all-done.2 = bf16[16,256,256]{2,1,0:T(8,128)(2,1)S(1)} async-done(((bf16[16,256,256]{2,1,0:T(8,128)(2,1)}), bf16[16,256,256]{2,1,0:T(8,128)(2,1)S(1)}, u32[]{:S(2)}, u32[]{:S(2)}) %all-to-all-start.2) | async-done | bytes 2097184 | tf_op jit(solution)/shard_map/all_to_all | solution.py:193
  55.0 0.0 copy-done.6
  55.0 11.8 %product.6 = (f32[4,32,2048]{2,1,0:T(8,128)S(1)}, f32[4,32,2048]{2,1,0:T(8,128)}) custom-call(s32[1]{0:T(128)} %bitcast.7.core_ref, bf16[4096,256]{1,0:T(8,128)(2,1)S(1)} %bitcast.32, bf16[2048,4096]{1,0:T(8,128)(2,1)} %int_ref.1, bf16[16,4096]{1,0:T(8,128)(2,1)S(1)} %get-tuple-element.477.k_ref, bf16[2048,128]{1,0:T(8,128)(2,1)S(1)} %get-tuple-element.478.m_ref), custom_call_target="tpu_custom_call" | custom-call | tf_op jit(solution)/shard_map/product/pallas_call | solution.py:196
  66.9 1.0 %copy-done.1 = f32[4,32,2048]{2,1,0:T(8,128)} copy-done((f32[4,32,2048]{2,1,0:T(8,128)}, f32[4,32,2048]{2,1,0:T(8,128)S(1)}, u32[]{:S(2)}) %copy-start.1) | copy-done | bytes 1048600
  67.8 4.7 %collective-permute-start.4 = (f32[4,32,2048]{2,1,0:T(8,128)}, f32[4,32,2048]{2,1,0:T(8,128)S(1)}, u32[]{:S(2)}, u32[]{:S(2)}) collective-permute-start(f32[4,32,2048]{2,1,0:T(8,128)} %get-tuple-element.341), channel_id=1, source_target_pairs={{0,1},{1,0},{2,3},{3,2},{4,5},{5,4},{6,7},{7,6},{8,9},{9,8},{10,11... | collective-permute-start | bytes 3145736 | tf_op jit(solution)/shard_map/ppermute | solution.py:212
  72.5 2.5 %collective-permute-done.4.got_ref = f32[4,32,2048]{2,1,0:T(8,128)S(1)} collective-permute-done((f32[4,32,2048]{2,1,0:T(8,128)}, f32[4,32,2048]{2,1,0:T(8,128)S(1)}, u32[]{:S(2)}, u32[]{:S(2)}) %collective-permute-start.4) | collective-permute-done | bytes 1048608 | tf_op jit(solution)/shard_map/ppermute | solution.py:212
  75.0 1.2 %copy-done.2 = f32[4,32,2048]{2,1,0:T(8,128)S(1)} copy-done((f32[4,32,2048]{2,1,0:T(8,128)S(1)}, f32[4,32,2048]{2,1,0:T(8,128)}, u32[]{:S(2)}) %copy-start.2) | copy-done | bytes 1048600
  76.2 0.1 share.6
  76.4 0.4 collective-permute-start.5
  76.7 1.8 %collective-permute-start.6 = (f32[32,2048]{1,0:T(8,128)S(1)}, f32[32,2048]{1,0:T(8,128)S(1)}, u32[]{:S(2)}, u32[]{:S(2)}) collective-permute-start(f32[32,2048]{1,0:T(8,128)S(1)} %get-tuple-element.344), channel_id=1, source_target_pairs={{0,4},{1,5},{2,6},{3,7},{4,0},{5,1},{6,2},{7,3},{8,12},{9,13},{10,... | collective-permute-start | bytes 786440 | tf_op jit(solution)/shard_map/ppermute | solution.py:224
  78.5 0.7 collective-permute-start.7
  81.7 0.1 pad_add_fusion.1.at_ref
  81.8 3.9 %collective-permute-done.5.b_ref = f32[32,2048]{1,0:T(8,128)S(1)} collective-permute-done((f32[32,2048]{1,0:T(8,128)S(1)}, f32[32,2048]{1,0:T(8,128)S(1)}, u32[]{:S(2)}, u32[]{:S(2)}) %collective-permute-start.5) | collective-permute-done | bytes 262176 | tf_op jit(solution)/shard_map/ppermute | solution.py:224
  85.8 4.5 %collective-permute-done.6.c_ref = f32[32,2048]{1,0:T(8,128)S(1)} collective-permute-done((f32[32,2048]{1,0:T(8,128)S(1)}, f32[32,2048]{1,0:T(8,128)S(1)}, u32[]{:S(2)}, u32[]{:S(2)}) %collective-permute-start.6) | collective-permute-done | bytes 262176 | tf_op jit(solution)/shard_map/ppermute | solution.py:224
  90.2 0.9 collective-permute-done.7.d_ref
  91.1 2.2 %expand.6 = bf16[2048,128]{1,0:T(8,128)(2,1)} custom-call(s32[2]{0:T(128)S(1)} %pad_add_fusion.1.at_ref, f32[32,2048]{1,0:T(8,128)S(1)} %get-tuple-element.342.a_ref, f32[32,2048]{1,0:T(8,128)S(1)} %collective-permute-done.5.b_ref, f32[32,2048]{1,0:T(8,128)S(1)} %collective-permute-done.6.c_ref, f32[32,2048]{1,0:T(8,128)S(1)} %collective-permute-done.7.d_ref, ...), custom_call_target="tpu_custom_call" | custom-call | tf_op jit(solution)/shard_map/expand/pallas_call | solution.py:225
  (30 shorter events, 0.1 us)
Async XLA Ops:
  0.0 1.1 %copy-start = (bf16[256,1024]{1,0:T(8,128)(2,1)S(1)}, bf16[256,1024]{1,0:T(8,128)(2,1)}, u32[]{:S(2)}) copy-start(bf16[256,1024]{1,0:T(8,128)(2,1)} %param.10) | copy-start | bytes 1572868
  0.0 9.0 %copy-start.3 = (s32[2,4096]{1,0:T(2,128)S(1)}, s32[2,4096]{1,0:T(2,128)}, u32[]{:S(2)}) copy-start(s32[2,4096]{1,0:T(2,128)} %k_orbs.1) | copy-start | bytes 98308
  0.0 9.1 %copy-start.22 = (s32[100]{0:T(128)S(1)}, s32[100]{0:T(128)}, u32[]{:S(2)}) copy-start(s32[100]{0:T(128)} %param.13) | copy-start | bytes 1204
  0.0 9.2 %copy-start.21 = (s32[800]{0:T(1024)S(1)}, s32[800]{0:T(1024)}, u32[]{:S(2)}) copy-start(s32[800]{0:T(1024)} %param.14) | copy-start | bytes 9604
  0.0 9.2 %copy-start.5 = (s32[2,1024]{1,0:T(2,128)S(1)}, s32[2,1024]{1,0:T(2,128)}, u32[]{:S(2)}) copy-start(s32[2,1024]{1,0:T(2,128)} %occ_orbs.1) | copy-start | bytes 24580
  0.0 9.2 %copy-start.4 = (s32[2,2048]{1,0:T(2,128)S(1)}, s32[2,2048]{1,0:T(2,128)}, u32[]{:S(2)}) copy-start(s32[2,2048]{1,0:T(2,128)} %m_orbs.1) | copy-start | bytes 49156
  2.2 16.3 %all-to-all-start.1 = ((bf16[8,32,1024]{2,1,0:T(8,128)(2,1)}), bf16[8,32,1024]{2,1,0:T(8,128)(2,1)S(1)}, u32[]{:S(2)}, u32[]{:S(2)}) async-start(bf16[8,32,1024]{2,1,0:T(8,128)(2,1)} %bitcast.8), calls=%async_computation.1 | async-start | bytes 1048576 | tf_op jit(solution)/shard_map/all_to_all | solution.py:162
  10.4 11.4 %copy-start.12 = (s32[8,1024]{1,0:T(8,128)}, s32[8,1024]{1,0:T(8,128)S(1)}, u32[]{:S(2)}) copy-start(s32[8,1024]{1,0:T(8,128)S(1)} %get-tuple-element.474.occ_ref) | copy-start | bytes 98308
  10.4 11.4 %copy-start.15 = (s32[8,1024]{1,0:T(8,128)}, s32[8,1024]{1,0:T(8,128)S(1)}, u32[]{:S(2)}) copy-start(s32[8,1024]{1,0:T(8,128)S(1)} %get-tuple-element.475.rank_ref) | copy-start | bytes 98308
  10.4 11.4 %copy-start.18 = (s32[256,128]{1,0:T(8,128)}, s32[256,128]{1,0:T(8,128)S(1)}, u32[]{:S(2)}) copy-start(s32[256,128]{1,0:T(8,128)S(1)} %get-tuple-element.473.own_ref) | copy-start | bytes 393220
  10.4 44.6 %copy-start.6 = (bf16[2048,128]{1,0:T(8,128)(2,1)}, bf16[2048,128]{1,0:T(8,128)(2,1)S(1)}, u32[]{:S(2)}) copy-start(bf16[2048,128]{1,0:T(8,128)(2,1)S(1)} %get-tuple-element.478.m_ref) | copy-start | bytes 1572868
  18.5 3.3 %copy-start.8 = (bf16[8,32,1024]{2,1,0:T(8,128)(2,1)}, bf16[8,32,1024]{2,1,0:T(8,128)(2,1)S(1)}, u32[]{:S(2)}) copy-start(bf16[8,32,1024]{2,1,0:T(8,128)(2,1)S(1)} %all-to-all-done.1) | copy-start | bytes 1572868
  21.8 33.2 %all-to-all-start.2 = ((bf16[16,256,256]{2,1,0:T(8,128)(2,1)}), bf16[16,256,256]{2,1,0:T(8,128)(2,1)S(1)}, u32[]{:S(2)}, u32[]{:S(2)}) async-start(bf16[16,256,256]{2,1,0:T(8,128)(2,1)} %compact.6), calls=%async_computation.2 | async-start | bytes 4194304 | tf_op jit(solution)/shard_map/all_to_all | solution.py:193
  66.9 1.0 %copy-start.1 = (f32[4,32,2048]{2,1,0:T(8,128)}, f32[4,32,2048]{2,1,0:T(8,128)S(1)}, u32[]{:S(2)}) copy-start(f32[4,32,2048]{2,1,0:T(8,128)S(1)} %get-tuple-element.340.keep_ref) | copy-start | bytes 3145732
  67.8 7.2 %collective-permute-start.4 = (f32[4,32,2048]{2,1,0:T(8,128)}, f32[4,32,2048]{2,1,0:T(8,128)S(1)}, u32[]{:S(2)}, u32[]{:S(2)}) collective-permute-start(f32[4,32,2048]{2,1,0:T(8,128)} %get-tuple-element.341), channel_id=1, source_target_pairs={{0,1},{1,0},{2,3},{3,2},{4,5},{5,4},{6,7},{7,6},{8,9},{9,8},{10,11... | collective-permute-start | bytes 3145736 | tf_op jit(solution)/shard_map/ppermute | solution.py:212
  75.0 1.2 %copy-start.2 = (f32[4,32,2048]{2,1,0:T(8,128)S(1)}, f32[4,32,2048]{2,1,0:T(8,128)}, u32[]{:S(2)}) copy-start(f32[4,32,2048]{2,1,0:T(8,128)} %copy-done.1) | copy-start | bytes 3145732
  76.3 17.0 %copy-start.7 = (bf16[2048,128]{1,0:T(8,128)(2,1)S(1)}, bf16[2048,128]{1,0:T(8,128)(2,1)}, u32[]{:S(2)}) copy-start(bf16[2048,128]{1,0:T(8,128)(2,1)} %copy-done.6) | copy-start | bytes 1572868
  76.3 17.0 %copy-start.9 = (bf16[8,32,1024]{2,1,0:T(8,128)(2,1)S(1)}, bf16[8,32,1024]{2,1,0:T(8,128)(2,1)}, u32[]{:S(2)}) copy-start(bf16[8,32,1024]{2,1,0:T(8,128)(2,1)} %copy-done.8) | copy-start | bytes 1572868
  76.4 9.4 %collective-permute-start.5 = (f32[32,2048]{1,0:T(8,128)S(1)}, f32[32,2048]{1,0:T(8,128)S(1)}, u32[]{:S(2)}, u32[]{:S(2)}) collective-permute-start(f32[32,2048]{1,0:T(8,128)S(1)} %get-tuple-element.343), channel_id=1, source_target_pairs={{0,2},{1,3},{2,4},{3,5},{4,6},{5,7},{6,0},{7,1},{8,10},{9,11},{10,... | collective-permute-start | bytes 786440 | tf_op jit(solution)/shard_map/ppermute | solution.py:224
  76.7 13.5 %collective-permute-start.6 = (f32[32,2048]{1,0:T(8,128)S(1)}, f32[32,2048]{1,0:T(8,128)S(1)}, u32[]{:S(2)}, u32[]{:S(2)}) collective-permute-start(f32[32,2048]{1,0:T(8,128)S(1)} %get-tuple-element.344), channel_id=1, source_target_pairs={{0,4},{1,5},{2,6},{3,7},{4,0},{5,1},{6,2},{7,3},{8,12},{9,13},{10,... | collective-permute-start | bytes 786440 | tf_op jit(solution)/shard_map/ppermute | solution.py:224
  78.5 12.6 %collective-permute-start.7 = (f32[32,2048]{1,0:T(8,128)S(1)}, f32[32,2048]{1,0:T(8,128)S(1)}, u32[]{:S(2)}, u32[]{:S(2)}) collective-permute-start(f32[32,2048]{1,0:T(8,128)S(1)} %get-tuple-element.345), channel_id=1, source_target_pairs={{0,6},{1,7},{2,0},{3,1},{4,2},{5,3},{6,4},{7,5},{8,14},{9,15},{10,... | collective-permute-start | bytes 786440 | tf_op jit(solution)/shard_map/ppermute | solution.py:224
  85.7 7.6 %copy-start.13 = (s32[8,1024]{1,0:T(8,128)S(1)}, s32[8,1024]{1,0:T(8,128)}, u32[]{:S(2)}) copy-start(s32[8,1024]{1,0:T(8,128)} %copy-done.12) | copy-start | bytes 98308
  85.7 7.6 %copy-start.16 = (s32[8,1024]{1,0:T(8,128)S(1)}, s32[8,1024]{1,0:T(8,128)}, u32[]{:S(2)}) copy-start(s32[8,1024]{1,0:T(8,128)} %copy-done.15) | copy-start | bytes 98308
  85.7 7.6 %copy-start.19 = (s32[256,128]{1,0:T(8,128)S(1)}, s32[256,128]{1,0:T(8,128)}, u32[]{:S(2)}) copy-start(s32[256,128]{1,0:T(8,128)} %copy-done.18) | copy-start | bytes 393220

commit v2 on v1

--- a/solution.py
+++ b/solution.py
@@ -12,8 +12,10 @@
 I32 = jnp.int32
 LANES = 128
 CAP = 32
+BASE = 16
+SPILL = 48
+PLACES = 8 * BASE + SPILL
 TM = 256
-VMEM_LIMIT = 48 * 1024 * 1024
 
 
 def pack_labels(labels):
@@ -39,7 +41,172 @@
     return jnp.transpose(row)
 
 
+def one_hot(mask):
+    return jnp.where(mask, 1.0, 0.0).astype(BF16)
+
+
+def rows_dot(a, b):
+    return lax.dot_general(a, b, (((1,), (1,)), ((), ())), preferred_element_type=F32)
+
+
+def iota(shape, axis):
+    return lax.broadcasted_iota(I32, shape, axis)
+
+
+def order_kernel(map_ref, amp_ref, *out_refs):
+    z, core = lax.axis_index("col") >> 1, lax.axis_index("col") & 1
+    k = map_ref[...]
+    col, row, within = k >> 12, (k >> 8) & 15, k & 1
+    place = ((((col >> 1) - z) & 3) * 2 + ((col & 1) ^ core)) * 32 + row * 2 + within
+    n = amp_ref.shape[0]
+    order = one_hot(iota((n, n), 0) == jnp.broadcast_to(place, (n, n)))
+    rows = jnp.dot(order, amp_ref[...], preferred_element_type=F32).astype(BF16)
+    for d, out_ref in enumerate(out_refs):
+        out_ref[...] = rows[d * 64 : d * 64 + 64, :]
+
+
 def symbols_kernel(
+    occ_ref, virt_ref, occ_orbs, k_orbs, m_orbs, own_orbs, other_orbs,
+    occ_out, rank_out, place_out, spread_out, k_out, k_col_out, m_out, own_out, other_out, bad_out,
+):
+    core = lax.axis_index("col") & 1
+    occ = pack_labels(occ_ref[0:1, :])
+    virt = pack_labels(virt_ref[0:7, :])
+    first = iota((LANES, LANES), 0)
+    second = iota((LANES, LANES), 1)
+    group = iota((8, LANES), 0)
+    used = jnp.zeros((8, 1), I32)
+    bad = jnp.zeros((1, LANES), I32)
+    for c in range(occ_orbs.shape[1] // LANES):
+        lanes = slice(c * LANES, (c + 1) * LANES)
+        sym = pair_symbols(occ, occ_orbs, c * LANES)
+        occ_out[:, lanes] = sym
+        same = as_column(sym) == jnp.broadcast_to(sym[0:1, :].astype(F32), (LANES, LANES))
+        rank = jnp.sum(jnp.where(same & (first < second), 1.0, 0.0), axis=0, keepdims=True).astype(I32)
+        rank_out[:, lanes] = jnp.broadcast_to(rank, (8, LANES))
+        mine = sym == group
+        extra = jnp.sum(jnp.where(mine, used, 0), axis=0, keepdims=True) + rank - BASE
+        used = used + jnp.maximum(jnp.sum(jnp.where(mine, 1, 0), axis=1, keepdims=True) - BASE, 0)
+        spilt = rank >= BASE
+        bad = jnp.maximum(bad, jnp.where(spilt & ((extra >= SPILL) | (rank >= CAP - 1)), 1, 0))
+        fits = spilt & (extra < SPILL)
+        place = jnp.where(spilt, jnp.where(fits, 8 * BASE + extra, -1), c * BASE + rank)
+        place_out[:, lanes] = jnp.broadcast_to(place, (8, LANES))
+        at = jnp.where(spilt, rank - BASE, -1)
+        entry = jnp.where(fits, sym[0:1, :] * SPILL + extra, -1)
+        to = one_hot(iota((BASE, LANES), 0) == jnp.broadcast_to(at, (BASE, LANES)))
+        source = one_hot(iota((8 * SPILL, LANES), 0) == jnp.broadcast_to(entry, (8 * SPILL, LANES)))
+        spread_out[c * BASE : (c + 1) * BASE, :] = rows_dot(to, source).astype(BF16)
+    bad_out[0, 0] = jnp.max(bad)
+    for start in range(0, k_orbs.shape[1], LANES):
+        sym = pair_symbols(virt, k_orbs, start)
+        wide = sym.astype(F32)
+        k_out[:, start : start + LANES] = jnp.concatenate([wide, wide], axis=0).astype(BF16)
+        k_col_out[start : start + LANES, :] = as_column(sym).astype(BF16)
+    for start in range(0, m_orbs.shape[1], LANES):
+        m_out[start : start + LANES, :] = as_column(pair_symbols(virt, m_orbs, start)).astype(BF16)
+    i, j = iota((LANES, 2 * LANES), 0), iota((LANES, 2 * LANES), 1)
+    pick = one_hot(j == (i >> 1) * 4 + core * 2 + (i & 1))
+    for orbs, out in ((own_orbs, own_out), (other_orbs, other_out)):
+        column = jnp.concatenate([as_column(pair_symbols(virt, orbs, s)) for s in (0, LANES)], axis=0)
+        out[...] = jnp.dot(pick, column.astype(BF16), preferred_element_type=F32)
+
+
+def compact_kernel(a_ref, b_ref, c_ref, d_ref, own_ref, other_ref, occ_ref, place_ref, mine_out, theirs_out):
+    z = lax.axis_index("col") >> 1
+    rows = jnp.concatenate([a_ref[...], b_ref[...], c_ref[...], d_ref[...]], axis=0)
+    pairs = rows.shape[1]
+    squeeze = one_hot(iota((PLACES, pairs), 0) == jnp.broadcast_to(place_ref[0:1, :], (PLACES, pairs)))
+    occ = jnp.broadcast_to(occ_ref[0:1, :].astype(F32), (LANES, pairs))
+    i, j = iota((LANES, 2 * LANES), 0), iota((LANES, 2 * LANES), 1)
+    row, source, within = i >> 3, (i >> 1) & 3, i & 1
+    for side, sym_ref, out in ((0, own_ref, mine_out), (1, other_ref, theirs_out)):
+        order = one_hot(j == (((z - source) & 3) * 2 + side) * 32 + row * 2 + within)
+        turned = jnp.dot(order, rows, preferred_element_type=F32)
+        sym = jnp.concatenate([sym_ref[...]] * (pairs // LANES), axis=1)
+        kept = jnp.where(sym == occ, turned, 0.0).astype(BF16)
+        out[...] = rows_dot(squeeze, kept).astype(BF16)
+
+
+def product_kernel(amp_ref, int_ref, k_ref, k_col_ref, m_ref, spread_ref, keep_ref, send_ref, kept):
+    core = lax.axis_index("col") & 1
+    depth = k_ref.shape[1]
+
+    @pl.when(pl.program_id(0) == 0)
+    def _():
+        i, j = iota((256, 256), 0), iota((256, 256), 1)
+        lane = (((i >> 1) & 1) ^ core) * 128 + (i >> 4) * 8 + ((i >> 2) & 3) * 2 + (i & 1)
+        order = one_hot(j == lane)
+        spread = spread_ref[...]
+        entry = iota((256, LANES), 1)
+        for source in range(16):
+            slots = amp_ref[source]
+            stack = jnp.concatenate([slots[: 8 * BASE]] + [slots[8 * BASE :]] * 8, axis=0)
+            block = rows_dot(order, stack)
+            sym = jnp.concatenate(
+                [k_col_ref[r * 256 + source * 16 : r * 256 + source * 16 + 16, :] for r in range(16)], axis=0
+            ).astype(F32)
+            parts = []
+            for t in range(8 * SPILL // LANES):
+                low = sym * SPILL - t * LANES
+                at = entry.astype(F32)
+                inside = (at >= low) & (at < low + SPILL)
+                part = block[:, 8 * BASE + t * LANES : 8 * BASE + (t + 1) * LANES]
+                parts.append(jnp.where(inside, part, 0.0).astype(BF16))
+            spilt = rows_dot(jnp.concatenate(parts, axis=1), spread).astype(BF16)
+            both = jnp.concatenate([block[:, : 8 * BASE].astype(BF16), spilt], axis=1)
+            for r in range(16):
+                kept[r * 256 + source * 16 : r * 256 + source * 16 + 16, :] = both[r * 16 : r * 16 + 16, :]
+
+    m_sym = m_ref[...]
+    chunk = 1024
+    total = jnp.zeros((m_ref.shape[0], 256), F32)
+    for at in range(0, depth, chunk):
+        parts = []
+        for lane in range(at, at + chunk, LANES):
+            lanes = slice(lane, lane + LANES)
+            same = m_sym == jnp.broadcast_to(k_ref[0:1, lanes], m_sym.shape)
+            parts.append(jnp.where(same, int_ref[:, lanes], jnp.zeros((), BF16)))
+        screened = jnp.concatenate(parts, axis=1)
+        total += jnp.dot(screened, kept[at : at + chunk, :], preferred_element_type=F32)
+    turned = jnp.transpose(total)
+    even = core == 0
+    for z in range(4):
+        for half in range(2):
+            at = half * 128 + z * 2 * BASE
+            low, high = turned[at : at + BASE, :], turned[at + BASE : at + 2 * BASE, :]
+            rows = slice(half * BASE, half * BASE + BASE)
+            keep_ref[z, rows, :] = jnp.where(even, low, high)
+            send_ref[z, rows, :] = jnp.where(even, high, low)
+
+
+def share_kernel(keep_ref, got_ref, own_ref, *out_refs):
+    z = lax.axis_index("col") >> 1
+    own_ref[...] = keep_ref[z] + got_ref[z]
+    for step, out_ref in enumerate(out_refs):
+        there = (z + step + 1) & 3
+        total = keep_ref[there] + got_ref[there]
+        largest = jnp.max(jnp.abs(total), axis=0, keepdims=True)
+        power = jnp.minimum(jnp.floor(14.9 - jnp.log2(jnp.maximum(largest, 1e-37))), 120.0)
+        scaled = total * jnp.exp2(power)
+        scaled = jnp.where(iota(total.shape, 0) == CAP - 1, power, scaled)
+        out_ref[...] = (scaled + jnp.where(scaled >= 0, 0.5, -0.5)).astype(I32).astype(jnp.int16)
+
+
+def expand_kernel(own_ref, a_ref, b_ref, c_ref, m_ref, occ_ref, rank_ref, out_ref):
+    lanes = pl.ds(pl.multiple_of(lax.axis_index("col") * LANES, LANES), LANES)
+    total = own_ref[...]
+    for ref in (a_ref, b_ref, c_ref):
+        part = ref[...].astype(I32).astype(F32)
+        total += part * jnp.exp2(-part[CAP - 1 : CAP, :])
+    slot = iota((CAP, LANES), 0)
+    pick = one_hot(slot == jnp.broadcast_to(rank_ref[0:1, lanes], (CAP, LANES)))
+    wide = lax.dot_general(total.astype(BF16), pick, (((0,), (0,)), ((), ())), preferred_element_type=F32)
+    same = m_ref[...].astype(F32) == jnp.broadcast_to(occ_ref[0:1, lanes].astype(F32), wide.shape)
+    out_ref[...] = jnp.where(same, wide, 0.0).astype(BF16)
+
+
+def plain_symbols_kernel(
     occ_ref, virt_ref, occ_orbs, k_orbs, m_orbs, own_orbs, occ_out, rank_out, k_out, m_out, own_out, most_out
 ):
     occ = pack_labels(occ_ref[0:1, :])
@@ -65,7 +232,7 @@
         own_out[start : start + LANES, :] = as_column(pair_symbols(virt, own_orbs, start)).astype(I32)
 
 
-def compact_kernel(copies, pass_ref, rows_ref, own_ref, occ_ref, rank_ref, out_ref):
+def plain_compact_kernel(copies, pass_ref, rows_ref, own_ref, occ_ref, rank_ref, out_ref):
     n, pairs = rows_ref.shape
     cols = pairs // LANES
     i = lax.broadcasted_iota(I32, (n, n), 0)
@@ -86,7 +253,7 @@
             out_ref[r, :, c * CAP : (c + 1) * CAP] = part
 
 
-def product_kernel(core_ref, amp_ref, int_ref, k_ref, m_ref, keep_ref, send_ref, kept):
+def plain_product_kernel(core_ref, amp_ref, int_ref, k_ref, m_ref, keep_ref, send_ref, kept):
     depth, width = amp_ref.shape
     block = depth // 16
 
@@ -118,13 +285,13 @@
         send_ref[z] = jnp.where(even, high, low)
 
 
-def share_kernel(z_ref, keep_ref, got_ref, *out_refs):
+def plain_share_kernel(z_ref, keep_ref, got_ref, *out_refs):
     for step, out_ref in enumerate(out_refs):
         z = (z_ref[0] + step) % 4
         out_ref[...] = keep_ref[z] + got_ref[z]
 
 
-def expand_kernel(at_ref, a_ref, b_ref, c_ref, d_ref, m_ref, occ_ref, rank_ref, out_ref):
+def plain_expand_kernel(at_ref, a_ref, b_ref, c_ref, d_ref, m_ref, occ_ref, rank_ref, out_ref):
     lanes = pl.ds(pl.multiple_of(at_ref[0] * LANES, LANES), LANES)
     total = (a_ref[...] + b_ref[...] + c_ref[...] + d_ref[...]).astype(BF16)
     slot = lax.broadcasted_iota(I32, (CAP, LANES), 0) + at_ref[1] * CAP
@@ -134,8 +301,8 @@
     out_ref[...] = jnp.where(same, wide, 0.0).astype(BF16)
 
 
-def params():
-    return pltpu.CompilerParams(vmem_limit_bytes=VMEM_LIMIT)
+def params(mib=16):
+    return pltpu.CompilerParams(vmem_limit_bytes=mib * 1024 * 1024)
 
 
 def whole():
@@ -146,7 +313,7 @@
     return pl.BlockSpec(memory_space=pltpu.SMEM)
 
 
-def body(amp_store, store_map, integrals, occ_irrep, virt_irrep, occ_orbs, k_orbs, m_orbs):
+def plain(amp_store, store_map, integrals, occ_irrep, virt_irrep, occ_orbs, k_orbs, m_orbs):
     rows = lax.axis_size("row")
     cols = lax.axis_size("col")
     stored, pairs = amp_store.shape
@@ -165,7 +332,7 @@
     occ_lab = jnp.pad(occ_irrep, (0, LANES - occ_irrep.shape[0])).reshape(1, LANES)
     virt_lab = jnp.pad(virt_irrep, (0, 8 * LANES - virt_irrep.shape[0])).reshape(8, LANES)
     occ_sym, rank, k_sym, m_sym, own_sym, most = pl.pallas_call(
-        symbols_kernel,
+        plain_symbols_kernel,
         out_shape=(
             shape((8, pairs), I32),
             shape((8, pairs), I32),
@@ -177,24 +344,24 @@
         in_specs=[whole()] * 6,
         out_specs=(whole(),) * 5 + (scalars(),),
         compiler_params=params(),
-        name="symbols",
+        name="plain_symbols",
     )(occ_lab, virt_lab, occ_orbs, k_orbs, m_orbs, own_orbs)
 
     def one_pass(step):
         width = cols * CAP
         compact = pl.pallas_call(
-            functools.partial(compact_kernel, rows),
+            functools.partial(plain_compact_kernel, rows),
             out_shape=shape((rows, stored, width), BF16),
             in_specs=[scalars()] + [whole()] * 4,
             out_specs=whole(),
             compiler_params=params(),
-            name="compact",
+            name="plain_compact",
         )(step.reshape(1), column_rows, own_sym, occ_sym, rank)
         gathered = lax.all_to_all(
             compact.reshape(rows * stored, width), "row", split_axis=0, concat_axis=0, tiled=True
         )
         keep, send = pl.pallas_call(
-            product_kernel,
+            plain_product_kernel,
             grid=(m_dev // TM,),
             out_shape=(shape((4, CAP, m_dev), F32),) * 2,
             in_specs=[
@@ -207,36 +374,132 @@
             out_specs=(pl.BlockSpec((4, CAP, TM), lambda i: (0, 0, i)),) * 2,
             scratch_shapes=[pltpu.VMEM((kblock, width), BF16)],
             compiler_params=params(),
-            name="product",
+            name="plain_product",
         )((my_col % 2).reshape(1), gathered, integrals, k_sym, m_sym)
         got = lax.ppermute(send, "col", [(i, i ^ 1) for i in range(cols)])
         shares = pl.pallas_call(
-            share_kernel,
+            plain_share_kernel,
             out_shape=(shape((CAP, m_dev), F32),) * 4,
             in_specs=[scalars(), whole(), whole()],
             out_specs=(whole(),) * 4,
             compiler_params=params(),
-            name="share",
+            name="plain_share",
         )((my_col // 2).reshape(1), keep, got)
         sums = [shares[0]]
         for distance in range(1, 4):
             hops = [(i, (i + 2 * distance) % cols) for i in range(cols)]
             sums.append(lax.ppermute(shares[distance], "col", hops))
         return pl.pallas_call(
-            expand_kernel,
+            plain_expand_kernel,
             out_shape=shape((m_dev, LANES), BF16),
             in_specs=[scalars()] + [whole()] * 7,
             out_specs=whole(),
             compiler_params=params(),
-            name="expand",
+            name="plain_expand",
         )(jnp.stack([my_col, step]), *sums, m_sym, occ_sym, rank)
 
     passes = most[0, 0] // CAP + 1
-    first = one_pass(jnp.zeros((), I32))
     return lax.while_loop(
         lambda state: state[0] < passes,
         lambda state: (state[0] + 1, state[1] + one_pass(state[0])),
-        (jnp.ones((), I32), first),
+        (jnp.zeros((), I32), jnp.zeros((m_dev, LANES), BF16)),
+    )[1]
+
+
+def body(amp_store, store_map, integrals, occ_irrep, virt_irrep, occ_orbs, k_orbs, m_orbs):
+    rows = lax.axis_size("row")
+    cols = lax.axis_size("col")
+    stored, pairs = amp_store.shape
+    kblock = k_orbs.shape[1]
+    m_dev = m_orbs.shape[1]
+    shape = jax.ShapeDtypeStruct
+    swap = [(i, i ^ 1) for i in range(cols)]
+    hops = [[(i, (i + 2 * d) % cols) for i in range(cols)] for d in range(4)]
+
+    def call(kernel, name, out_shape, operands, mib=16, **kw):
+        return pl.pallas_call(
+            kernel,
+            out_shape=out_shape,
+            in_specs=[whole()] * len(operands),
+            out_specs=kw.pop("out_specs", jax.tree.map(lambda _: whole(), out_shape)),
+            compiler_params=params(mib),
+            name=name,
+            **kw,
+        )(*operands)
+
+    own_orbs = lax.dynamic_slice_in_dim(
+        k_orbs.reshape(2, rows, stored), lax.axis_index("row") * 16, 16, axis=2
+    ).reshape(2, stored)
+    other_orbs = lax.ppermute(own_orbs, "col", swap)
+
+    ordered = call(order_kernel, "order", (shape((64, pairs), BF16),) * 4, (store_map.reshape(1, stored), amp_store))
+    arrived = [ordered[0]] + [lax.ppermute(ordered[d], "col", hops[d]) for d in range(1, 4)]
+
+    occ_lab = jnp.pad(occ_irrep, (0, LANES - occ_irrep.shape[0])).reshape(1, LANES)
+    virt_lab = jnp.pad(virt_irrep, (0, 8 * LANES - virt_irrep.shape[0])).reshape(8, LANES)
+    occ_sym, rank, place, spread, k_sym, k_col, m_sym, own_sym, other_sym, bad = call(
+        symbols_kernel,
+        "symbols",
+        (
+            shape((8, pairs), I32),
+            shape((8, pairs), I32),
+            shape((8, pairs), I32),
+            shape((8 * BASE, 8 * SPILL), BF16),
+            shape((16, kblock), BF16),
+            shape((kblock, LANES), BF16),
+            shape((m_dev, LANES), BF16),
+            shape((LANES, LANES), F32),
+            shape((LANES, LANES), F32),
+            shape((1, 1), I32),
+        ),
+        (occ_lab, virt_lab, occ_orbs, k_orbs, m_orbs, own_orbs, other_orbs),
+        out_specs=(whole(),) * 9 + (scalars(),),
+    )
+
+    mine, theirs = call(
+        compact_kernel,
+        "compact",
+        (shape((PLACES, LANES), BF16),) * 2,
+        (*arrived, own_sym, other_sym, occ_sym, place),
+    )
+    got = lax.ppermute(theirs, "col", swap)
+    spreading = jnp.broadcast_to(jnp.concatenate([mine, got], axis=1)[None], (rows, PLACES, stored))
+    gathered = lax.all_to_all(spreading, "row", split_axis=0, concat_axis=0, tiled=True)
+
+    keep, send = pl.pallas_call(
+        product_kernel,
+        grid=(m_dev // 512,),
+        out_shape=(shape((4, CAP, m_dev), F32),) * 2,
+        in_specs=[
+            whole(),
+            pl.BlockSpec((512, kblock), lambda i: (i, 0)),
+            whole(),
+            whole(),
+            pl.BlockSpec((512, LANES), lambda i: (i, 0)),
+            whole(),
+        ],
+        out_specs=(pl.BlockSpec((4, CAP, 512), lambda i: (0, 0, i)),) * 2,
+        scratch_shapes=[pltpu.VMEM((kblock, 256), BF16)],
+        compiler_params=params(24),
+        name="product",
+    )(gathered, integrals, k_sym, k_col, m_sym, spread)
+    partner = lax.ppermute(send, "col", swap)
+    shares = call(
+        share_kernel,
+        "share",
+        (shape((CAP, m_dev), F32),) + (shape((CAP, m_dev), jnp.int16),) * 3,
+        (keep, partner),
+    )
+    sums = [shares[0]] + [lax.ppermute(shares[d], "col", hops[d]) for d in range(1, 4)]
+    result = call(expand_kernel, "expand", shape((m_dev, LANES), BF16), (*sums, m_sym, occ_sym, rank))
+
+    return lax.while_loop(
+        lambda state: state[0] > 0,
+        lambda state: (
+            jnp.zeros((), I32),
+            plain(amp_store, store_map, integrals, occ_irrep, virt_irrep, occ_orbs, k_orbs, m_orbs),
+        ),
+        (bad[0, 0], result),
     )[1]
 
 

time: 93.9 us -> 73 us (0.78)
  waiting for transfers between devices: 46.2 us -> 9.84 us
  blocking collectives: 0 us -> 26.3 us
  starting transfers between devices: 21.1 us -> 14.6 us
  between operations: 2.74 us -> 0.23 us
  matrix products: 1.1 us -> 0 us
    all_to_all x2 -> x0, waiting for transfers between devices: 34.5 us -> none  [the longest x1 26.4 us: one_pass(): lax.all_to_all(compact.reshape(rows * stored, width), 'row', split_axis=0...]
    all_to_all x0 -> x1, blocking collectives: none -> 26.3 us  [body(): lax.all_to_all(spreading, 'row', split_axis=0, concat_axis=0, tiled=True)]
    all_to_all x2 -> x0, starting transfers between devices: 13.6 us -> none  [the longest x1 6.81 us: body(): lax.all_to_all(ordered, 'col', split_axis=0, concat_axis=0, tiled=True)]
    ppermute x4 -> x9, starting transfers between devices: 7.52 us -> 14.6 us  [the longest x3 5.82 us: body(): lax.ppermute(ordered[d], 'col', hops[d])]
    ppermute x4 -> x9, waiting for transfers between devices: 11.8 us -> 9.84 us  [the longest x3 5.09 us: body(): lax.ppermute(shares[d], 'col', hops[d])]
    unnamed x37 -> x3, local copies, waits for them, and re-layouts: 2.53 us -> 0.77 us
    dot_general x1 -> x0, matrix products: 1.1 us -> none  [body(): ordered = jnp.dot(order, amp_store, preferred_element_type=F32).astype(BF16)]
    pallas_call x5 -> x6, Pallas kernels: 18.7 us -> 18.4 us  [the longest x1 12.2 us: body(): pl.pallas_call(product_kernel, grid=(m_dev // 512,), out_shape=(shape((4,...]
  transfers between devices with their start and end apart: 6 -> 9, of which waited for: 6 -> 5; matrix products, arithmetic and copies ran while one was open for 0% -> 2% of each run, Pallas kernels for 1% -> 6%
where the time goes in v2:
time: 73 us; the launch traced here: 72.6 us
  blocking collectives  26.3 us (36%)
  Pallas kernels  18.4 us (25%)
  starting transfers between devices  14.6 us (20%)
  waiting for transfers between devices  9.84 us (13%)
  local copies, waits for them, and re-layouts  2.36 us (3%)
  loops' own time  0.82 us (1%)
    all_to_all x1, blocking collectives, body(): lax.all_to_all(spreading, 'row', split_axis=0, concat_axis=0, tiled=True)  26.3 us
    pallas_call x1, Pallas kernels, body(): pl.pallas_call(product_kernel, grid=(m_dev // 512,), out_shape=(shape((4,...  12.2 us
    pallas_call x5, Pallas kernels, call(): pl.pallas_call(kernel, out_shape=out_shape, in_specs=[whole()] * len(oper...  6.2 us
    ppermute x3, starting transfers between devices, body(): lax.ppermute(ordered[d], 'col', hops[d])  5.82 us
    ppermute x3, waiting for transfers between devices, body(): lax.ppermute(shares[d], 'col', hops[d])  5.09 us
    ppermute x3, starting transfers between devices, body(): lax.ppermute(shares[d], 'col', hops[d])  4.1 us
    ppermute x1, starting transfers between devices, body(): partner = lax.ppermute(send, 'col', swap)  2.36 us
    ppermute x1, waiting for transfers between devices, body(): partner = lax.ppermute(send, 'col', swap)  2.29 us
  transfers between devices with their start and end apart: 9, of which 5 were waited for; matrix products, arithmetic and copies ran while one was open for 2% of the time, Pallas kernels for 6%

profile of v2, /device:TPU:1, one launch (start us, length us, event | category | flops | bytes accessed | tf_op | source)
XLA Modules:
  0.0 72.6 jit_solution(3527762367060798182)
XLA Ops:
  0.0 0.8 %copy.14 = s32[1,2,16,256]{3,2,1,0:T(8,128)S(1)} copy(s32[1,2,16,256]{3,1,2,0:T(2,128)} %bitcast.16) | data formatting | bytes 65536
  0.8 0.1 constant_dynamic-slice_fusion
  0.8 0.1 reshape.106.own_orbs
  0.9 1.5 %collective-permute-start.4 = (s32[2,256]{1,0:T(2,128)S(1)}, s32[2,256]{1,0:T(2,128)S(1)}, u32[]{:S(2)}, u32[]{:S(2)}) collective-permute-start(s32[2,256]{1,0:T(2,128)S(1)} %reshape.106.own_orbs), channel_id=1, source_target_pairs={{0,1},{1,0},{2,3},{3,2},{4,5},{5,4},{6,7},{7,6},{8,9},{9,8},{10,11... | collective-permute-start | bytes 6152 | tf_op jit(solution)/shard_map/ppermute | solution.py:433
  2.4 1.4 %order.1 = (bf16[64,1024]{1,0:T(8,128)(2,1)S(1)}, bf16[64,1024]{1,0:T(8,128)(2,1)S(1)}, bf16[64,1024]{1,0:T(8,128)(2,1)S(1)}, bf16[64,1024]{1,0:T(8,128)(2,1)S(1)}) custom-call(s32[1,256]{1,0:T(1,128)} %bitcast.13.map_ref, bf16[256,1024]{1,0:T(8,128)(2,1)} %amp_ref.1), custom_call_target="tpu_custom_call" | custom-call | tf_op jit(solution)/shard_map/order/pallas_call | solution.py:420
  3.7 1.8 %collective-permute-start.5 = (bf16[64,1024]{1,0:T(8,128)(2,1)S(1)}, bf16[64,1024]{1,0:T(8,128)(2,1)S(1)}, u32[]{:S(2)}, u32[]{:S(2)}) collective-permute-start(bf16[64,1024]{1,0:T(8,128)(2,1)S(1)} %get-tuple-element.403), channel_id=1, source_target_pairs={{0,2},{1,3},{2,4},{3,5},{4,6},{5,7},{6,0},{7,1},{8,10},{9,11},{10,... | collective-permute-start | bytes 393224 | tf_op jit(solution)/shard_map/ppermute | solution.py:436
  5.5 3.3 %collective-permute-start.6 = (bf16[64,1024]{1,0:T(8,128)(2,1)S(1)}, bf16[64,1024]{1,0:T(8,128)(2,1)S(1)}, u32[]{:S(2)}, u32[]{:S(2)}) collective-permute-start(bf16[64,1024]{1,0:T(8,128)(2,1)S(1)} %get-tuple-element.404), channel_id=1, source_target_pairs={{0,4},{1,5},{2,6},{3,7},{4,0},{5,1},{6,2},{7,3},{8,12},{9,13},{10,... | collective-permute-start | bytes 393224 | tf_op jit(solution)/shard_map/ppermute | solution.py:436
  8.8 0.7 %collective-permute-start.7 = (bf16[64,1024]{1,0:T(8,128)(2,1)S(1)}, bf16[64,1024]{1,0:T(8,128)(2,1)S(1)}, u32[]{:S(2)}, u32[]{:S(2)}) collective-permute-start(bf16[64,1024]{1,0:T(8,128)(2,1)S(1)} %get-tuple-element.405), channel_id=1, source_target_pairs={{0,6},{1,7},{2,0},{3,1},{4,2},{5,3},{6,4},{7,5},{8,14},{9,15},{10,... | collective-permute-start | bytes 393224 | tf_op jit(solution)/shard_map/ppermute | solution.py:436
  9.6 0.7 pad_bitcast_fusion.2.virt_ref
  10.2 0.7 pad_bitcast_fusion.3.occ_ref
  10.9 0.0 collective-permute-done.4.other_orbs
  10.9 2.8 %symbols.1 = (s32[8,1024]{1,0:T(8,128)S(1)}, s32[8,1024]{1,0:T(8,128)S(1)}, s32[8,1024]{1,0:T(8,128)S(1)}, bf16[128,384]{1,0:T(8,128)(2,1)S(1)}, bf16[16,4096]{1...) custom-call(s32[1,128]{1,0:T(1,128)S(1)} %pad_bitcast_fusion.3.occ_r, ...), custom_call_target="tpu_custom_call" | custom-call | tf_op jit(solution)/shard_map/symbols/pallas_call | solution.py:420
  13.7 0.0 collective-permute-done.5.b_ref
  13.7 1.6 %collective-permute-done.6.c_ref = bf16[64,1024]{1,0:T(8,128)(2,1)S(1)} collective-permute-done((bf16[64,1024]{1,0:T(8,128)(2,1)S(1)}, bf16[64,1024]{1,0:T(8,128)(2,1)S(1)}, u32[]{:S(2)}, u32[]{:S(2)}) %collective-permute-start.6) | collective-permute-done | bytes 131104 | tf_op jit(solution)/shard_map/ppermute | solution.py:436
  15.3 0.0 collective-permute-done.7.d_ref
  15.3 0.6 compact.1
  15.9 0.9 %collective-permute-start.8 = (bf16[176,128]{1,0:T(8,128)(2,1)S(1)}, bf16[176,128]{1,0:T(8,128)(2,1)S(1)}, u32[]{:S(2)}, u32[]{:S(2)}) collective-permute-start(bf16[176,128]{1,0:T(8,128)(2,1)S(1)} %get-tuple-element.411), channel_id=1, source_target_pairs={{0,1},{1,0},{2,3},{3,2},{4,5},{5,4},{6,7},{7,6},{8,9},{9,8},{10,11... | collective-permute-start | bytes 135176 | tf_op jit(solution)/shard_map/ppermute | solution.py:465
  16.7 0.9 %collective-permute-done.8 = bf16[176,128]{1,0:T(8,128)(2,1)S(1)} collective-permute-done((bf16[176,128]{1,0:T(8,128)(2,1)S(1)}, bf16[176,128]{1,0:T(8,128)(2,1)S(1)}, u32[]{:S(2)}, u32[]{:S(2)}) %collective-permute-start.8) | collective-permute-done | bytes 45088 | tf_op jit(solution)/shard_map/ppermute | solution.py:465
  17.6 0.1 broadcast_in_dim.2
  17.7 26.3 %all_to_all.22.amp_ref = bf16[16,176,256]{2,1,0:T(8,128)(2,1)S(1)} all-to-all(bf16[16,176,256]{2,1,0:T(8,128)(2,1)S(1)} %broadcast_in_dim.2), channel_id=1, replica_groups=mesh['row'=16,'col'=8] {'row'}, dimensions={0} | all-to-all | bytes 2883584 | tf_op jit(solution)/shard_map/all_to_all | solution.py:467
  44.0 12.2 %product.1 = (f32[4,32,2048]{2,1,0:T(8,128)S(1)}, f32[4,32,2048]{2,1,0:T(8,128)S(1)}) custom-call(bf16[16,176,256]{2,1,0:T(8,128)(2,1)S(1)} %all_to_all.22.amp_ref, bf16[2048,4096]{1,0:T(8,128)(2,1)} %int_ref.1, bf16[16,4096]{1,0:T(8,128)(2,1)S(1)} %get-tuple-element.412.k_ref, bf16[4096,128]{1,0:T(8,128)(2,1)S(1)} %get-tuple-element.413.k_col_ref, ...), custom_call_target="tpu_custom_call" | custom-call | tf_op jit(solution)/shard_map/product/pallas_call | solution.py:469
  56.3 0.0 copy-start.1
  56.3 2.4 %collective-permute-start.9 = (f32[4,32,2048]{2,1,0:T(8,128)S(1)}, f32[4,32,2048]{2,1,0:T(8,128)S(1)}, u32[]{:S(2)}, u32[]{:S(2)}) collective-permute-start(f32[4,32,2048]{2,1,0:T(8,128)S(1)} %get-tuple-element.417), channel_id=1, source_target_pairs={{0,1},{1,0},{2,3},{3,2},{4,5},{5,4},{6,7},{7,6},{8,9},{9,8},{10,11... | collective-permute-start | bytes 3145736 | tf_op jit(solution)/shard_map/ppermute | solution.py:486
  58.6 2.3 %collective-permute-done.9.got_ref = f32[4,32,2048]{2,1,0:T(8,128)S(1)} collective-permute-done((f32[4,32,2048]{2,1,0:T(8,128)S(1)}, f32[4,32,2048]{2,1,0:T(8,128)S(1)}, u32[]{:S(2)}, u32[]{:S(2)}) %collective-permute-start.9) | collective-permute-done | bytes 1048608 | tf_op jit(solution)/shard_map/ppermute | solution.py:486
  60.9 0.3 share.1
  61.3 1.0 %collective-permute-start.10 = (s16[32,2048]{1,0:T(8,128)(2,1)S(1)}, s16[32,2048]{1,0:T(8,128)(2,1)S(1)}, u32[]{:S(2)}, u32[]{:S(2)}) collective-permute-start(s16[32,2048]{1,0:T(8,128)(2,1)S(1)} %get-tuple-element.419), channel_id=1, source_target_pairs={{0,2},{1,3},{2,4},{3,5},{4,6},{5,7},{6,0},{7,1},{8,10},{9,11},{10,... | collective-permute-start | bytes 393224 | tf_op jit(solution)/shard_map/ppermute | solution.py:493
  62.3 2.1 %collective-permute-start.11 = (s16[32,2048]{1,0:T(8,128)(2,1)S(1)}, s16[32,2048]{1,0:T(8,128)(2,1)S(1)}, u32[]{:S(2)}, u32[]{:S(2)}) collective-permute-start(s16[32,2048]{1,0:T(8,128)(2,1)S(1)} %get-tuple-element.420), channel_id=1, source_target_pairs={{0,4},{1,5},{2,6},{3,7},{4,0},{5,1},{6,2},{7,3},{8,12},{9,13},{10,... | collective-permute-start | bytes 393224 | tf_op jit(solution)/shard_map/ppermute | solution.py:493
  64.4 1.0 %collective-permute-start.12 = (s16[32,2048]{1,0:T(8,128)(2,1)S(1)}, s16[32,2048]{1,0:T(8,128)(2,1)S(1)}, u32[]{:S(2)}, u32[]{:S(2)}) collective-permute-start(s16[32,2048]{1,0:T(8,128)(2,1)S(1)} %get-tuple-element.421), channel_id=1, source_target_pairs={{0,6},{1,7},{2,0},{3,1},{4,2},{5,3},{6,4},{7,5},{8,14},{9,15},{10,... | collective-permute-start | bytes 393224 | tf_op jit(solution)/shard_map/ppermute | solution.py:493
  65.4 1.9 %collective-permute-done.10.a_ref = s16[32,2048]{1,0:T(8,128)(2,1)S(1)} collective-permute-done((s16[32,2048]{1,0:T(8,128)(2,1)S(1)}, s16[32,2048]{1,0:T(8,128)(2,1)S(1)}, u32[]{:S(2)}, u32[]{:S(2)}) %collective-permute-start.10) | collective-permute-done | bytes 131104 | tf_op jit(solution)/shard_map/ppermute | solution.py:493
  67.3 3.2 %collective-permute-done.11.b_ref = s16[32,2048]{1,0:T(8,128)(2,1)S(1)} collective-permute-done((s16[32,2048]{1,0:T(8,128)(2,1)S(1)}, s16[32,2048]{1,0:T(8,128)(2,1)S(1)}, u32[]{:S(2)}, u32[]{:S(2)}) %collective-permute-start.11) | collective-permute-done | bytes 131104 | tf_op jit(solution)/shard_map/ppermute | solution.py:493
  70.4 1.2 %expand.1 = bf16[2048,128]{1,0:T(8,128)(2,1)} custom-call(f32[32,2048]{1,0:T(8,128)S(1)} %get-tuple-element.418.own_ref, s16[32,2048]{1,0:T(8,128)(2,1)S(1)} %collective-permute-done.10.a_ref, s16[32,2048]{1,0:T(8,128)(2,1)S(1)} %collective-permute-done.11.b_ref, s16[32,2048]{1,0:T(8,128)(2,1)S(1)} %collective-permute-done.12.c_ref, ...), custom_call_target="tpu_custom_call" | custom-call | tf_op jit(solution)/shard_map/expand/pallas_call | solution.py:420
  71.6 0.8 %while.22 = (s32[]{:T(128)}, bf16[2048,128]{1,0:T(8,128)(2,1)}, s32[100]{0:T(128)}, s32[800]{0:T(1024)}, s32[2,4096]{1,0:T(2,128)}, /*index=5*/s32[2,1024]{1,0:T...) while((s32[]{:T(128)}, bf16[2048,128]{1,0:T(8,128)(2,1)}, ...), condition=%region_3.4_spmd, body=%region_0.3_spmd | while | flops 134819376 | bytes 18436136 | solution.py:496
  (3 shorter events, 0.0 us)
Async XLA Ops:
  0.9 10.0 %collective-permute-start.4 = (s32[2,256]{1,0:T(2,128)S(1)}, s32[2,256]{1,0:T(2,128)S(1)}, u32[]{:S(2)}, u32[]{:S(2)}) collective-permute-start(s32[2,256]{1,0:T(2,128)S(1)} %reshape.106.own_orbs), channel_id=1, source_target_pairs={{0,1},{1,0},{2,3},{3,2},{4,5},{5,4},{6,7},{7,6},{8,9},{9,8},{10,11... | collective-permute-start | bytes 6152 | tf_op jit(solution)/shard_map/ppermute | solution.py:433
  3.7 10.0 %collective-permute-start.5 = (bf16[64,1024]{1,0:T(8,128)(2,1)S(1)}, bf16[64,1024]{1,0:T(8,128)(2,1)S(1)}, u32[]{:S(2)}, u32[]{:S(2)}) collective-permute-start(bf16[64,1024]{1,0:T(8,128)(2,1)S(1)} %get-tuple-element.403), channel_id=1, source_target_pairs={{0,2},{1,3},{2,4},{3,5},{4,6},{5,7},{6,0},{7,1},{8,10},{9,11},{10,... | collective-permute-start | bytes 393224 | tf_op jit(solution)/shard_map/ppermute | solution.py:436
  5.5 9.8 %collective-permute-start.6 = (bf16[64,1024]{1,0:T(8,128)(2,1)S(1)}, bf16[64,1024]{1,0:T(8,128)(2,1)S(1)}, u32[]{:S(2)}, u32[]{:S(2)}) collective-permute-start(bf16[64,1024]{1,0:T(8,128)(2,1)S(1)} %get-tuple-element.404), channel_id=1, source_target_pairs={{0,4},{1,5},{2,6},{3,7},{4,0},{5,1},{6,2},{7,3},{8,12},{9,13},{10,... | collective-permute-start | bytes 393224 | tf_op jit(solution)/shard_map/ppermute | solution.py:436
  8.8 6.5 %collective-permute-start.7 = (bf16[64,1024]{1,0:T(8,128)(2,1)S(1)}, bf16[64,1024]{1,0:T(8,128)(2,1)S(1)}, u32[]{:S(2)}, u32[]{:S(2)}) collective-permute-start(bf16[64,1024]{1,0:T(8,128)(2,1)S(1)} %get-tuple-element.405), channel_id=1, source_target_pairs={{0,6},{1,7},{2,0},{3,1},{4,2},{5,3},{6,4},{7,5},{8,14},{9,15},{10,... | collective-permute-start | bytes 393224 | tf_op jit(solution)/shard_map/ppermute | solution.py:436
  15.9 1.8 %collective-permute-start.8 = (bf16[176,128]{1,0:T(8,128)(2,1)S(1)}, bf16[176,128]{1,0:T(8,128)(2,1)S(1)}, u32[]{:S(2)}, u32[]{:S(2)}) collective-permute-start(bf16[176,128]{1,0:T(8,128)(2,1)S(1)} %get-tuple-element.411), channel_id=1, source_target_pairs={{0,1},{1,0},{2,3},{3,2},{4,5},{5,4},{6,7},{7,6},{8,9},{9,8},{10,11... | collective-permute-start | bytes 135176 | tf_op jit(solution)/shard_map/ppermute | solution.py:465
  56.3 15.3 %copy-start.1 = (s32[2,2048]{1,0:T(2,128)S(1)}, s32[2,2048]{1,0:T(2,128)}, u32[]{:S(2)}) copy-start(s32[2,2048]{1,0:T(2,128)} %m_orbs.1) | copy-start | bytes 49156
  56.3 4.6 %collective-permute-start.9 = (f32[4,32,2048]{2,1,0:T(8,128)S(1)}, f32[4,32,2048]{2,1,0:T(8,128)S(1)}, u32[]{:S(2)}, u32[]{:S(2)}) collective-permute-start(f32[4,32,2048]{2,1,0:T(8,128)S(1)} %get-tuple-element.417), channel_id=1, source_target_pairs={{0,1},{1,0},{2,3},{3,2},{4,5},{5,4},{6,7},{7,6},{8,9},{9,8},{10,11... | collective-permute-start | bytes 3145736 | tf_op jit(solution)/shard_map/ppermute | solution.py:486
  61.3 6.0 %collective-permute-start.10 = (s16[32,2048]{1,0:T(8,128)(2,1)S(1)}, s16[32,2048]{1,0:T(8,128)(2,1)S(1)}, u32[]{:S(2)}, u32[]{:S(2)}) collective-permute-start(s16[32,2048]{1,0:T(8,128)(2,1)S(1)} %get-tuple-element.419), channel_id=1, source_target_pairs={{0,2},{1,3},{2,4},{3,5},{4,6},{5,7},{6,0},{7,1},{8,10},{9,11},{10,... | collective-permute-start | bytes 393224 | tf_op jit(solution)/shard_map/ppermute | solution.py:493
  62.3 8.2 %collective-permute-start.11 = (s16[32,2048]{1,0:T(8,128)(2,1)S(1)}, s16[32,2048]{1,0:T(8,128)(2,1)S(1)}, u32[]{:S(2)}, u32[]{:S(2)}) collective-permute-start(s16[32,2048]{1,0:T(8,128)(2,1)S(1)} %get-tuple-element.420), channel_id=1, source_target_pairs={{0,4},{1,5},{2,6},{3,7},{4,0},{5,1},{6,2},{7,3},{8,12},{9,13},{10,... | collective-permute-start | bytes 393224 | tf_op jit(solution)/shard_map/ppermute | solution.py:493
  64.4 6.1 %collective-permute-start.12 = (s16[32,2048]{1,0:T(8,128)(2,1)S(1)}, s16[32,2048]{1,0:T(8,128)(2,1)S(1)}, u32[]{:S(2)}, u32[]{:S(2)}) collective-permute-start(s16[32,2048]{1,0:T(8,128)(2,1)S(1)} %get-tuple-element.421), channel_id=1, source_target_pairs={{0,6},{1,7},{2,0},{3,1},{4,2},{5,3},{6,4},{7,5},{8,14},{9,15},{10,... | collective-permute-start | bytes 393224 | tf_op jit(solution)/shard_map/ppermute | solution.py:493

commit v3 on v2

--- a/solution.py
+++ b/solution.py
@@ -16,6 +16,8 @@
 SPILL = 48
 PLACES = 8 * BASE + SPILL
 TM = 256
+ROOM = 64
+TILE = 1024
 
 
 def pack_labels(labels):
@@ -93,9 +95,9 @@
         place = jnp.where(spilt, jnp.where(fits, 8 * BASE + extra, -1), c * BASE + rank)
         place_out[:, lanes] = jnp.broadcast_to(place, (8, LANES))
         at = jnp.where(spilt, rank - BASE, -1)
-        entry = jnp.where(fits, sym[0:1, :] * SPILL + extra, -1)
+        entry = jnp.where(fits, sym[0:1, :] * ROOM + extra, -1)
         to = one_hot(iota((BASE, LANES), 0) == jnp.broadcast_to(at, (BASE, LANES)))
-        source = one_hot(iota((8 * SPILL, LANES), 0) == jnp.broadcast_to(entry, (8 * SPILL, LANES)))
+        source = one_hot(iota((8 * ROOM, LANES), 0) == jnp.broadcast_to(entry, (8 * ROOM, LANES)))
         spread_out[c * BASE : (c + 1) * BASE, :] = rows_dot(to, source).astype(BF16)
     bad_out[0, 0] = jnp.max(bad)
     for start in range(0, k_orbs.shape[1], LANES):
@@ -128,56 +130,74 @@
         out[...] = rows_dot(squeeze, kept).astype(BF16)
 
 
-def product_kernel(amp_ref, int_ref, k_ref, k_col_ref, m_ref, spread_ref, keep_ref, send_ref, kept):
+def product_kernel(amp_ref, int_ref, k_ref, k_col_ref, m_ref, spread_ref, keep_ref, send_ref, kept, local, sems):
     core = lax.axis_index("col") & 1
     depth = k_ref.shape[1]
-
-    @pl.when(pl.program_id(0) == 0)
-    def _():
-        i, j = iota((256, 256), 0), iota((256, 256), 1)
-        lane = (((i >> 1) & 1) ^ core) * 128 + (i >> 4) * 8 + ((i >> 2) & 3) * 2 + (i & 1)
-        order = one_hot(j == lane)
-        spread = spread_ref[...]
-        entry = iota((256, LANES), 1)
-        for source in range(16):
-            slots = amp_ref[source]
-            stack = jnp.concatenate([slots[: 8 * BASE]] + [slots[8 * BASE :]] * 8, axis=0)
-            block = rows_dot(order, stack)
-            sym = jnp.concatenate(
-                [k_col_ref[r * 256 + source * 16 : r * 256 + source * 16 + 16, :] for r in range(16)], axis=0
-            ).astype(F32)
+    tiles = int_ref.shape[0] // TILE
+
+    def fetch(n):
+        rows = pl.ds(pl.multiple_of(n * TILE, TILE), TILE)
+        return pltpu.make_async_copy(int_ref.at[rows], local.at[rows], sems.at[n])
+
+    def begin(n, carry):
+        fetch(n).start()
+        return carry
+
+    lax.fori_loop(0, tiles, begin, 0)
+
+    i, j = iota((256, 256), 0), iota((256, 256), 1)
+    order = one_hot(j == (((i >> 1) & 1) ^ core) * 128 + (i >> 4) * 8 + ((i >> 2) & 3) * 2 + (i & 1))
+    spread = spread_ref[...]
+    nought = jnp.zeros((), BF16)
+    gap = jnp.zeros((ROOM - SPILL, 256), BF16)
+    second = iota((16, LANES), 1) >= ROOM
+    groups = [
+        jnp.broadcast_to(jnp.where(second, 2.0 * t + 1.0, 2.0 * t).astype(BF16)[0:1, :], (256, LANES))
+        for t in range(4)
+    ]
+
+    def unpack(source, carry):
+        slots = amp_ref[source]
+        stack = jnp.concatenate([slots, gap, slots[8 * BASE :], gap], axis=0)
+        block = rows_dot(order, stack).astype(BF16)
+        at = [pl.ds(pl.multiple_of(r * 256 + source * 16, 16), 16) for r in range(16)]
+        sym = jnp.concatenate([k_col_ref[rows, :] for rows in at], axis=0)
+        shared = [jnp.where(sym == group, block[:, 8 * BASE :], nought) for group in groups]
+        spilt = rows_dot(jnp.concatenate(shared, axis=1), spread).astype(BF16)
+        for r, rows in enumerate(at):
+            kept[rows, : 8 * BASE] = block[r * 16 : r * 16 + 16, : 8 * BASE]
+            kept[rows, 8 * BASE :] = spilt[r * 16 : r * 16 + 16, :]
+        return carry
+
+    lax.fori_loop(0, 16, unpack, 0, unroll=8)
+
+    even = core == 0
+    chunk = 1024
+
+    def multiply(n, carry):
+        rows = pl.ds(pl.multiple_of(n * TILE, TILE), TILE)
+        fetch(n).wait()
+        m_sym = m_ref[rows, :]
+        total = jnp.zeros((TILE, 256), F32)
+        for at in range(0, depth, chunk):
             parts = []
-            for t in range(8 * SPILL // LANES):
-                low = sym * SPILL - t * LANES
-                at = entry.astype(F32)
-                inside = (at >= low) & (at < low + SPILL)
-                part = block[:, 8 * BASE + t * LANES : 8 * BASE + (t + 1) * LANES]
-                parts.append(jnp.where(inside, part, 0.0).astype(BF16))
-            spilt = rows_dot(jnp.concatenate(parts, axis=1), spread).astype(BF16)
-            both = jnp.concatenate([block[:, : 8 * BASE].astype(BF16), spilt], axis=1)
-            for r in range(16):
-                kept[r * 256 + source * 16 : r * 256 + source * 16 + 16, :] = both[r * 16 : r * 16 + 16, :]
-
-    m_sym = m_ref[...]
-    chunk = 1024
-    total = jnp.zeros((m_ref.shape[0], 256), F32)
-    for at in range(0, depth, chunk):
-        parts = []
-        for lane in range(at, at + chunk, LANES):
-            lanes = slice(lane, lane + LANES)
-            same = m_sym == jnp.broadcast_to(k_ref[0:1, lanes], m_sym.shape)
-            parts.append(jnp.where(same, int_ref[:, lanes], jnp.zeros((), BF16)))
-        screened = jnp.concatenate(parts, axis=1)
-        total += jnp.dot(screened, kept[at : at + chunk, :], preferred_element_type=F32)
-    turned = jnp.transpose(total)
-    even = core == 0
-    for z in range(4):
-        for half in range(2):
-            at = half * 128 + z * 2 * BASE
-            low, high = turned[at : at + BASE, :], turned[at + BASE : at + 2 * BASE, :]
-            rows = slice(half * BASE, half * BASE + BASE)
-            keep_ref[z, rows, :] = jnp.where(even, low, high)
-            send_ref[z, rows, :] = jnp.where(even, high, low)
+            for start in range(at, at + chunk, LANES):
+                lanes = slice(start, start + LANES)
+                same = m_sym == jnp.broadcast_to(k_ref[0:1, lanes], m_sym.shape)
+                parts.append(jnp.where(same, local[rows, lanes], nought))
+            screened = jnp.concatenate(parts, axis=1)
+            total += jnp.dot(screened, kept[at : at + chunk, :], preferred_element_type=F32)
+        turned = jnp.transpose(total)
+        for z in range(4):
+            for half in range(2):
+                at = half * 128 + z * 2 * BASE
+                low, high = turned[at : at + BASE, :], turned[at + BASE : at + 2 * BASE, :]
+                slots = slice(half * BASE, half * BASE + BASE)
+                keep_ref[z, slots, rows] = jnp.where(even, low, high)
+                send_ref[z, slots, rows] = jnp.where(even, high, low)
+        return carry
+
+    lax.fori_loop(0, tiles, multiply, 0)
 
 
 def share_kernel(keep_ref, got_ref, own_ref, *out_refs):
@@ -420,7 +440,7 @@
         return pl.pallas_call(
             kernel,
             out_shape=out_shape,
-            in_specs=[whole()] * len(operands),
+            in_specs=kw.pop("in_specs", [whole()] * len(operands)),
             out_specs=kw.pop("out_specs", jax.tree.map(lambda _: whole(), out_shape)),
             compiler_params=params(mib),
             name=name,
@@ -444,7 +464,7 @@
             shape((8, pairs), I32),
             shape((8, pairs), I32),
             shape((8, pairs), I32),
-            shape((8 * BASE, 8 * SPILL), BF16),
+            shape((8 * BASE, 8 * ROOM), BF16),
             shape((16, kblock), BF16),
             shape((kblock, LANES), BF16),
             shape((m_dev, LANES), BF16),
@@ -466,23 +486,19 @@
     spreading = jnp.broadcast_to(jnp.concatenate([mine, got], axis=1)[None], (rows, PLACES, stored))
     gathered = lax.all_to_all(spreading, "row", split_axis=0, concat_axis=0, tiled=True)
 
-    keep, send = pl.pallas_call(
+    keep, send = call(
         product_kernel,
-        grid=(m_dev // 512,),
-        out_shape=(shape((4, CAP, m_dev), F32),) * 2,
-        in_specs=[
-            whole(),
-            pl.BlockSpec((512, kblock), lambda i: (i, 0)),
-            whole(),
-            whole(),
-            pl.BlockSpec((512, LANES), lambda i: (i, 0)),
-            whole(),
+        "product",
+        (shape((4, CAP, m_dev), F32),) * 2,
+        (gathered, integrals, k_sym, k_col, m_sym, spread),
+        30,
+        in_specs=[whole(), pl.BlockSpec(memory_space=pl.ANY)] + [whole()] * 4,
+        scratch_shapes=[
+            pltpu.VMEM((kblock, 256), BF16),
+            pltpu.VMEM((m_dev, kblock), BF16),
+            pltpu.SemaphoreType.DMA((m_dev // TILE,)),
         ],
-        out_specs=(pl.BlockSpec((4, CAP, 512), lambda i: (0, 0, i)),) * 2,
-        scratch_shapes=[pltpu.VMEM((kblock, 256), BF16)],
-        compiler_params=params(24),
-        name="product",
-    )(gathered, integrals, k_sym, k_col, m_sym, spread)
+    )
     partner = lax.ppermute(send, "col", swap)
     shares = call(
         share_kernel,

time: 73 us -> 68.9 us (0.944)
  Pallas kernels: 18.4 us -> 14.4 us
    pallas_call x6, Pallas kernels: 18.4 us -> 14.4 us  [call(): pl.pallas_call(kernel, out_shape=out_shape, in_specs=kw.pop('in_specs', [...]
where the time goes in v3:
time: 68.9 us; the launch traced here: 68.6 us
  blocking collectives  26.3 us (38%)
  starting transfers between devices  14.6 us (21%)
  Pallas kernels  14.4 us (21%)
  waiting for transfers between devices  9.84 us (14%)
  local copies, waits for them, and re-layouts  2.36 us (3%)
  loops' own time  0.82 us (1%)
    all_to_all x1, blocking collectives, body(): lax.all_to_all(spreading, 'row', split_axis=0, concat_axis=0, tiled=True)  26.3 us
    pallas_call x6, Pallas kernels, call(): pl.pallas_call(kernel, out_shape=out_shape, in_specs=kw.pop('in_specs', [...  14.4 us
    ppermute x3, starting transfers between devices, body(): lax.ppermute(ordered[d], 'col', hops[d])  5.82 us
    ppermute x3, waiting for transfers between devices, body(): lax.ppermute(shares[d], 'col', hops[d])  5.09 us
    ppermute x3, starting transfers between devices, body(): lax.ppermute(shares[d], 'col', hops[d])  4.09 us
    ppermute x1, starting transfers between devices, body(): partner = lax.ppermute(send, 'col', swap)  2.37 us
    ppermute x1, waiting for transfers between devices, body(): partner = lax.ppermute(send, 'col', swap)  2.29 us
    ppermute x3, waiting for transfers between devices, body(): lax.ppermute(ordered[d], 'col', hops[d])  1.58 us
  transfers between devices with their start and end apart: 9, of which 5 were waited for; matrix products, arithmetic and copies ran while one was open for 2% of the time, Pallas kernels for 6%

profile of v3, /device:TPU:1, one launch (start us, length us, event | category | flops | bytes accessed | tf_op | source)
XLA Modules:
  0.0 68.6 jit_solution(16867355970803635004)
XLA Ops:
  0.0 0.8 %copy.14 = s32[1,2,16,256]{3,2,1,0:T(8,128)S(1)} copy(s32[1,2,16,256]{3,1,2,0:T(2,128)} %bitcast.16) | data formatting | bytes 65536
  0.8 0.1 constant_dynamic-slice_fusion
  0.8 0.1 reshape.106.own_orbs
  0.9 1.5 %collective-permute-start.4 = (s32[2,256]{1,0:T(2,128)S(1)}, s32[2,256]{1,0:T(2,128)S(1)}, u32[]{:S(2)}, u32[]{:S(2)}) collective-permute-start(s32[2,256]{1,0:T(2,128)S(1)} %reshape.106.own_orbs), channel_id=1, source_target_pairs={{0,1},{1,0},{2,3},{3,2},{4,5},{5,4},{6,7},{7,6},{8,9},{9,8},{10,11... | collective-permute-start | bytes 6152 | tf_op jit(solution)/shard_map/ppermute | solution.py:453
  2.4 1.4 %order.1 = (bf16[64,1024]{1,0:T(8,128)(2,1)S(1)}, bf16[64,1024]{1,0:T(8,128)(2,1)S(1)}, bf16[64,1024]{1,0:T(8,128)(2,1)S(1)}, bf16[64,1024]{1,0:T(8,128)(2,1)S(1)}) custom-call(s32[1,256]{1,0:T(1,128)} %bitcast.13.map_ref, bf16[256,1024]{1,0:T(8,128)(2,1)} %amp_ref.1), custom_call_target="tpu_custom_call" | custom-call | tf_op jit(solution)/shard_map/order/pallas_call | solution.py:440
  3.7 1.8 %collective-permute-start.5 = (bf16[64,1024]{1,0:T(8,128)(2,1)S(1)}, bf16[64,1024]{1,0:T(8,128)(2,1)S(1)}, u32[]{:S(2)}, u32[]{:S(2)}) collective-permute-start(bf16[64,1024]{1,0:T(8,128)(2,1)S(1)} %get-tuple-element.403), channel_id=1, source_target_pairs={{0,2},{1,3},{2,4},{3,5},{4,6},{5,7},{6,0},{7,1},{8,10},{9,11},{10,... | collective-permute-start | bytes 393224 | tf_op jit(solution)/shard_map/ppermute | solution.py:456
  5.5 3.3 %collective-permute-start.6 = (bf16[64,1024]{1,0:T(8,128)(2,1)S(1)}, bf16[64,1024]{1,0:T(8,128)(2,1)S(1)}, u32[]{:S(2)}, u32[]{:S(2)}) collective-permute-start(bf16[64,1024]{1,0:T(8,128)(2,1)S(1)} %get-tuple-element.404), channel_id=1, source_target_pairs={{0,4},{1,5},{2,6},{3,7},{4,0},{5,1},{6,2},{7,3},{8,12},{9,13},{10,... | collective-permute-start | bytes 393224 | tf_op jit(solution)/shard_map/ppermute | solution.py:456
  8.8 0.7 %collective-permute-start.7 = (bf16[64,1024]{1,0:T(8,128)(2,1)S(1)}, bf16[64,1024]{1,0:T(8,128)(2,1)S(1)}, u32[]{:S(2)}, u32[]{:S(2)}) collective-permute-start(bf16[64,1024]{1,0:T(8,128)(2,1)S(1)} %get-tuple-element.405), channel_id=1, source_target_pairs={{0,6},{1,7},{2,0},{3,1},{4,2},{5,3},{6,4},{7,5},{8,14},{9,15},{10,... | collective-permute-start | bytes 393224 | tf_op jit(solution)/shard_map/ppermute | solution.py:456
  9.6 0.7 %pad_bitcast_fusion.2.virt_ref = s32[8,128]{1,0:T(8,128)S(1)} fusion(s32[800]{0:T(1024)} %param.16), kind=kLoop, calls=%fused_computation.21 | loop fusion | bytes 7296 | tf_op jit(solution)/shard_map/reshape | solution.py:459
  10.2 0.7 pad_bitcast_fusion.3.occ_ref
  10.9 0.0 collective-permute-done.4.other_orbs
  10.9 2.8 %symbols.1 = (s32[8,1024]{1,0:T(8,128)S(1)}, s32[8,1024]{1,0:T(8,128)S(1)}, s32[8,1024]{1,0:T(8,128)S(1)}, bf16[128,512]{1,0:T(8,128)(2,1)S(1)}, bf16[16,4096]{1...) custom-call(s32[1,128]{1,0:T(1,128)S(1)} %pad_bitcast_fusion.3.occ_r, ...), custom_call_target="tpu_custom_call" | custom-call | tf_op jit(solution)/shard_map/symbols/pallas_call | solution.py:440
  13.7 0.0 collective-permute-done.5.b_ref
  13.7 1.6 %collective-permute-done.6.c_ref = bf16[64,1024]{1,0:T(8,128)(2,1)S(1)} collective-permute-done((bf16[64,1024]{1,0:T(8,128)(2,1)S(1)}, bf16[64,1024]{1,0:T(8,128)(2,1)S(1)}, u32[]{:S(2)}, u32[]{:S(2)}) %collective-permute-start.6) | collective-permute-done | bytes 131104 | tf_op jit(solution)/shard_map/ppermute | solution.py:456
  15.3 0.0 collective-permute-done.7.d_ref
  15.3 0.6 compact.1
  15.9 0.9 %collective-permute-start.8 = (bf16[176,128]{1,0:T(8,128)(2,1)S(1)}, bf16[176,128]{1,0:T(8,128)(2,1)S(1)}, u32[]{:S(2)}, u32[]{:S(2)}) collective-permute-start(bf16[176,128]{1,0:T(8,128)(2,1)S(1)} %get-tuple-element.411), channel_id=1, source_target_pairs={{0,1},{1,0},{2,3},{3,2},{4,5},{5,4},{6,7},{7,6},{8,9},{9,8},{10,11... | collective-permute-start | bytes 135176 | tf_op jit(solution)/shard_map/ppermute | solution.py:485
  16.7 0.9 %collective-permute-done.8 = bf16[176,128]{1,0:T(8,128)(2,1)S(1)} collective-permute-done((bf16[176,128]{1,0:T(8,128)(2,1)S(1)}, bf16[176,128]{1,0:T(8,128)(2,1)S(1)}, u32[]{:S(2)}, u32[]{:S(2)}) %collective-permute-start.8) | collective-permute-done | bytes 45088 | tf_op jit(solution)/shard_map/ppermute | solution.py:485
  17.6 0.1 broadcast_in_dim.2
  17.7 26.3 %all_to_all.22.amp_ref = bf16[16,176,256]{2,1,0:T(8,128)(2,1)S(1)} all-to-all(bf16[16,176,256]{2,1,0:T(8,128)(2,1)S(1)} %broadcast_in_dim.2), channel_id=1, replica_groups=mesh['row'=16,'col'=8] {'row'}, dimensions={0} | all-to-all | bytes 2883584 | tf_op jit(solution)/shard_map/all_to_all | solution.py:487
  44.0 8.2 %product.1 = (f32[4,32,2048]{2,1,0:T(8,128)S(1)}, f32[4,32,2048]{2,1,0:T(8,128)S(1)}) custom-call(bf16[16,176,256]{2,1,0:T(8,128)(2,1)S(1)} %all_to_all.22.amp_ref, bf16[2048,4096]{1,0:T(8,128)(2,1)} %int_ref.1, bf16[16,4096]{1,0:T(8,128)(2,1)S(1)} %get-tuple-element.412.k_ref, bf16[4096,128]{1,0:T(8,128)(2,1)S(1)} %get-tuple-element.413.k_col_ref, ...), custom_call_target="tpu_custom_call" | custom-call | tf_op jit(solution)/shard_map/product/pallas_call | solution.py:440
  52.2 0.0 copy-start.1
  52.3 2.4 %collective-permute-start.9 = (f32[4,32,2048]{2,1,0:T(8,128)S(1)}, f32[4,32,2048]{2,1,0:T(8,128)S(1)}, u32[]{:S(2)}, u32[]{:S(2)}) collective-permute-start(f32[4,32,2048]{2,1,0:T(8,128)S(1)} %get-tuple-element.417), channel_id=1, source_target_pairs={{0,1},{1,0},{2,3},{3,2},{4,5},{5,4},{6,7},{7,6},{8,9},{9,8},{10,11... | collective-permute-start | bytes 3145736 | tf_op jit(solution)/shard_map/ppermute | solution.py:502
  54.6 2.3 %collective-permute-done.9.got_ref = f32[4,32,2048]{2,1,0:T(8,128)S(1)} collective-permute-done((f32[4,32,2048]{2,1,0:T(8,128)S(1)}, f32[4,32,2048]{2,1,0:T(8,128)S(1)}, u32[]{:S(2)}, u32[]{:S(2)}) %collective-permute-start.9) | collective-permute-done | bytes 1048608 | tf_op jit(solution)/shard_map/ppermute | solution.py:502
  56.9 0.3 share.1
  57.3 1.0 %collective-permute-start.10 = (s16[32,2048]{1,0:T(8,128)(2,1)S(1)}, s16[32,2048]{1,0:T(8,128)(2,1)S(1)}, u32[]{:S(2)}, u32[]{:S(2)}) collective-permute-start(s16[32,2048]{1,0:T(8,128)(2,1)S(1)} %get-tuple-element.419), channel_id=1, source_target_pairs={{0,2},{1,3},{2,4},{3,5},{4,6},{5,7},{6,0},{7,1},{8,10},{9,11},{10,... | collective-permute-start | bytes 393224 | tf_op jit(solution)/shard_map/ppermute | solution.py:509
  58.3 2.1 %collective-permute-start.11 = (s16[32,2048]{1,0:T(8,128)(2,1)S(1)}, s16[32,2048]{1,0:T(8,128)(2,1)S(1)}, u32[]{:S(2)}, u32[]{:S(2)}) collective-permute-start(s16[32,2048]{1,0:T(8,128)(2,1)S(1)} %get-tuple-element.420), channel_id=1, source_target_pairs={{0,4},{1,5},{2,6},{3,7},{4,0},{5,1},{6,2},{7,3},{8,12},{9,13},{10,... | collective-permute-start | bytes 393224 | tf_op jit(solution)/shard_map/ppermute | solution.py:509
  60.4 1.0 %collective-permute-start.12 = (s16[32,2048]{1,0:T(8,128)(2,1)S(1)}, s16[32,2048]{1,0:T(8,128)(2,1)S(1)}, u32[]{:S(2)}, u32[]{:S(2)}) collective-permute-start(s16[32,2048]{1,0:T(8,128)(2,1)S(1)} %get-tuple-element.421), channel_id=1, source_target_pairs={{0,6},{1,7},{2,0},{3,1},{4,2},{5,3},{6,4},{7,5},{8,14},{9,15},{10,... | collective-permute-start | bytes 393224 | tf_op jit(solution)/shard_map/ppermute | solution.py:509
  61.3 1.9 %collective-permute-done.10.a_ref = s16[32,2048]{1,0:T(8,128)(2,1)S(1)} collective-permute-done((s16[32,2048]{1,0:T(8,128)(2,1)S(1)}, s16[32,2048]{1,0:T(8,128)(2,1)S(1)}, u32[]{:S(2)}, u32[]{:S(2)}) %collective-permute-start.10) | collective-permute-done | bytes 131104 | tf_op jit(solution)/shard_map/ppermute | solution.py:509
  63.2 3.2 %collective-permute-done.11.b_ref = s16[32,2048]{1,0:T(8,128)(2,1)S(1)} collective-permute-done((s16[32,2048]{1,0:T(8,128)(2,1)S(1)}, s16[32,2048]{1,0:T(8,128)(2,1)S(1)}, u32[]{:S(2)}, u32[]{:S(2)}) %collective-permute-start.11) | collective-permute-done | bytes 131104 | tf_op jit(solution)/shard_map/ppermute | solution.py:509
  66.4 1.2 %expand.1 = bf16[2048,128]{1,0:T(8,128)(2,1)} custom-call(f32[32,2048]{1,0:T(8,128)S(1)} %get-tuple-element.418.own_ref, s16[32,2048]{1,0:T(8,128)(2,1)S(1)} %collective-permute-done.10.a_ref, s16[32,2048]{1,0:T(8,128)(2,1)S(1)} %collective-permute-done.11.b_ref, s16[32,2048]{1,0:T(8,128)(2,1)S(1)} %collective-permute-done.12.c_ref, ...), custom_call_target="tpu_custom_call" | custom-call | tf_op jit(solution)/shard_map/expand/pallas_call | solution.py:440
  67.6 0.8 %while.22 = (s32[]{:T(128)}, bf16[2048,128]{1,0:T(8,128)(2,1)}, s32[100]{0:T(128)}, s32[800]{0:T(1024)}, s32[2,4096]{1,0:T(2,128)}, /*index=5*/s32[2,1024]{1,0:T...) while((s32[]{:T(128)}, bf16[2048,128]{1,0:T(8,128)(2,1)}, ...), condition=%region_3.4_spmd, body=%region_0.3_spmd | while | flops 134819376 | bytes 18436136 | solution.py:512
  (3 shorter events, 0.0 us)
Async XLA Ops:
  0.9 10.0 %collective-permute-start.4 = (s32[2,256]{1,0:T(2,128)S(1)}, s32[2,256]{1,0:T(2,128)S(1)}, u32[]{:S(2)}, u32[]{:S(2)}) collective-permute-start(s32[2,256]{1,0:T(2,128)S(1)} %reshape.106.own_orbs), channel_id=1, source_target_pairs={{0,1},{1,0},{2,3},{3,2},{4,5},{5,4},{6,7},{7,6},{8,9},{9,8},{10,11... | collective-permute-start | bytes 6152 | tf_op jit(solution)/shard_map/ppermute | solution.py:453
  3.7 10.0 %collective-permute-start.5 = (bf16[64,1024]{1,0:T(8,128)(2,1)S(1)}, bf16[64,1024]{1,0:T(8,128)(2,1)S(1)}, u32[]{:S(2)}, u32[]{:S(2)}) collective-permute-start(bf16[64,1024]{1,0:T(8,128)(2,1)S(1)} %get-tuple-element.403), channel_id=1, source_target_pairs={{0,2},{1,3},{2,4},{3,5},{4,6},{5,7},{6,0},{7,1},{8,10},{9,11},{10,... | collective-permute-start | bytes 393224 | tf_op jit(solution)/shard_map/ppermute | solution.py:456
  5.5 9.8 %collective-permute-start.6 = (bf16[64,1024]{1,0:T(8,128)(2,1)S(1)}, bf16[64,1024]{1,0:T(8,128)(2,1)S(1)}, u32[]{:S(2)}, u32[]{:S(2)}) collective-permute-start(bf16[64,1024]{1,0:T(8,128)(2,1)S(1)} %get-tuple-element.404), channel_id=1, source_target_pairs={{0,4},{1,5},{2,6},{3,7},{4,0},{5,1},{6,2},{7,3},{8,12},{9,13},{10,... | collective-permute-start | bytes 393224 | tf_op jit(solution)/shard_map/ppermute | solution.py:456
  8.8 6.5 %collective-permute-start.7 = (bf16[64,1024]{1,0:T(8,128)(2,1)S(1)}, bf16[64,1024]{1,0:T(8,128)(2,1)S(1)}, u32[]{:S(2)}, u32[]{:S(2)}) collective-permute-start(bf16[64,1024]{1,0:T(8,128)(2,1)S(1)} %get-tuple-element.405), channel_id=1, source_target_pairs={{0,6},{1,7},{2,0},{3,1},{4,2},{5,3},{6,4},{7,5},{8,14},{9,15},{10,... | collective-permute-start | bytes 393224 | tf_op jit(solution)/shard_map/ppermute | solution.py:456
  15.9 1.8 %collective-permute-start.8 = (bf16[176,128]{1,0:T(8,128)(2,1)S(1)}, bf16[176,128]{1,0:T(8,128)(2,1)S(1)}, u32[]{:S(2)}, u32[]{:S(2)}) collective-permute-start(bf16[176,128]{1,0:T(8,128)(2,1)S(1)} %get-tuple-element.411), channel_id=1, source_target_pairs={{0,1},{1,0},{2,3},{3,2},{4,5},{5,4},{6,7},{7,6},{8,9},{9,8},{10,11... | collective-permute-start | bytes 135176 | tf_op jit(solution)/shard_map/ppermute | solution.py:485
  52.2 15.4 %copy-start.1 = (s32[2,2048]{1,0:T(2,128)S(1)}, s32[2,2048]{1,0:T(2,128)}, u32[]{:S(2)}) copy-start(s32[2,2048]{1,0:T(2,128)} %m_orbs.1) | copy-start | bytes 49156
  52.3 4.7 %collective-permute-start.9 = (f32[4,32,2048]{2,1,0:T(8,128)S(1)}, f32[4,32,2048]{2,1,0:T(8,128)S(1)}, u32[]{:S(2)}, u32[]{:S(2)}) collective-permute-start(f32[4,32,2048]{2,1,0:T(8,128)S(1)} %get-tuple-element.417), channel_id=1, source_target_pairs={{0,1},{1,0},{2,3},{3,2},{4,5},{5,4},{6,7},{7,6},{8,9},{9,8},{10,11... | collective-permute-start | bytes 3145736 | tf_op jit(solution)/shard_map/ppermute | solution.py:502
  57.3 6.0 %collective-permute-start.10 = (s16[32,2048]{1,0:T(8,128)(2,1)S(1)}, s16[32,2048]{1,0:T(8,128)(2,1)S(1)}, u32[]{:S(2)}, u32[]{:S(2)}) collective-permute-start(s16[32,2048]{1,0:T(8,128)(2,1)S(1)} %get-tuple-element.419), channel_id=1, source_target_pairs={{0,2},{1,3},{2,4},{3,5},{4,6},{5,7},{6,0},{7,1},{8,10},{9,11},{10,... | collective-permute-start | bytes 393224 | tf_op jit(solution)/shard_map/ppermute | solution.py:509
  58.3 8.2 %collective-permute-start.11 = (s16[32,2048]{1,0:T(8,128)(2,1)S(1)}, s16[32,2048]{1,0:T(8,128)(2,1)S(1)}, u32[]{:S(2)}, u32[]{:S(2)}) collective-permute-start(s16[32,2048]{1,0:T(8,128)(2,1)S(1)} %get-tuple-element.420), channel_id=1, source_target_pairs={{0,4},{1,5},{2,6},{3,7},{4,0},{5,1},{6,2},{7,3},{8,12},{9,13},{10,... | collective-permute-start | bytes 393224 | tf_op jit(solution)/shard_map/ppermute | solution.py:509
  60.4 6.1 %collective-permute-start.12 = (s16[32,2048]{1,0:T(8,128)(2,1)S(1)}, s16[32,2048]{1,0:T(8,128)(2,1)S(1)}, u32[]{:S(2)}, u32[]{:S(2)}) collective-permute-start(s16[32,2048]{1,0:T(8,128)(2,1)S(1)} %get-tuple-element.421), channel_id=1, source_target_pairs={{0,6},{1,7},{2,0},{3,1},{4,2},{5,3},{6,4},{7,5},{8,14},{9,15},{10,... | collective-permute-start | bytes 393224 | tf_op jit(solution)/shard_map/ppermute | solution.py:509

commit v4 on v3

--- a/solution.py
+++ b/solution.py
@@ -68,8 +68,8 @@
 
 
 def symbols_kernel(
-    occ_ref, virt_ref, occ_orbs, k_orbs, m_orbs, own_orbs, other_orbs,
-    occ_out, rank_out, place_out, spread_out, k_out, k_col_out, m_out, own_out, other_out, bad_out,
+    occ_ref, virt_ref, occ_orbs, k_orbs, m_orbs, other_orbs,
+    occ_out, rank_out, place_out, spread_out, k_out, k_col_out, m_out, own_out, other_out, bad_out, other_col,
 ):
     core = lax.axis_index("col") & 1
     occ = pack_labels(occ_ref[0:1, :])
@@ -105,13 +105,15 @@
         wide = sym.astype(F32)
         k_out[:, start : start + LANES] = jnp.concatenate([wide, wide], axis=0).astype(BF16)
         k_col_out[start : start + LANES, :] = as_column(sym).astype(BF16)
+        other_col[start : start + LANES, :] = as_column(pair_symbols(virt, other_orbs, start)).astype(BF16)
     for start in range(0, m_orbs.shape[1], LANES):
         m_out[start : start + LANES, :] = as_column(pair_symbols(virt, m_orbs, start)).astype(BF16)
     i, j = iota((LANES, 2 * LANES), 0), iota((LANES, 2 * LANES), 1)
     pick = one_hot(j == (i >> 1) * 4 + core * 2 + (i & 1))
-    for orbs, out in ((own_orbs, own_out), (other_orbs, other_out)):
-        column = jnp.concatenate([as_column(pair_symbols(virt, orbs, s)) for s in (0, LANES)], axis=0)
-        out[...] = jnp.dot(pick, column.astype(BF16), preferred_element_type=F32)
+    mine = pl.multiple_of(lax.axis_index("row") * 16, 16)
+    for ref, out in ((k_col_out, own_out), (other_col, other_out)):
+        column = jnp.concatenate([ref[pl.ds(r * 256 + mine, 16), :] for r in range(16)], axis=0)
+        out[...] = jnp.dot(pick, column, preferred_element_type=F32)
 
 
 def compact_kernel(a_ref, b_ref, c_ref, d_ref, own_ref, other_ref, occ_ref, place_ref, mine_out, theirs_out):
@@ -447,14 +449,10 @@
             **kw,
         )(*operands)
 
-    own_orbs = lax.dynamic_slice_in_dim(
-        k_orbs.reshape(2, rows, stored), lax.axis_index("row") * 16, 16, axis=2
-    ).reshape(2, stored)
-    other_orbs = lax.ppermute(own_orbs, "col", swap)
-
     ordered = call(order_kernel, "order", (shape((64, pairs), BF16),) * 4, (store_map.reshape(1, stored), amp_store))
     arrived = [ordered[0]] + [lax.ppermute(ordered[d], "col", hops[d]) for d in range(1, 4)]
 
+    other_orbs = lax.ppermute(k_orbs, "col", swap)
     occ_lab = jnp.pad(occ_irrep, (0, LANES - occ_irrep.shape[0])).reshape(1, LANES)
     virt_lab = jnp.pad(virt_irrep, (0, 8 * LANES - virt_irrep.shape[0])).reshape(8, LANES)
     occ_sym, rank, place, spread, k_sym, k_col, m_sym, own_sym, other_sym, bad = call(
@@ -472,8 +470,9 @@
             shape((LANES, LANES), F32),
             shape((1, 1), I32),
         ),
-        (occ_lab, virt_lab, occ_orbs, k_orbs, m_orbs, own_orbs, other_orbs),
+        (occ_lab, virt_lab, occ_orbs, k_orbs, m_orbs, other_orbs),
         out_specs=(whole(),) * 9 + (scalars(),),
+        scratch_shapes=[pltpu.VMEM((kblock, LANES), BF16)],
     )
 
     mine, theirs = call(
@@ -509,14 +508,11 @@
     sums = [shares[0]] + [lax.ppermute(shares[d], "col", hops[d]) for d in range(1, 4)]
     result = call(expand_kernel, "expand", shape((m_dev, LANES), BF16), (*sums, m_sym, occ_sym, rank))
 
-    return lax.while_loop(
-        lambda state: state[0] > 0,
-        lambda state: (
-            jnp.zeros((), I32),
-            plain(amp_store, store_map, integrals, occ_irrep, virt_irrep, occ_orbs, k_orbs, m_orbs),
-        ),
-        (bad[0, 0], result),
-    )[1]
+    return lax.cond(
+        bad[0, 0] > 0,
+        lambda: plain(amp_store, store_map, integrals, occ_irrep, virt_irrep, occ_orbs, k_orbs, m_orbs),
+        lambda: result,
+    )
 
 
 def solution(mesh):

time: 68.9 us -> 67.4 us (0.978)
  waiting for transfers between devices: 9.84 us -> 8.5 us
  local copies, waits for them, and re-layouts: 2.36 us -> 1.49 us
  between operations: 0.23 us -> 0.98 us
  Pallas kernels: 14.4 us -> 15.1 us
    unnamed x3 -> x14, local copies, waits for them, and re-layouts: 0.77 us -> 0.04 us
    pallas_call x6, Pallas kernels: 14.4 us -> 15.1 us  [call(): pl.pallas_call(kernel, out_shape=out_shape, in_specs=kw.pop('in_specs', [...]
    ppermute x3, waiting for transfers between devices: 1.58 us -> 0.89 us  [body(): lax.ppermute(ordered[d], 'col', hops[d])]
  transfers between devices with their start and end apart: 9 -> 9, of which waited for: 5 -> 5; matrix products, arithmetic and copies ran while one was open for 2% -> 2% of each run, Pallas kernels for 6% -> 7%
where the time goes in v4:
time: 67.4 us; the launch traced here: 67.2 us
  blocking collectives  26.3 us (39%)
  Pallas kernels  15.1 us (22%)
  starting transfers between devices  14.6 us (22%)
  waiting for transfers between devices  8.5 us (13%)
  local copies, waits for them, and re-layouts  1.49 us (2%)
  between operations  0.98 us (1%)
    all_to_all x1, blocking collectives, body(): lax.all_to_all(spreading, 'row', split_axis=0, concat_axis=0, tiled=True)  26.3 us
    pallas_call x6, Pallas kernels, call(): pl.pallas_call(kernel, out_shape=out_shape, in_specs=kw.pop('in_specs', [...  15.1 us
    ppermute x3, starting transfers between devices, body(): lax.ppermute(ordered[d], 'col', hops[d])  5.82 us
    ppermute x3, waiting for transfers between devices, body(): lax.ppermute(shares[d], 'col', hops[d])  4.44 us
    ppermute x3, starting transfers between devices, body(): lax.ppermute(shares[d], 'col', hops[d])  4.09 us
    ppermute x1, starting transfers between devices, body(): partner = lax.ppermute(send, 'col', swap)  2.37 us
    ppermute x1, waiting for transfers between devices, body(): partner = lax.ppermute(send, 'col', swap)  2.29 us
    ppermute x1, starting transfers between devices, body(): other_orbs = lax.ppermute(k_orbs, 'col', swap)  1.42 us
  transfers between devices with their start and end apart: 9, of which 5 were waited for; matrix products, arithmetic and copies ran while one was open for 2% of the time, Pallas kernels for 7%

profile of v4, /device:TPU:1, one launch (start us, length us, event | category | flops | bytes accessed | tf_op | source)
XLA Modules:
  0.0 67.2 jit_solution(2510118933409179094)
XLA Ops:
  0.0 1.4 %collective-permute-start.4 = (s32[2,4096]{1,0:T(2,128)}, s32[2,4096]{1,0:T(2,128)S(1)}, u32[]{:S(2)}, u32[]{:S(2)}) collective-permute-start(s32[2,4096]{1,0:T(2,128)} %k_orbs.1), channel_id=1, source_target_pairs={{0,1},{1,0},{2,3},{3,2},{4,5},{5,4},{6,7},{7,6},{8,9},{9,8},{10,11... | collective-permute-start | bytes 98312 | tf_op jit(solution)/shard_map/ppermute | solution.py:455
  1.4 1.4 %order.1 = (bf16[64,1024]{1,0:T(8,128)(2,1)S(1)}, bf16[64,1024]{1,0:T(8,128)(2,1)S(1)}, bf16[64,1024]{1,0:T(8,128)(2,1)S(1)}, bf16[64,1024]{1,0:T(8,128)(2,1)S(1)}) custom-call(s32[1,256]{1,0:T(1,128)} %bitcast.37, bf16[256,1024]{1,0:T(8,128)(2,1)} %amp_ref.1), custom_call_target="tpu_custom_call" | custom-call | tf_op jit(solution)/shard_map/order/pallas_call | solution.py:442
  2.8 1.8 %collective-permute-start.5 = (bf16[64,1024]{1,0:T(8,128)(2,1)S(1)}, bf16[64,1024]{1,0:T(8,128)(2,1)S(1)}, u32[]{:S(2)}, u32[]{:S(2)}) collective-permute-start(bf16[64,1024]{1,0:T(8,128)(2,1)S(1)} %get-tuple-element.381), channel_id=1, source_target_pairs={{0,2},{1,3},{2,4},{3,5},{4,6},{5,7},{6,0},{7,1},{8,10},{9,11},{10,... | collective-permute-start | bytes 393224 | tf_op jit(solution)/shard_map/ppermute | solution.py:453
  4.6 3.3 %collective-permute-start.6 = (bf16[64,1024]{1,0:T(8,128)(2,1)S(1)}, bf16[64,1024]{1,0:T(8,128)(2,1)S(1)}, u32[]{:S(2)}, u32[]{:S(2)}) collective-permute-start(bf16[64,1024]{1,0:T(8,128)(2,1)S(1)} %get-tuple-element.382), channel_id=1, source_target_pairs={{0,4},{1,5},{2,6},{3,7},{4,0},{5,1},{6,2},{7,3},{8,12},{9,13},{10,... | collective-permute-start | bytes 393224 | tf_op jit(solution)/shard_map/ppermute | solution.py:453
  7.9 0.7 %collective-permute-start.7 = (bf16[64,1024]{1,0:T(8,128)(2,1)S(1)}, bf16[64,1024]{1,0:T(8,128)(2,1)S(1)}, u32[]{:S(2)}, u32[]{:S(2)}) collective-permute-start(bf16[64,1024]{1,0:T(8,128)(2,1)S(1)} %get-tuple-element.383), channel_id=1, source_target_pairs={{0,6},{1,7},{2,0},{3,1},{4,2},{5,3},{6,4},{7,5},{8,14},{9,15},{10,... | collective-permute-start | bytes 393224 | tf_op jit(solution)/shard_map/ppermute | solution.py:453
  8.6 0.7 %pad_bitcast_fusion.2.virt_ref = s32[8,128]{1,0:T(8,128)S(1)} fusion(s32[800]{0:T(1024)} %param.16), kind=kLoop, calls=%fused_computation.21 | loop fusion | bytes 7296 | tf_op jit(solution)/shard_map/reshape | solution.py:457
  9.3 0.7 pad_bitcast_fusion.3.occ_ref
  10.0 3.5 %symbols.1 = (s32[8,1024]{1,0:T(8,128)S(1)}, s32[8,1024]{1,0:T(8,128)S(1)}, s32[8,1024]{1,0:T(8,128)S(1)}, bf16[128,512]{1,0:T(8,128)(2,1)S(1)}, bf16[16,4096]{1...) custom-call(s32[1,128]{1,0:T(1,128)S(1)} %pad_bitcast_fusion.3.occ_r, ...), custom_call_target="tpu_custom_call" | custom-call | tf_op jit(solution)/shard_map/symbols/pallas_call | solution.py:442
  13.5 0.9 %collective-permute-done.6.c_ref = bf16[64,1024]{1,0:T(8,128)(2,1)S(1)} collective-permute-done((bf16[64,1024]{1,0:T(8,128)(2,1)S(1)}, bf16[64,1024]{1,0:T(8,128)(2,1)S(1)}, u32[]{:S(2)}, u32[]{:S(2)}) %collective-permute-start.6) | collective-permute-done | bytes 131104 | tf_op jit(solution)/shard_map/ppermute | solution.py:453
  14.4 0.6 compact.1
  14.9 0.9 %collective-permute-start.8 = (bf16[176,128]{1,0:T(8,128)(2,1)S(1)}, bf16[176,128]{1,0:T(8,128)(2,1)S(1)}, u32[]{:S(2)}, u32[]{:S(2)}) collective-permute-start(bf16[176,128]{1,0:T(8,128)(2,1)S(1)} %get-tuple-element.389), channel_id=1, source_target_pairs={{0,1},{1,0},{2,3},{3,2},{4,5},{5,4},{6,7},{7,6},{8,9},{9,8},{10,11... | collective-permute-start | bytes 135176 | tf_op jit(solution)/shard_map/ppermute | solution.py:484
  15.8 0.9 %collective-permute-done.8 = bf16[176,128]{1,0:T(8,128)(2,1)S(1)} collective-permute-done((bf16[176,128]{1,0:T(8,128)(2,1)S(1)}, bf16[176,128]{1,0:T(8,128)(2,1)S(1)}, u32[]{:S(2)}, u32[]{:S(2)}) %collective-permute-start.8) | collective-permute-done | bytes 45088 | tf_op jit(solution)/shard_map/ppermute | solution.py:484
  16.7 0.1 broadcast_in_dim.2
  16.8 26.3 %all_to_all.22.amp_ref = bf16[16,176,256]{2,1,0:T(8,128)(2,1)S(1)} all-to-all(bf16[16,176,256]{2,1,0:T(8,128)(2,1)S(1)} %broadcast_in_dim.2), channel_id=1, replica_groups=mesh['row'=16,'col'=8] {'row'}, dimensions={0} | all-to-all | bytes 2883584 | tf_op jit(solution)/shard_map/all_to_all | solution.py:486
  43.1 8.2 %product.1 = (f32[4,32,2048]{2,1,0:T(8,128)S(1)}, f32[4,32,2048]{2,1,0:T(8,128)S(1)}) custom-call(bf16[16,176,256]{2,1,0:T(8,128)(2,1)S(1)} %all_to_all.22.amp_ref, bf16[2048,4096]{1,0:T(8,128)(2,1)} %int_ref.1, bf16[16,4096]{1,0:T(8,128)(2,1)S(1)} %get-tuple-element.390.k_ref, bf16[4096,128]{1,0:T(8,128)(2,1)S(1)} %get-tuple-element.391.k_col_ref, ...), custom_call_target="tpu_custom_call" | custom-call | tf_op jit(solution)/shard_map/product/pallas_call | solution.py:442
  51.3 0.0 copy-start
  51.3 0.0 copy-start.1
  51.3 0.0 copy-start.2
  51.3 0.0 copy-start.3
  51.3 0.0 copy-start.4
  51.4 0.0 copy-start.5
  51.4 0.0 copy-start.6
  51.4 2.4 %collective-permute-start.9 = (f32[4,32,2048]{2,1,0:T(8,128)S(1)}, f32[4,32,2048]{2,1,0:T(8,128)S(1)}, u32[]{:S(2)}, u32[]{:S(2)}) collective-permute-start(f32[4,32,2048]{2,1,0:T(8,128)S(1)} %get-tuple-element.395), channel_id=1, source_target_pairs={{0,1},{1,0},{2,3},{3,2},{4,5},{5,4},{6,7},{7,6},{8,9},{9,8},{10,11... | collective-permute-start | bytes 3145736 | tf_op jit(solution)/shard_map/ppermute | solution.py:501
  53.7 2.3 %collective-permute-done.9.got_ref = f32[4,32,2048]{2,1,0:T(8,128)S(1)} collective-permute-done((f32[4,32,2048]{2,1,0:T(8,128)S(1)}, f32[4,32,2048]{2,1,0:T(8,128)S(1)}, u32[]{:S(2)}, u32[]{:S(2)}) %collective-permute-start.9) | collective-permute-done | bytes 1048608 | tf_op jit(solution)/shard_map/ppermute | solution.py:501
  56.0 0.3 share.1
  56.4 1.0 %collective-permute-start.10 = (s16[32,2048]{1,0:T(8,128)(2,1)S(1)}, s16[32,2048]{1,0:T(8,128)(2,1)S(1)}, u32[]{:S(2)}, u32[]{:S(2)}) collective-permute-start(s16[32,2048]{1,0:T(8,128)(2,1)S(1)} %get-tuple-element.397), channel_id=1, source_target_pairs={{0,2},{1,3},{2,4},{3,5},{4,6},{5,7},{6,0},{7,1},{8,10},{9,11},{10,... | collective-permute-start | bytes 393224 | tf_op jit(solution)/shard_map/ppermute | solution.py:508
  57.4 2.1 %collective-permute-start.11 = (s16[32,2048]{1,0:T(8,128)(2,1)S(1)}, s16[32,2048]{1,0:T(8,128)(2,1)S(1)}, u32[]{:S(2)}, u32[]{:S(2)}) collective-permute-start(s16[32,2048]{1,0:T(8,128)(2,1)S(1)} %get-tuple-element.398), channel_id=1, source_target_pairs={{0,4},{1,5},{2,6},{3,7},{4,0},{5,1},{6,2},{7,3},{8,12},{9,13},{10,... | collective-permute-start | bytes 393224 | tf_op jit(solution)/shard_map/ppermute | solution.py:508
  59.5 1.0 %collective-permute-start.12 = (s16[32,2048]{1,0:T(8,128)(2,1)S(1)}, s16[32,2048]{1,0:T(8,128)(2,1)S(1)}, u32[]{:S(2)}, u32[]{:S(2)}) collective-permute-start(s16[32,2048]{1,0:T(8,128)(2,1)S(1)} %get-tuple-element.399), channel_id=1, source_target_pairs={{0,6},{1,7},{2,0},{3,1},{4,2},{5,3},{6,4},{7,5},{8,14},{9,15},{10,... | collective-permute-start | bytes 393224 | tf_op jit(solution)/shard_map/ppermute | solution.py:508
  61.1 1.2 %collective-permute-done.10.a_ref = s16[32,2048]{1,0:T(8,128)(2,1)S(1)} collective-permute-done((s16[32,2048]{1,0:T(8,128)(2,1)S(1)}, s16[32,2048]{1,0:T(8,128)(2,1)S(1)}, u32[]{:S(2)}, u32[]{:S(2)}) %collective-permute-start.10) | collective-permute-done | bytes 131104 | tf_op jit(solution)/shard_map/ppermute | solution.py:508
  62.4 3.2 %collective-permute-done.11.b_ref = s16[32,2048]{1,0:T(8,128)(2,1)S(1)} collective-permute-done((s16[32,2048]{1,0:T(8,128)(2,1)S(1)}, s16[32,2048]{1,0:T(8,128)(2,1)S(1)}, u32[]{:S(2)}, u32[]{:S(2)}) %collective-permute-start.11) | collective-permute-done | bytes 131104 | tf_op jit(solution)/shard_map/ppermute | solution.py:508
  65.6 1.2 %expand.1 = bf16[2048,128]{1,0:T(8,128)(2,1)} custom-call(f32[32,2048]{1,0:T(8,128)S(1)} %get-tuple-element.396.own_ref, s16[32,2048]{1,0:T(8,128)(2,1)S(1)} %collective-permute-done.10.a_ref, s16[32,2048]{1,0:T(8,128)(2,1)S(1)} %collective-permute-done.11.b_ref, s16[32,2048]{1,0:T(8,128)(2,1)S(1)} %collective-permute-done.12.c_ref, ...), custom_call_target="tpu_custom_call" | custom-call | tf_op jit(solution)/shard_map/expand/pallas_call | solution.py:442
  66.8 0.2 conditional.1
  (12 shorter events, 0.0 us)
Async XLA Ops:
  0.0 10.0 %collective-permute-start.4 = (s32[2,4096]{1,0:T(2,128)}, s32[2,4096]{1,0:T(2,128)S(1)}, u32[]{:S(2)}, u32[]{:S(2)}) collective-permute-start(s32[2,4096]{1,0:T(2,128)} %k_orbs.1), channel_id=1, source_target_pairs={{0,1},{1,0},{2,3},{3,2},{4,5},{5,4},{6,7},{7,6},{8,9},{9,8},{10,11... | collective-permute-start | bytes 98312 | tf_op jit(solution)/shard_map/ppermute | solution.py:455
  2.8 10.7 %collective-permute-start.5 = (bf16[64,1024]{1,0:T(8,128)(2,1)S(1)}, bf16[64,1024]{1,0:T(8,128)(2,1)S(1)}, u32[]{:S(2)}, u32[]{:S(2)}) collective-permute-start(bf16[64,1024]{1,0:T(8,128)(2,1)S(1)} %get-tuple-element.381), channel_id=1, source_target_pairs={{0,2},{1,3},{2,4},{3,5},{4,6},{5,7},{6,0},{7,1},{8,10},{9,11},{10,... | collective-permute-start | bytes 393224 | tf_op jit(solution)/shard_map/ppermute | solution.py:453
  4.6 9.8 %collective-permute-start.6 = (bf16[64,1024]{1,0:T(8,128)(2,1)S(1)}, bf16[64,1024]{1,0:T(8,128)(2,1)S(1)}, u32[]{:S(2)}, u32[]{:S(2)}) collective-permute-start(bf16[64,1024]{1,0:T(8,128)(2,1)S(1)} %get-tuple-element.382), channel_id=1, source_target_pairs={{0,4},{1,5},{2,6},{3,7},{4,0},{5,1},{6,2},{7,3},{8,12},{9,13},{10,... | collective-permute-start | bytes 393224 | tf_op jit(solution)/shard_map/ppermute | solution.py:453
  7.9 6.5 %collective-permute-start.7 = (bf16[64,1024]{1,0:T(8,128)(2,1)S(1)}, bf16[64,1024]{1,0:T(8,128)(2,1)S(1)}, u32[]{:S(2)}, u32[]{:S(2)}) collective-permute-start(bf16[64,1024]{1,0:T(8,128)(2,1)S(1)} %get-tuple-element.383), channel_id=1, source_target_pairs={{0,6},{1,7},{2,0},{3,1},{4,2},{5,3},{6,4},{7,5},{8,14},{9,15},{10,... | collective-permute-start | bytes 393224 | tf_op jit(solution)/shard_map/ppermute | solution.py:453
  14.9 1.7 %collective-permute-start.8 = (bf16[176,128]{1,0:T(8,128)(2,1)S(1)}, bf16[176,128]{1,0:T(8,128)(2,1)S(1)}, u32[]{:S(2)}, u32[]{:S(2)}) collective-permute-start(bf16[176,128]{1,0:T(8,128)(2,1)S(1)} %get-tuple-element.389), channel_id=1, source_target_pairs={{0,1},{1,0},{2,3},{3,2},{4,5},{5,4},{6,7},{7,6},{8,9},{9,8},{10,11... | collective-permute-start | bytes 135176 | tf_op jit(solution)/shard_map/ppermute | solution.py:484
  51.3 15.4 %copy-start = (bf16[256,1024]{1,0:T(8,128)(2,1)S(1)}, bf16[256,1024]{1,0:T(8,128)(2,1)}, u32[]{:S(2)}) copy-start(bf16[256,1024]{1,0:T(8,128)(2,1)} %amp_ref.1) | copy-start | bytes 1572868
  51.3 15.4 %copy-start.1 = (s32[2,4096]{1,0:T(2,128)S(1)}, s32[2,4096]{1,0:T(2,128)}, u32[]{:S(2)}) copy-start(s32[2,4096]{1,0:T(2,128)} %k_orbs.1) | copy-start | bytes 98308
  51.3 15.4 %copy-start.2 = (s32[2,2048]{1,0:T(2,128)S(1)}, s32[2,2048]{1,0:T(2,128)}, u32[]{:S(2)}) copy-start(s32[2,2048]{1,0:T(2,128)} %m_orbs.1) | copy-start | bytes 49156
  51.3 15.4 %copy-start.3 = (s32[2,1024]{1,0:T(2,128)S(1)}, s32[2,1024]{1,0:T(2,128)}, u32[]{:S(2)}) copy-start(s32[2,1024]{1,0:T(2,128)} %occ_orbs.1) | copy-start | bytes 24580
  51.3 15.4 %copy-start.4 = (s32[800]{0:T(1024)S(1)}, s32[800]{0:T(1024)}, u32[]{:S(2)}) copy-start(s32[800]{0:T(1024)} %param.16) | copy-start | bytes 9604
  51.4 15.4 %copy-start.5 = (s32[256]{0:T(256)S(1)}, s32[256]{0:T(256)}, u32[]{:S(2)}) copy-start(s32[256]{0:T(256)} %param.13) | copy-start | bytes 3076
  51.4 15.4 %copy-start.6 = (s32[100]{0:T(128)S(1)}, s32[100]{0:T(128)}, u32[]{:S(2)}) copy-start(s32[100]{0:T(128)} %param.15) | copy-start | bytes 1204
  51.4 4.7 %collective-permute-start.9 = (f32[4,32,2048]{2,1,0:T(8,128)S(1)}, f32[4,32,2048]{2,1,0:T(8,128)S(1)}, u32[]{:S(2)}, u32[]{:S(2)}) collective-permute-start(f32[4,32,2048]{2,1,0:T(8,128)S(1)} %get-tuple-element.395), channel_id=1, source_target_pairs={{0,1},{1,0},{2,3},{3,2},{4,5},{5,4},{6,7},{7,6},{8,9},{9,8},{10,11... | collective-permute-start | bytes 3145736 | tf_op jit(solution)/shard_map/ppermute | solution.py:501
  56.4 6.0 %collective-permute-start.10 = (s16[32,2048]{1,0:T(8,128)(2,1)S(1)}, s16[32,2048]{1,0:T(8,128)(2,1)S(1)}, u32[]{:S(2)}, u32[]{:S(2)}) collective-permute-start(s16[32,2048]{1,0:T(8,128)(2,1)S(1)} %get-tuple-element.397), channel_id=1, source_target_pairs={{0,2},{1,3},{2,4},{3,5},{4,6},{5,7},{6,0},{7,1},{8,10},{9,11},{10,... | collective-permute-start | bytes 393224 | tf_op jit(solution)/shard_map/ppermute | solution.py:508
  57.4 8.2 %collective-permute-start.11 = (s16[32,2048]{1,0:T(8,128)(2,1)S(1)}, s16[32,2048]{1,0:T(8,128)(2,1)S(1)}, u32[]{:S(2)}, u32[]{:S(2)}) collective-permute-start(s16[32,2048]{1,0:T(8,128)(2,1)S(1)} %get-tuple-element.398), channel_id=1, source_target_pairs={{0,4},{1,5},{2,6},{3,7},{4,0},{5,1},{6,2},{7,3},{8,12},{9,13},{10,... | collective-permute-start | bytes 393224 | tf_op jit(solution)/shard_map/ppermute | solution.py:508
  59.5 6.1 %collective-permute-start.12 = (s16[32,2048]{1,0:T(8,128)(2,1)S(1)}, s16[32,2048]{1,0:T(8,128)(2,1)S(1)}, u32[]{:S(2)}, u32[]{:S(2)}) collective-permute-start(s16[32,2048]{1,0:T(8,128)(2,1)S(1)} %get-tuple-element.399), channel_id=1, source_target_pairs={{0,6},{1,7},{2,0},{3,1},{4,2},{5,3},{6,4},{7,5},{8,14},{9,15},{10,... | collective-permute-start | bytes 393224 | tf_op jit(solution)/shard_map/ppermute | solution.py:508

commit v5 on v4

--- a/solution.py
+++ b/solution.py
@@ -16,8 +16,6 @@
 SPILL = 48
 PLACES = 8 * BASE + SPILL
 TM = 256
-ROOM = 64
-TILE = 1024
 
 
 def pack_labels(labels):
@@ -34,13 +32,15 @@
 
 
 def pair_symbols(packed, orbs_ref, start):
-    lanes = slice(start, start + LANES)
+    lanes = pl.ds(start, LANES)
     return look_up(packed, orbs_ref[0:1, lanes]) ^ look_up(packed, orbs_ref[1:2, lanes])
 
 
 def as_column(symbols):
     row = jnp.broadcast_to(symbols[0:1, :].astype(F32), (LANES, LANES))
-    return jnp.transpose(row)
+    same = lax.broadcasted_iota(I32, (LANES, LANES), 0) == lax.broadcasted_iota(I32, (LANES, LANES), 1)
+    diagonal = jnp.where(same, row, 0.0).astype(BF16)
+    return jnp.dot(diagonal, jnp.ones((LANES, LANES), BF16), preferred_element_type=F32)
 
 
 def one_hot(mask):
@@ -68,17 +68,19 @@
 
 
 def symbols_kernel(
-    occ_ref, virt_ref, occ_orbs, k_orbs, m_orbs, other_orbs,
-    occ_out, rank_out, place_out, spread_out, k_out, k_col_out, m_out, own_out, other_out, bad_out, other_col,
+    labels_ref, occ_orbs, k_orbs, m_orbs, other_orbs, int_ref,
+    occ_out, rank_out, place_out, from_out, k_out, m_out, own_out, other_out, early, bad_out, own_col, other_col, sem,
 ):
     core = lax.axis_index("col") & 1
-    occ = pack_labels(occ_ref[0:1, :])
-    virt = pack_labels(virt_ref[0:7, :])
+    occ = pack_labels(labels_ref[7:8, :])
+    virt = pack_labels(labels_ref[0:7, :])
     first = iota((LANES, LANES), 0)
     second = iota((LANES, LANES), 1)
     group = iota((8, LANES), 0)
     used = jnp.zeros((8, 1), I32)
     bad = jnp.zeros((1, LANES), I32)
+    lane = iota((8, LANES), 1)
+    table = jnp.full((8, LANES), LANES - 1, I32)
     for c in range(occ_orbs.shape[1] // LANES):
         lanes = slice(c * LANES, (c + 1) * LANES)
         sym = pair_symbols(occ, occ_orbs, c * LANES)
@@ -88,32 +90,55 @@
         rank_out[:, lanes] = jnp.broadcast_to(rank, (8, LANES))
         mine = sym == group
         extra = jnp.sum(jnp.where(mine, used, 0), axis=0, keepdims=True) + rank - BASE
-        used = used + jnp.maximum(jnp.sum(jnp.where(mine, 1, 0), axis=1, keepdims=True) - BASE, 0)
+        over = jnp.maximum(jnp.sum(jnp.where(mine, 1, 0), axis=1, keepdims=True) - BASE, 0)
+        at = lane - c * BASE
+        table = jnp.where((at >= 0) & (at < jnp.minimum(over, BASE)) & (used + at < SPILL), used + at, table)
+        used = used + over
         spilt = rank >= BASE
         bad = jnp.maximum(bad, jnp.where(spilt & ((extra >= SPILL) | (rank >= CAP - 1)), 1, 0))
-        fits = spilt & (extra < SPILL)
-        place = jnp.where(spilt, jnp.where(fits, 8 * BASE + extra, -1), c * BASE + rank)
+        place = jnp.where(spilt, jnp.where(extra < SPILL, 8 * BASE + extra, -1), c * BASE + rank)
         place_out[:, lanes] = jnp.broadcast_to(place, (8, LANES))
-        at = jnp.where(spilt, rank - BASE, -1)
-        entry = jnp.where(fits, sym[0:1, :] * ROOM + extra, -1)
-        to = one_hot(iota((BASE, LANES), 0) == jnp.broadcast_to(at, (BASE, LANES)))
-        source = one_hot(iota((8 * ROOM, LANES), 0) == jnp.broadcast_to(entry, (8 * ROOM, LANES)))
-        spread_out[c * BASE : (c + 1) * BASE, :] = rows_dot(to, source).astype(BF16)
     bad_out[0, 0] = jnp.max(bad)
-    for start in range(0, k_orbs.shape[1], LANES):
+    table = jnp.concatenate([table.astype(F32), jnp.zeros((LANES - 8, LANES), F32)], axis=0).astype(BF16)
+
+    step = early.shape[0] * LANES // k_orbs.shape[1]
+
+    def contracted(n, carry):
+        some = pl.ds(pl.multiple_of(n * step, step), step)
+        pltpu.make_async_copy(int_ref.at[some], early.at[some], sem).start()
+        start = pl.multiple_of(n * LANES, LANES)
+        rows = pl.ds(start, LANES)
         sym = pair_symbols(virt, k_orbs, start)
         wide = sym.astype(F32)
-        k_out[:, start : start + LANES] = jnp.concatenate([wide, wide], axis=0).astype(BF16)
-        k_col_out[start : start + LANES, :] = as_column(sym).astype(BF16)
-        other_col[start : start + LANES, :] = as_column(pair_symbols(virt, other_orbs, start)).astype(BF16)
-    for start in range(0, m_orbs.shape[1], LANES):
-        m_out[start : start + LANES, :] = as_column(pair_symbols(virt, m_orbs, start)).astype(BF16)
+        k_out[:, rows] = jnp.concatenate([wide, wide], axis=0).astype(BF16)
+        column = as_column(sym)
+        own_col[rows, :] = column.astype(BF16)
+        group = one_hot(column == second.astype(F32))
+        from_out[rows, :] = jnp.dot(group, table, preferred_element_type=F32).astype(I32)
+        return carry
+
+    lax.fori_loop(0, k_orbs.shape[1] // LANES, contracted, 0, unroll=8)
+
+    def output(n, carry):
+        start = pl.multiple_of(n * LANES, LANES)
+        m_out[pl.ds(start, LANES), :] = as_column(pair_symbols(virt, m_orbs, start)).astype(BF16)
+        return carry
+
+    lax.fori_loop(0, m_orbs.shape[1] // LANES, output, 0, unroll=8)
+
     i, j = iota((LANES, 2 * LANES), 0), iota((LANES, 2 * LANES), 1)
     pick = one_hot(j == (i >> 1) * 4 + core * 2 + (i & 1))
-    mine = pl.multiple_of(lax.axis_index("row") * 16, 16)
-    for ref, out in ((k_col_out, own_out), (other_col, other_out)):
-        column = jnp.concatenate([ref[pl.ds(r * 256 + mine, 16), :] for r in range(16)], axis=0)
+    mine = lax.axis_index("row") * 16
+    tile = pl.multiple_of(mine & LANES, LANES)
+    for r in range(16):
+        other_col[r * LANES : (r + 1) * LANES, :] = as_column(
+            pair_symbols(virt, other_orbs, r * 256 + tile)
+        ).astype(BF16)
+    inside = pl.multiple_of(mine & (LANES - 1), 16)
+    for ref, out, far, at in ((own_col, own_out, 256, pl.multiple_of(mine, 16)), (other_col, other_out, LANES, inside)):
+        column = jnp.concatenate([ref[pl.ds(r * far + at, 16), :] for r in range(16)], axis=0)
         out[...] = jnp.dot(pick, column, preferred_element_type=F32)
+    pltpu.make_async_copy(int_ref.at[pl.ds(0, early.shape[0])], early, sem).wait()
 
 
 def compact_kernel(a_ref, b_ref, c_ref, d_ref, own_ref, other_ref, occ_ref, place_ref, mine_out, theirs_out):
@@ -132,74 +157,58 @@
         out[...] = rows_dot(squeeze, kept).astype(BF16)
 
 
-def product_kernel(amp_ref, int_ref, k_ref, k_col_ref, m_ref, spread_ref, keep_ref, send_ref, kept, local, sems):
+def multiply(rows_ref, kept_ref, k_ref, m_sym, keep_ref, send_ref):
+    even = (lax.axis_index("col") & 1) == 0
+    depth, chunk = k_ref.shape[1], 1024
+    total = jnp.zeros((m_sym.shape[0], 256), F32)
+    for at in range(0, depth, chunk):
+        parts = []
+        for start in range(at, at + chunk, LANES):
+            lanes = slice(start, start + LANES)
+            same = m_sym == jnp.broadcast_to(k_ref[0:1, lanes], m_sym.shape)
+            parts.append(jnp.where(same, rows_ref[:, lanes], jnp.zeros((), BF16)))
+        screened = jnp.concatenate(parts, axis=1)
+        total += jnp.dot(screened, kept_ref[at : at + chunk, :], preferred_element_type=F32)
+    turned = jnp.transpose(total)
+    for z in range(4):
+        for half in range(2):
+            at = half * 128 + z * 2 * BASE
+            low, high = turned[at : at + BASE, :], turned[at + BASE : at + 2 * BASE, :]
+            slots = slice(half * BASE, half * BASE + BASE)
+            keep_ref[z, slots, :] = jnp.where(even, low, high)
+            send_ref[z, slots, :] = jnp.where(even, high, low)
+
+
+def first_kernel(amp_ref, early, int_ref, k_ref, from_ref, m_ref, keep_ref, send_ref, kept, later, sem):
     core = lax.axis_index("col") & 1
-    depth = k_ref.shape[1]
-    tiles = int_ref.shape[0] // TILE
-
-    def fetch(n):
-        rows = pl.ds(pl.multiple_of(n * TILE, TILE), TILE)
-        return pltpu.make_async_copy(int_ref.at[rows], local.at[rows], sems.at[n])
-
-    def begin(n, carry):
-        fetch(n).start()
-        return carry
-
-    lax.fori_loop(0, tiles, begin, 0)
+    half = early.shape[0]
+    fetch = pltpu.make_async_copy(int_ref.at[pl.ds(half, half)], later, sem)
+    fetch.start()
 
     i, j = iota((256, 256), 0), iota((256, 256), 1)
     order = one_hot(j == (((i >> 1) & 1) ^ core) * 128 + (i >> 4) * 8 + ((i >> 2) & 3) * 2 + (i & 1))
-    spread = spread_ref[...]
-    nought = jnp.zeros((), BF16)
-    gap = jnp.zeros((ROOM - SPILL, 256), BF16)
-    second = iota((16, LANES), 1) >= ROOM
-    groups = [
-        jnp.broadcast_to(jnp.where(second, 2.0 * t + 1.0, 2.0 * t).astype(BF16)[0:1, :], (256, LANES))
-        for t in range(4)
-    ]
+    gap = jnp.zeros((256 - PLACES, 256), BF16)
 
     def unpack(source, carry):
-        slots = amp_ref[source]
-        stack = jnp.concatenate([slots, gap, slots[8 * BASE :], gap], axis=0)
-        block = rows_dot(order, stack).astype(BF16)
+        block = rows_dot(order, jnp.concatenate([amp_ref[source], gap], axis=0))
         at = [pl.ds(pl.multiple_of(r * 256 + source * 16, 16), 16) for r in range(16)]
-        sym = jnp.concatenate([k_col_ref[rows, :] for rows in at], axis=0)
-        shared = [jnp.where(sym == group, block[:, 8 * BASE :], nought) for group in groups]
-        spilt = rows_dot(jnp.concatenate(shared, axis=1), spread).astype(BF16)
+        main = block[:, : 8 * BASE].astype(BF16)
         for r, rows in enumerate(at):
-            kept[rows, : 8 * BASE] = block[r * 16 : r * 16 + 16, : 8 * BASE]
-            kept[rows, 8 * BASE :] = spilt[r * 16 : r * 16 + 16, :]
+            shared = block[r * 16 : r * 16 + 16, 8 * BASE :]
+            index = from_ref[rows, :]
+            spilt = [jnp.take_along_axis(shared[h : h + 8], index[h : h + 8], axis=1) for h in (0, 8)]
+            kept[rows, : 8 * BASE] = main[r * 16 : r * 16 + 16, :]
+            kept[rows, 8 * BASE :] = jnp.concatenate(spilt, axis=0).astype(BF16)
         return carry
 
     lax.fori_loop(0, 16, unpack, 0, unroll=8)
-
-    even = core == 0
-    chunk = 1024
-
-    def multiply(n, carry):
-        rows = pl.ds(pl.multiple_of(n * TILE, TILE), TILE)
-        fetch(n).wait()
-        m_sym = m_ref[rows, :]
-        total = jnp.zeros((TILE, 256), F32)
-        for at in range(0, depth, chunk):
-            parts = []
-            for start in range(at, at + chunk, LANES):
-                lanes = slice(start, start + LANES)
-                same = m_sym == jnp.broadcast_to(k_ref[0:1, lanes], m_sym.shape)
-                parts.append(jnp.where(same, local[rows, lanes], nought))
-            screened = jnp.concatenate(parts, axis=1)
-            total += jnp.dot(screened, kept[at : at + chunk, :], preferred_element_type=F32)
-        turned = jnp.transpose(total)
-        for z in range(4):
-            for half in range(2):
-                at = half * 128 + z * 2 * BASE
-                low, high = turned[at : at + BASE, :], turned[at + BASE : at + 2 * BASE, :]
-                slots = slice(half * BASE, half * BASE + BASE)
-                keep_ref[z, slots, rows] = jnp.where(even, low, high)
-                send_ref[z, slots, rows] = jnp.where(even, high, low)
-        return carry
-
-    lax.fori_loop(0, tiles, multiply, 0)
+    multiply(early, kept, k_ref, m_ref[:half, :], keep_ref, send_ref)
+    fetch.wait()
+
+
+def second_kernel(int_ref, kept_ref, k_ref, m_ref, keep_ref, send_ref):
+    half = int_ref.shape[0]
+    multiply(int_ref, kept_ref, k_ref, m_ref[half:, :], keep_ref, send_ref)
 
 
 def share_kernel(keep_ref, got_ref, own_ref, *out_refs):
@@ -215,17 +224,21 @@
         out_ref[...] = (scaled + jnp.where(scaled >= 0, 0.5, -0.5)).astype(I32).astype(jnp.int16)
 
 
-def expand_kernel(own_ref, a_ref, b_ref, c_ref, m_ref, occ_ref, rank_ref, out_ref):
+def expand_kernel(*refs):
+    m_ref, occ_ref, rank_ref, out_ref = refs[-4:]
     lanes = pl.ds(pl.multiple_of(lax.axis_index("col") * LANES, LANES), LANES)
-    total = own_ref[...]
-    for ref in (a_ref, b_ref, c_ref):
-        part = ref[...].astype(I32).astype(F32)
-        total += part * jnp.exp2(-part[CAP - 1 : CAP, :])
     slot = iota((CAP, LANES), 0)
     pick = one_hot(slot == jnp.broadcast_to(rank_ref[0:1, lanes], (CAP, LANES)))
-    wide = lax.dot_general(total.astype(BF16), pick, (((0,), (0,)), ((), ())), preferred_element_type=F32)
-    same = m_ref[...].astype(F32) == jnp.broadcast_to(occ_ref[0:1, lanes].astype(F32), wide.shape)
-    out_ref[...] = jnp.where(same, wide, 0.0).astype(BF16)
+    half = refs[0].shape[1]
+    for part in range(2):
+        total = refs[part * 4][...]
+        for ref in refs[part * 4 + 1 : part * 4 + 4]:
+            got = ref[...].astype(I32).astype(F32)
+            total += got * jnp.exp2(-got[CAP - 1 : CAP, :])
+        rows = slice(part * half, part * half + half)
+        wide = lax.dot_general(total.astype(BF16), pick, (((0,), (0,)), ((), ())), preferred_element_type=F32)
+        same = m_ref[rows, :].astype(F32) == jnp.broadcast_to(occ_ref[0:1, lanes].astype(F32), wide.shape)
+        out_ref[rows, :] = jnp.where(same, wide, 0.0).astype(BF16)
 
 
 def plain_symbols_kernel(
@@ -453,26 +466,33 @@
     arrived = [ordered[0]] + [lax.ppermute(ordered[d], "col", hops[d]) for d in range(1, 4)]
 
     other_orbs = lax.ppermute(k_orbs, "col", swap)
-    occ_lab = jnp.pad(occ_irrep, (0, LANES - occ_irrep.shape[0])).reshape(1, LANES)
-    virt_lab = jnp.pad(virt_irrep, (0, 8 * LANES - virt_irrep.shape[0])).reshape(8, LANES)
-    occ_sym, rank, place, spread, k_sym, k_col, m_sym, own_sym, other_sym, bad = call(
+    labels = jnp.concatenate(
+        [jnp.pad(virt_irrep, (0, 7 * LANES - virt_irrep.shape[0])), jnp.pad(occ_irrep, (0, LANES - occ_irrep.shape[0]))]
+    ).reshape(8, LANES)
+    half = m_dev // 2
+    occ_sym, rank, place, origin, k_sym, m_sym, own_sym, other_sym, early, bad = call(
         symbols_kernel,
         "symbols",
         (
             shape((8, pairs), I32),
             shape((8, pairs), I32),
             shape((8, pairs), I32),
-            shape((8 * BASE, 8 * ROOM), BF16),
+            shape((kblock, LANES), I32),
             shape((16, kblock), BF16),
-            shape((kblock, LANES), BF16),
             shape((m_dev, LANES), BF16),
             shape((LANES, LANES), F32),
             shape((LANES, LANES), F32),
+            shape((half, kblock), BF16),
             shape((1, 1), I32),
         ),
-        (occ_lab, virt_lab, occ_orbs, k_orbs, m_orbs, other_orbs),
+        (labels, occ_orbs, k_orbs, m_orbs, other_orbs, integrals),
+        in_specs=[whole()] * 5 + [pl.BlockSpec(memory_space=pl.ANY)],
         out_specs=(whole(),) * 9 + (scalars(),),
-        scratch_shapes=[pltpu.VMEM((kblock, LANES), BF16)],
+        scratch_shapes=[
+            pltpu.VMEM((kblock, LANES), BF16),
+            pltpu.VMEM((kblock // 2, LANES), BF16),
+            pltpu.SemaphoreType.DMA,
+        ],
     )
 
     mine, theirs = call(
@@ -485,27 +505,34 @@
     spreading = jnp.broadcast_to(jnp.concatenate([mine, got], axis=1)[None], (rows, PLACES, stored))
     gathered = lax.all_to_all(spreading, "row", split_axis=0, concat_axis=0, tiled=True)
 
-    keep, send = call(
-        product_kernel,
-        "product",
-        (shape((4, CAP, m_dev), F32),) * 2,
-        (gathered, integrals, k_sym, k_col, m_sym, spread),
-        30,
-        in_specs=[whole(), pl.BlockSpec(memory_space=pl.ANY)] + [whole()] * 4,
-        scratch_shapes=[
-            pltpu.VMEM((kblock, 256), BF16),
-            pltpu.VMEM((m_dev, kblock), BF16),
-            pltpu.SemaphoreType.DMA((m_dev // TILE,)),
-        ],
+    pieces = (shape((4, CAP, half), F32),) * 2
+    *first, kept, later = call(
+        first_kernel,
+        "first",
+        pieces + (shape((kblock, 256), BF16), shape((half, kblock), BF16)),
+        (gathered, early, integrals, k_sym, origin, m_sym),
+        20,
+        in_specs=[whole()] * 2 + [pl.BlockSpec(memory_space=pl.ANY)] + [whole()] * 3,
+        scratch_shapes=[pltpu.SemaphoreType.DMA],
     )
-    partner = lax.ppermute(send, "col", swap)
-    shares = call(
-        share_kernel,
-        "share",
-        (shape((CAP, m_dev), F32),) + (shape((CAP, m_dev), jnp.int16),) * 3,
-        (keep, partner),
+    second = call(
+        second_kernel,
+        "second",
+        pieces,
+        (later, kept, k_sym, m_sym),
+        12,
+        cost_estimate=pl.CostEstimate(flops=half * kblock * 512, bytes_accessed=half * kblock * 2, transcendentals=0),
     )
-    sums = [shares[0]] + [lax.ppermute(shares[d], "col", hops[d]) for d in range(1, 4)]
+    sums = []
+    for keep, send in (first, second):
+        partner = lax.ppermute(send, "col", swap)
+        shares = call(
+            share_kernel,
+            "share",
+            (shape((CAP, half), F32),) + (shape((CAP, half), jnp.int16),) * 3,
+            (keep, partner),
+        )
+        sums += [shares[0]] + [lax.ppermute(shares[d], "col", hops[d]) for d in range(1, 4)]
     result = call(expand_kernel, "expand", shape((m_dev, LANES), BF16), (*sums, m_sym, occ_sym, rank))
 
     return lax.cond(

time: 67.4 us -> 66.2 us (0.982); the launches traced: 67.2 us -> 65.2 us
  waiting for transfers between devices: 8.5 us -> 2.57 us
  starting transfers between devices: 14.6 us -> 18.2 us
  local copies, waits for them, and re-layouts: 1.49 us -> 0.14 us
  Pallas kernels: 15.1 us -> 16.2 us
  other arithmetic: 0.01 us -> 0.72 us
    ppermute x3 -> x6, starting transfers between devices: 4.09 us -> 7.25 us  [body(): lax.ppermute(shares[d], 'col', hops[d])]
    ppermute x3 -> x6, waiting for transfers between devices: 4.44 us -> 1.32 us  [body(): lax.ppermute(shares[d], 'col', hops[d])]
    ppermute x1 -> x2, waiting for transfers between devices: 2.29 us -> 0.01 us  [body(): partner = lax.ppermute(send, 'col', swap)]
    reshape x2 -> x0, local copies, waits for them, and re-layouts: 1.35 us -> none  [the longest x1 0.69 us: body(): jnp.pad(virt_irrep, (0, 8 * LANES - virt_irrep.shape[0])).reshape(8, LANES)]
    pallas_call x6 -> x8, Pallas kernels: 15.1 us -> 16.2 us  [call(): pl.pallas_call(kernel, out_shape=out_shape, in_specs=kw.pop('in_specs', [...]
    ppermute x3, waiting for transfers between devices: 0.89 us -> 0.01 us  [body(): lax.ppermute(ordered[d], 'col', hops[d])]
    ppermute x3, starting transfers between devices: 5.82 us -> 6.57 us  [body(): lax.ppermute(ordered[d], 'col', hops[d])]
    reshape x0 -> x1, other arithmetic: none -> 0.71 us  [body(): labels = jnp.concatenate([jnp.pad(virt_irrep, (0, 7 * LANES - virt_irrep....]
  transfers between devices with their start and end apart: 9 -> 13, of which waited for: 5 -> 5; matrix products, arithmetic and copies ran while one was open for 2% -> 1% of each run, Pallas kernels for 7% -> 13%
where the time goes in v5:
time: 66.2 us; the launch traced here: 65.2 us
  blocking collectives  26.3 us (40%)
  starting transfers between devices  18.2 us (27%)
  Pallas kernels  16.2 us (24%)
  waiting for transfers between devices  2.57 us (4%)
  between operations  1.01 us (2%)
  other arithmetic  0.72 us (1%)
    all_to_all x1, blocking collectives, body(): lax.all_to_all(spreading, 'row', split_axis=0, concat_axis=0, tiled=True)  26.3 us
    pallas_call x8, Pallas kernels, call(): pl.pallas_call(kernel, out_shape=out_shape, in_specs=kw.pop('in_specs', [...  16.2 us
    ppermute x6, starting transfers between devices, body(): lax.ppermute(shares[d], 'col', hops[d])  7.25 us
    ppermute x3, starting transfers between devices, body(): lax.ppermute(ordered[d], 'col', hops[d])  6.57 us
    ppermute x2, starting transfers between devices, body(): partner = lax.ppermute(send, 'col', swap)  2.48 us
    ppermute x1, starting transfers between devices, body(): other_orbs = lax.ppermute(k_orbs, 'col', swap)  1.52 us
  transfers between devices with their start and end apart: 13, of which 5 were waited for; matrix products, arithmetic and copies ran while one was open for 1% of the time, Pallas kernels for 13%

profile of v5, /device:TPU:1, one launch (start us, length us, event | category | flops | bytes accessed | tf_op | source)
XLA Modules:
  0.0 65.2 jit_solution(17283424528557135273)
XLA Ops:
  0.0 1.4 %order.1 = (bf16[64,1024]{1,0:T(8,128)(2,1)S(1)}, bf16[64,1024]{1,0:T(8,128)(2,1)S(1)}, bf16[64,1024]{1,0:T(8,128)(2,1)S(1)}, bf16[64,1024]{1,0:T(8,128)(2,1)S(1)}) custom-call(s32[1,256]{1,0:T(1,128)} %bitcast.35, bf16[256,1024]{1,0:T(8,128)(2,1)} %amp_ref.1), custom_call_target="tpu_custom_call" | custom-call | tf_op jit(solution)/shard_map/order/pallas_call | solution.py:455
  1.4 2.5 %collective-permute-start.5 = (bf16[64,1024]{1,0:T(8,128)(2,1)S(1)}, bf16[64,1024]{1,0:T(8,128)(2,1)S(1)}, u32[]{:S(2)}, u32[]{:S(2)}) collective-permute-start(bf16[64,1024]{1,0:T(8,128)(2,1)S(1)} %get-tuple-element.389), channel_id=1, source_target_pairs={{0,2},{1,3},{2,4},{3,5},{4,6},{5,7},{6,0},{7,1},{8,10},{9,11},{10,... | collective-permute-start | bytes 393224 | tf_op jit(solution)/shard_map/ppermute | solution.py:466
  3.9 3.3 %collective-permute-start.6 = (bf16[64,1024]{1,0:T(8,128)(2,1)S(1)}, bf16[64,1024]{1,0:T(8,128)(2,1)S(1)}, u32[]{:S(2)}, u32[]{:S(2)}) collective-permute-start(bf16[64,1024]{1,0:T(8,128)(2,1)S(1)} %get-tuple-element.390), channel_id=1, source_target_pairs={{0,4},{1,5},{2,6},{3,7},{4,0},{5,1},{6,2},{7,3},{8,12},{9,13},{10,... | collective-permute-start | bytes 393224 | tf_op jit(solution)/shard_map/ppermute | solution.py:466
  7.2 0.7 %collective-permute-start.7 = (bf16[64,1024]{1,0:T(8,128)(2,1)S(1)}, bf16[64,1024]{1,0:T(8,128)(2,1)S(1)}, u32[]{:S(2)}, u32[]{:S(2)}) collective-permute-start(bf16[64,1024]{1,0:T(8,128)(2,1)S(1)} %get-tuple-element.391), channel_id=1, source_target_pairs={{0,6},{1,7},{2,0},{3,1},{4,2},{5,3},{6,4},{7,5},{8,14},{9,15},{10,... | collective-permute-start | bytes 393224 | tf_op jit(solution)/shard_map/ppermute | solution.py:466
  7.9 1.5 %collective-permute-start.4 = (s32[2,4096]{1,0:T(2,128)}, s32[2,4096]{1,0:T(2,128)S(1)}, u32[]{:S(2)}, u32[]{:S(2)}) collective-permute-start(s32[2,4096]{1,0:T(2,128)} %k_orbs.1), channel_id=1, source_target_pairs={{0,1},{1,0},{2,3},{3,2},{4,5},{5,4},{6,7},{7,6},{8,9},{9,8},{10,11... | collective-permute-start | bytes 98312 | tf_op jit(solution)/shard_map/ppermute | solution.py:468
  9.4 0.7 %fusion.2.labels_ref = s32[8,128]{1,0:T(8,128)S(1)} fusion(s32[100]{0:T(128)} %param.15, s32[800]{0:T(1024)} %param.16), kind=kLoop, calls=%fused_computation.22 | loop fusion | flops 1024 | bytes 7696 | tf_op jit(solution)/shard_map/reshape | solution.py:471
  10.2 0.4 collective-permute-done.4.other_orbs
  10.5 5.8 %symbols.1 = (s32[8,1024]{1,0:T(8,128)S(1)}, s32[8,1024]{1,0:T(8,128)S(1)}, s32[8,1024]{1,0:T(8,128)S(1)}, s32[4096,128]{1,0:T(8,128)S(1)}, bf16[16,4096]{1,0:T(...) custom-call(s32[8,128]{1,0:T(8,128)S(1)} %fusion.2.labels_ref, ...), custom_call_target="tpu_custom_call" | custom-call | tf_op jit(solution)/shard_map/symbols/pallas_call | solution.py:455
  16.3 0.6 compact.1
  16.9 0.4 collective-permute-start.8
  17.4 0.9 %collective-permute-done.8 = bf16[176,128]{1,0:T(8,128)(2,1)S(1)} collective-permute-done((bf16[176,128]{1,0:T(8,128)(2,1)S(1)}, bf16[176,128]{1,0:T(8,128)(2,1)S(1)}, u32[]{:S(2)}, u32[]{:S(2)}) %collective-permute-start.8) | collective-permute-done | bytes 45088 | tf_op jit(solution)/shard_map/ppermute | solution.py:504
  18.3 0.1 broadcast_in_dim.2
  18.4 26.3 %all_to_all.22.amp_ref = bf16[16,176,256]{2,1,0:T(8,128)(2,1)S(1)} all-to-all(bf16[16,176,256]{2,1,0:T(8,128)(2,1)S(1)} %broadcast_in_dim.2), channel_id=1, replica_groups=mesh['row'=16,'col'=8] {'row'}, dimensions={0} | all-to-all | bytes 2883584 | tf_op jit(solution)/shard_map/all_to_all | solution.py:506
  44.6 4.5 %first.1 = (f32[4,32,1024]{2,1,0:T(8,128)S(1)}, f32[4,32,1024]{2,1,0:T(8,128)S(1)}, bf16[4096,256]{1,0:T(8,128)(2,1)S(1)}, bf16[1024,4096]{1,0:T(8,128)(2,1)S(1)}) custom-call(bf16[16,176,256]{2,1,0:T(8,128)(2,1)S(1)} %all_to_all.22.amp_ref, bf16[1024,4096]{1,0:T(8,128)(2,1)S(1)} %get-tuple-element.398.early, bf16[2048,4096]{1,0:T(8,128)(2,1)} %int_ref.3, ...), custom_call_target="tpu_custom_call" | custom-call | tf_op jit(solution)/shard_map/first/pallas_call | solution.py:455
  49.2 2.4 %collective-permute-start.9 = (f32[4,32,1024]{2,1,0:T(8,128)S(1)}, f32[4,32,1024]{2,1,0:T(8,128)S(1)}, u32[]{:S(2)}, u32[]{:S(2)}) collective-permute-start(f32[4,32,1024]{2,1,0:T(8,128)S(1)} %get-tuple-element.403), channel_id=1, source_target_pairs={{0,1},{1,0},{2,3},{3,2},{4,5},{5,4},{6,7},{7,6},{8,9},{9,8},{10,11... | collective-permute-start | bytes 1572872 | tf_op jit(solution)/shard_map/ppermute | solution.py:528
  51.6 2.4 %second.1 = (f32[4,32,1024]{2,1,0:T(8,128)S(1)}, f32[4,32,1024]{2,1,0:T(8,128)S(1)}) custom-call(bf16[1024,4096]{1,0:T(8,128)(2,1)S(1)} %get-tuple-element.408.int_ref, bf16[4096,256]{1,0:T(8,128)(2,1)S(1)} %get-tuple-element.409.kept_ref, bf16[16,4096]{1,0:T(8,128)(2,1)S(1)} %get-tuple-element.399.k_ref, bf16[2048,128]{1,0:T(8,128)(2,1)S(1)} %get-tuple-element.401.m_ref.refs_8_), custom_call_target="tpu_custom_call" | custom-call | flops 2147483648 | bytes 8388608 | tf_op jit(solution)/shard_map/second/pallas_call | solution.py:455
  54.0 0.0 copy-start
  54.0 0.0 copy-start.2
  54.0 0.0 copy-start.3
  54.1 0.1 collective-permute-start.13
  54.2 0.2 share.2
  54.4 0.8 %collective-permute-start.10 = (s16[32,1024]{1,0:T(8,128)(2,1)S(1)}, s16[32,1024]{1,0:T(8,128)(2,1)S(1)}, u32[]{:S(2)}, u32[]{:S(2)}) collective-permute-start(s16[32,1024]{1,0:T(8,128)(2,1)S(1)} %get-tuple-element.405), channel_id=1, source_target_pairs={{0,2},{1,3},{2,4},{3,5},{4,6},{5,7},{6,0},{7,1},{8,10},{9,11},{10,... | collective-permute-start | bytes 196616 | tf_op jit(solution)/shard_map/ppermute | solution.py:535
  55.2 0.2 collective-permute-start.11
  55.3 2.3 %collective-permute-start.12 = (s16[32,1024]{1,0:T(8,128)(2,1)S(1)}, s16[32,1024]{1,0:T(8,128)(2,1)S(1)}, u32[]{:S(2)}, u32[]{:S(2)}) collective-permute-start(s16[32,1024]{1,0:T(8,128)(2,1)S(1)} %get-tuple-element.407), channel_id=1, source_target_pairs={{0,6},{1,7},{2,0},{3,1},{4,2},{5,3},{6,4},{7,5},{8,14},{9,15},{10,... | collective-permute-start | bytes 196616 | tf_op jit(solution)/shard_map/ppermute | solution.py:535
  57.6 0.2 share.3
  57.8 0.1 collective-permute-start.14
  58.0 2.1 %collective-permute-start.15 = (s16[32,1024]{1,0:T(8,128)(2,1)S(1)}, s16[32,1024]{1,0:T(8,128)(2,1)S(1)}, u32[]{:S(2)}, u32[]{:S(2)}) collective-permute-start(s16[32,1024]{1,0:T(8,128)(2,1)S(1)} %get-tuple-element.414), channel_id=1, source_target_pairs={{0,4},{1,5},{2,6},{3,7},{4,0},{5,1},{6,2},{7,3},{8,12},{9,13},{10,... | collective-permute-start | bytes 196616 | tf_op jit(solution)/shard_map/ppermute | solution.py:535
  60.0 1.8 %collective-permute-start.16 = (s16[32,1024]{1,0:T(8,128)(2,1)S(1)}, s16[32,1024]{1,0:T(8,128)(2,1)S(1)}, u32[]{:S(2)}, u32[]{:S(2)}) collective-permute-start(s16[32,1024]{1,0:T(8,128)(2,1)S(1)} %get-tuple-element.415), channel_id=1, source_target_pairs={{0,6},{1,7},{2,0},{3,1},{4,2},{5,3},{6,4},{7,5},{8,14},{9,15},{10,... | collective-permute-start | bytes 196616 | tf_op jit(solution)/shard_map/ppermute | solution.py:535
  62.5 0.3 collective-permute-done.14.refs_5_
  62.8 0.3 collective-permute-done.15.refs_6_
  63.1 0.7 %collective-permute-done.16.refs_7_ = s16[32,1024]{1,0:T(8,128)(2,1)S(1)} collective-permute-done((s16[32,1024]{1,0:T(8,128)(2,1)S(1)}, s16[32,1024]{1,0:T(8,128)(2,1)S(1)}, u32[]{:S(2)}, u32[]{:S(2)}) %collective-permute-start.16) | collective-permute-done | bytes 65568 | tf_op jit(solution)/shard_map/ppermute | solution.py:535
  63.8 1.2 %expand.1 = bf16[2048,128]{1,0:T(8,128)(2,1)} custom-call(f32[32,1024]{1,0:T(8,128)S(1)} %get-tuple-element.404.refs_0_, s16[32,1024]{1,0:T(8,128)(2,1)S(1)} %collective-permute-done.10.refs_1_, s16[32,1024]{1,0:T(8,128)(2,1)S(1)} %collective-permute-done.11.refs_2_, s16[32,1024]{1,0:T(8,128)(2,1)S(1)} %collective-permute-done.12.refs_3_, ...), custom_call_target="tpu_custom_call" | custom-call | tf_op jit(solution)/shard_map/expand/pallas_call | solution.py:455
  (21 shorter events, 0.1 us)
Async XLA Ops:
  1.4 15.0 %collective-permute-start.5 = (bf16[64,1024]{1,0:T(8,128)(2,1)S(1)}, bf16[64,1024]{1,0:T(8,128)(2,1)S(1)}, u32[]{:S(2)}, u32[]{:S(2)}) collective-permute-start(bf16[64,1024]{1,0:T(8,128)(2,1)S(1)} %get-tuple-element.389), channel_id=1, source_target_pairs={{0,2},{1,3},{2,4},{3,5},{4,6},{5,7},{6,0},{7,1},{8,10},{9,11},{10,... | collective-permute-start | bytes 393224 | tf_op jit(solution)/shard_map/ppermute | solution.py:466
  3.9 12.4 %collective-permute-start.6 = (bf16[64,1024]{1,0:T(8,128)(2,1)S(1)}, bf16[64,1024]{1,0:T(8,128)(2,1)S(1)}, u32[]{:S(2)}, u32[]{:S(2)}) collective-permute-start(bf16[64,1024]{1,0:T(8,128)(2,1)S(1)} %get-tuple-element.390), channel_id=1, source_target_pairs={{0,4},{1,5},{2,6},{3,7},{4,0},{5,1},{6,2},{7,3},{8,12},{9,13},{10,... | collective-permute-start | bytes 393224 | tf_op jit(solution)/shard_map/ppermute | solution.py:466
  7.2 9.1 %collective-permute-start.7 = (bf16[64,1024]{1,0:T(8,128)(2,1)S(1)}, bf16[64,1024]{1,0:T(8,128)(2,1)S(1)}, u32[]{:S(2)}, u32[]{:S(2)}) collective-permute-start(bf16[64,1024]{1,0:T(8,128)(2,1)S(1)} %get-tuple-element.391), channel_id=1, source_target_pairs={{0,6},{1,7},{2,0},{3,1},{4,2},{5,3},{6,4},{7,5},{8,14},{9,15},{10,... | collective-permute-start | bytes 393224 | tf_op jit(solution)/shard_map/ppermute | solution.py:466
  7.9 2.6 %collective-permute-start.4 = (s32[2,4096]{1,0:T(2,128)}, s32[2,4096]{1,0:T(2,128)S(1)}, u32[]{:S(2)}, u32[]{:S(2)}) collective-permute-start(s32[2,4096]{1,0:T(2,128)} %k_orbs.1), channel_id=1, source_target_pairs={{0,1},{1,0},{2,3},{3,2},{4,5},{5,4},{6,7},{7,6},{8,9},{9,8},{10,11... | collective-permute-start | bytes 98312 | tf_op jit(solution)/shard_map/ppermute | solution.py:468
  16.9 1.3 %collective-permute-start.8 = (bf16[176,128]{1,0:T(8,128)(2,1)S(1)}, bf16[176,128]{1,0:T(8,128)(2,1)S(1)}, u32[]{:S(2)}, u32[]{:S(2)}) collective-permute-start(bf16[176,128]{1,0:T(8,128)(2,1)S(1)} %get-tuple-element.397), channel_id=1, source_target_pairs={{0,1},{1,0},{2,3},{3,2},{4,5},{5,4},{6,7},{7,6},{8,9},{9,8},{10,11... | collective-permute-start | bytes 135176 | tf_op jit(solution)/shard_map/ppermute | solution.py:504
  49.2 5.0 %collective-permute-start.9 = (f32[4,32,1024]{2,1,0:T(8,128)S(1)}, f32[4,32,1024]{2,1,0:T(8,128)S(1)}, u32[]{:S(2)}, u32[]{:S(2)}) collective-permute-start(f32[4,32,1024]{2,1,0:T(8,128)S(1)} %get-tuple-element.403), channel_id=1, source_target_pairs={{0,1},{1,0},{2,3},{3,2},{4,5},{5,4},{6,7},{7,6},{8,9},{9,8},{10,11... | collective-permute-start | bytes 1572872 | tf_op jit(solution)/shard_map/ppermute | solution.py:528
  54.0 11.0 %copy-start = (bf16[256,1024]{1,0:T(8,128)(2,1)S(1)}, bf16[256,1024]{1,0:T(8,128)(2,1)}, u32[]{:S(2)}) copy-start(bf16[256,1024]{1,0:T(8,128)(2,1)} %amp_ref.1) | copy-start | bytes 1572868
  54.0 11.0 %copy-start.1 = (s32[2,4096]{1,0:T(2,128)S(1)}, s32[2,4096]{1,0:T(2,128)}, u32[]{:S(2)}) copy-start(s32[2,4096]{1,0:T(2,128)} %k_orbs.1) | copy-start | bytes 98308
  54.0 10.9 %copy-start.2 = (s32[2,2048]{1,0:T(2,128)S(1)}, s32[2,2048]{1,0:T(2,128)}, u32[]{:S(2)}) copy-start(s32[2,2048]{1,0:T(2,128)} %m_orbs.1) | copy-start | bytes 49156
  54.0 10.9 %copy-start.3 = (s32[2,1024]{1,0:T(2,128)S(1)}, s32[2,1024]{1,0:T(2,128)}, u32[]{:S(2)}) copy-start(s32[2,1024]{1,0:T(2,128)} %occ_orbs.1) | copy-start | bytes 24580
  54.0 10.9 %copy-start.4 = (s32[800]{0:T(1024)S(1)}, s32[800]{0:T(1024)}, u32[]{:S(2)}) copy-start(s32[800]{0:T(1024)} %param.16) | copy-start | bytes 9604
  54.0 10.9 %copy-start.5 = (s32[256]{0:T(256)S(1)}, s32[256]{0:T(256)}, u32[]{:S(2)}) copy-start(s32[256]{0:T(256)} %param.13) | copy-start | bytes 3076
  54.1 10.9 %copy-start.6 = (s32[100]{0:T(128)S(1)}, s32[100]{0:T(128)}, u32[]{:S(2)}) copy-start(s32[100]{0:T(128)} %param.15) | copy-start | bytes 1204
  54.1 3.6 %collective-permute-start.13 = (f32[4,32,1024]{2,1,0:T(8,128)S(1)}, f32[4,32,1024]{2,1,0:T(8,128)S(1)}, u32[]{:S(2)}, u32[]{:S(2)}) collective-permute-start(f32[4,32,1024]{2,1,0:T(8,128)S(1)} %get-tuple-element.411), channel_id=1, source_target_pairs={{0,1},{1,0},{2,3},{3,2},{4,5},{5,4},{6,7},{7,6},{8,9},{9,8},{10,11... | collective-permute-start | bytes 1572872 | tf_op jit(solution)/shard_map/ppermute | solution.py:528
  54.4 5.6 %collective-permute-start.10 = (s16[32,1024]{1,0:T(8,128)(2,1)S(1)}, s16[32,1024]{1,0:T(8,128)(2,1)S(1)}, u32[]{:S(2)}, u32[]{:S(2)}) collective-permute-start(s16[32,1024]{1,0:T(8,128)(2,1)S(1)} %get-tuple-element.405), channel_id=1, source_target_pairs={{0,2},{1,3},{2,4},{3,5},{4,6},{5,7},{6,0},{7,1},{8,10},{9,11},{10,... | collective-permute-start | bytes 196616 | tf_op jit(solution)/shard_map/ppermute | solution.py:535
  55.2 7.3 %collective-permute-start.11 = (s16[32,1024]{1,0:T(8,128)(2,1)S(1)}, s16[32,1024]{1,0:T(8,128)(2,1)S(1)}, u32[]{:S(2)}, u32[]{:S(2)}) collective-permute-start(s16[32,1024]{1,0:T(8,128)(2,1)S(1)} %get-tuple-element.406), channel_id=1, source_target_pairs={{0,4},{1,5},{2,6},{3,7},{4,0},{5,1},{6,2},{7,3},{8,12},{9,13},{10,... | collective-permute-start | bytes 196616 | tf_op jit(solution)/shard_map/ppermute | solution.py:535
  55.3 7.1 %collective-permute-start.12 = (s16[32,1024]{1,0:T(8,128)(2,1)S(1)}, s16[32,1024]{1,0:T(8,128)(2,1)S(1)}, u32[]{:S(2)}, u32[]{:S(2)}) collective-permute-start(s16[32,1024]{1,0:T(8,128)(2,1)S(1)} %get-tuple-element.407), channel_id=1, source_target_pairs={{0,6},{1,7},{2,0},{3,1},{4,2},{5,3},{6,4},{7,5},{8,14},{9,15},{10,... | collective-permute-start | bytes 196616 | tf_op jit(solution)/shard_map/ppermute | solution.py:535
  57.8 4.9 %collective-permute-start.14 = (s16[32,1024]{1,0:T(8,128)(2,1)S(1)}, s16[32,1024]{1,0:T(8,128)(2,1)S(1)}, u32[]{:S(2)}, u32[]{:S(2)}) collective-permute-start(s16[32,1024]{1,0:T(8,128)(2,1)S(1)} %get-tuple-element.413), channel_id=1, source_target_pairs={{0,2},{1,3},{2,4},{3,5},{4,6},{5,7},{6,0},{7,1},{8,10},{9,11},{10,... | collective-permute-start | bytes 196616 | tf_op jit(solution)/shard_map/ppermute | solution.py:535
  58.0 5.1 %collective-permute-start.15 = (s16[32,1024]{1,0:T(8,128)(2,1)S(1)}, s16[32,1024]{1,0:T(8,128)(2,1)S(1)}, u32[]{:S(2)}, u32[]{:S(2)}) collective-permute-start(s16[32,1024]{1,0:T(8,128)(2,1)S(1)} %get-tuple-element.414), channel_id=1, source_target_pairs={{0,4},{1,5},{2,6},{3,7},{4,0},{5,1},{6,2},{7,3},{8,12},{9,13},{10,... | collective-permute-start | bytes 196616 | tf_op jit(solution)/shard_map/ppermute | solution.py:535
  60.0 3.8 %collective-permute-start.16 = (s16[32,1024]{1,0:T(8,128)(2,1)S(1)}, s16[32,1024]{1,0:T(8,128)(2,1)S(1)}, u32[]{:S(2)}, u32[]{:S(2)}) collective-permute-start(s16[32,1024]{1,0:T(8,128)(2,1)S(1)} %get-tuple-element.415), channel_id=1, source_target_pairs={{0,6},{1,7},{2,0},{3,1},{4,2},{5,3},{6,4},{7,5},{8,14},{9,15},{10,... | collective-permute-start | bytes 196616 | tf_op jit(solution)/shard_map/ppermute | solution.py:535

commit v6 on v5

--- a/solution.py
+++ b/solution.py
@@ -68,8 +68,8 @@
 
 
 def symbols_kernel(
-    labels_ref, occ_orbs, k_orbs, m_orbs, other_orbs, int_ref,
-    occ_out, rank_out, place_out, from_out, k_out, m_out, own_out, other_out, early, bad_out, own_col, other_col, sem,
+    labels_ref, occ_orbs, k_orbs, other_orbs, int_ref,
+    occ_out, rank_out, place_out, from_out, k_out, own_out, other_out, early, bad_out, own_col, other_col, sem,
 ):
     core = lax.axis_index("col") & 1
     occ = pack_labels(labels_ref[7:8, :])
@@ -119,13 +119,6 @@
 
     lax.fori_loop(0, k_orbs.shape[1] // LANES, contracted, 0, unroll=8)
 
-    def output(n, carry):
-        start = pl.multiple_of(n * LANES, LANES)
-        m_out[pl.ds(start, LANES), :] = as_column(pair_symbols(virt, m_orbs, start)).astype(BF16)
-        return carry
-
-    lax.fori_loop(0, m_orbs.shape[1] // LANES, output, 0, unroll=8)
-
     i, j = iota((LANES, 2 * LANES), 0), iota((LANES, 2 * LANES), 1)
     pick = one_hot(j == (i >> 1) * 4 + core * 2 + (i & 1))
     mine = lax.axis_index("row") * 16
@@ -139,6 +132,17 @@
         column = jnp.concatenate([ref[pl.ds(r * far + at, 16), :] for r in range(16)], axis=0)
         out[...] = jnp.dot(pick, column, preferred_element_type=F32)
     pltpu.make_async_copy(int_ref.at[pl.ds(0, early.shape[0])], early, sem).wait()
+
+
+def outputs_kernel(labels_ref, m_orbs, m_out):
+    virt = pack_labels(labels_ref[0:7, :])
+
+    def output(n, carry):
+        start = pl.multiple_of(n * LANES, LANES)
+        m_out[pl.ds(start, LANES), :] = as_column(pair_symbols(virt, m_orbs, start)).astype(BF16)
+        return carry
+
+    lax.fori_loop(0, m_orbs.shape[1] // LANES, output, 0, unroll=8)
 
 
 def compact_kernel(a_ref, b_ref, c_ref, d_ref, own_ref, other_ref, occ_ref, place_ref, mine_out, theirs_out):
@@ -470,7 +474,7 @@
         [jnp.pad(virt_irrep, (0, 7 * LANES - virt_irrep.shape[0])), jnp.pad(occ_irrep, (0, LANES - occ_irrep.shape[0]))]
     ).reshape(8, LANES)
     half = m_dev // 2
-    occ_sym, rank, place, origin, k_sym, m_sym, own_sym, other_sym, early, bad = call(
+    occ_sym, rank, place, origin, k_sym, own_sym, other_sym, early, bad = call(
         symbols_kernel,
         "symbols",
         (
@@ -479,15 +483,14 @@
             shape((8, pairs), I32),
             shape((kblock, LANES), I32),
             shape((16, kblock), BF16),
-            shape((m_dev, LANES), BF16),
             shape((LANES, LANES), F32),
             shape((LANES, LANES), F32),
             shape((half, kblock), BF16),
             shape((1, 1), I32),
         ),
-        (labels, occ_orbs, k_orbs, m_orbs, other_orbs, integrals),
-        in_specs=[whole()] * 5 + [pl.BlockSpec(memory_space=pl.ANY)],
-        out_specs=(whole(),) * 9 + (scalars(),),
+        (labels, occ_orbs, k_orbs, other_orbs, integrals),
+        in_specs=[whole()] * 4 + [pl.BlockSpec(memory_space=pl.ANY)],
+        out_specs=(whole(),) * 8 + (scalars(),),
         scratch_shapes=[
             pltpu.VMEM((kblock, LANES), BF16),
             pltpu.VMEM((kblock // 2, LANES), BF16),
@@ -502,6 +505,9 @@
         (*arrived, own_sym, other_sym, occ_sym, place),
     )
     got = lax.ppermute(theirs, "col", swap)
+    later_labels, mine = lax.optimization_barrier((labels, mine))
+    m_sym = call(outputs_kernel, "outputs", shape((m_dev, LANES), BF16), (later_labels, m_orbs))
+    mine, m_sym = lax.optimization_barrier((mine, m_sym))
     spreading = jnp.broadcast_to(jnp.concatenate([mine, got], axis=1)[None], (rows, PLACES, stored))
     gathered = lax.all_to_all(spreading, "row", split_axis=0, concat_axis=0, tiled=True)
 

time: 66.2 us -> 66.4 us (level)
    pallas_call x8 -> x9, Pallas kernels: 16.2 us -> 16.8 us  [call(): pl.pallas_call(kernel, out_shape=out_shape, in_specs=kw.pop('in_specs', [...]
  transfers between devices with their start and end apart: 13 -> 13, of which waited for: 5 -> 4; matrix products, arithmetic and copies ran while one was open for 1% -> 1% of each run, Pallas kernels for 13% -> 14%
where the time goes in v6:
time: 66.4 us; the launch traced here: 65.3 us
  blocking collectives  26.3 us (40%)
  starting transfers between devices  18.4 us (28%)
  Pallas kernels  16.8 us (25%)
  waiting for transfers between devices  1.99 us (3%)
  between operations  1.01 us (2%)
  other arithmetic  0.72 us (1%)
    all_to_all x1, blocking collectives, body(): lax.all_to_all(spreading, 'row', split_axis=0, concat_axis=0, tiled=True)  26.3 us
    pallas_call x9, Pallas kernels, call(): pl.pallas_call(kernel, out_shape=out_shape, in_specs=kw.pop('in_specs', [...  16.8 us
    ppermute x6, starting transfers between devices, body(): lax.ppermute(shares[d], 'col', hops[d])  7.43 us
    ppermute x3, starting transfers between devices, body(): lax.ppermute(ordered[d], 'col', hops[d])  6.57 us
    ppermute x2, starting transfers between devices, body(): partner = lax.ppermute(send, 'col', swap)  2.46 us
    ppermute x1, starting transfers between devices, body(): other_orbs = lax.ppermute(k_orbs, 'col', swap)  1.52 us
    ppermute x6, waiting for transfers between devices, body(): lax.ppermute(shares[d], 'col', hops[d])  1.33 us
  transfers between devices with their start and end apart: 13, of which 4 were waited for; matrix products, arithmetic and copies ran while one was open for 1% of the time, Pallas kernels for 14%

profile of v6, /device:TPU:1, one launch (start us, length us, event | category | flops | bytes accessed | tf_op | source)
XLA Modules:
  0.0 65.3 jit_solution(9733257911070247059)
XLA Ops:
  0.0 1.4 %order.1 = (bf16[64,1024]{1,0:T(8,128)(2,1)S(1)}, bf16[64,1024]{1,0:T(8,128)(2,1)S(1)}, bf16[64,1024]{1,0:T(8,128)(2,1)S(1)}, bf16[64,1024]{1,0:T(8,128)(2,1)S(1)}) custom-call(s32[1,256]{1,0:T(1,128)} %bitcast.35, bf16[256,1024]{1,0:T(8,128)(2,1)} %amp_ref.1), custom_call_target="tpu_custom_call" | custom-call | tf_op jit(solution)/shard_map/order/pallas_call | solution.py:459
  1.4 2.5 %collective-permute-start.5 = (bf16[64,1024]{1,0:T(8,128)(2,1)S(1)}, bf16[64,1024]{1,0:T(8,128)(2,1)S(1)}, u32[]{:S(2)}, u32[]{:S(2)}) collective-permute-start(bf16[64,1024]{1,0:T(8,128)(2,1)S(1)} %get-tuple-element.392), channel_id=1, source_target_pairs={{0,2},{1,3},{2,4},{3,5},{4,6},{5,7},{6,0},{7,1},{8,10},{9,11},{10,... | collective-permute-start | bytes 393224 | tf_op jit(solution)/shard_map/ppermute | solution.py:470
  3.9 3.3 %collective-permute-start.6 = (bf16[64,1024]{1,0:T(8,128)(2,1)S(1)}, bf16[64,1024]{1,0:T(8,128)(2,1)S(1)}, u32[]{:S(2)}, u32[]{:S(2)}) collective-permute-start(bf16[64,1024]{1,0:T(8,128)(2,1)S(1)} %get-tuple-element.393), channel_id=1, source_target_pairs={{0,4},{1,5},{2,6},{3,7},{4,0},{5,1},{6,2},{7,3},{8,12},{9,13},{10,... | collective-permute-start | bytes 393224 | tf_op jit(solution)/shard_map/ppermute | solution.py:470
  7.2 0.7 %collective-permute-start.7 = (bf16[64,1024]{1,0:T(8,128)(2,1)S(1)}, bf16[64,1024]{1,0:T(8,128)(2,1)S(1)}, u32[]{:S(2)}, u32[]{:S(2)}) collective-permute-start(bf16[64,1024]{1,0:T(8,128)(2,1)S(1)} %get-tuple-element.394), channel_id=1, source_target_pairs={{0,6},{1,7},{2,0},{3,1},{4,2},{5,3},{6,4},{7,5},{8,14},{9,15},{10,... | collective-permute-start | bytes 393224 | tf_op jit(solution)/shard_map/ppermute | solution.py:470
  7.9 1.5 %collective-permute-start.4 = (s32[2,4096]{1,0:T(2,128)}, s32[2,4096]{1,0:T(2,128)S(1)}, u32[]{:S(2)}, u32[]{:S(2)}) collective-permute-start(s32[2,4096]{1,0:T(2,128)} %k_orbs.1), channel_id=1, source_target_pairs={{0,1},{1,0},{2,3},{3,2},{4,5},{5,4},{6,7},{7,6},{8,9},{9,8},{10,11... | collective-permute-start | bytes 98312 | tf_op jit(solution)/shard_map/ppermute | solution.py:472
  9.4 0.7 %fusion.2.labels_ref = s32[8,128]{1,0:T(8,128)S(1)} fusion(s32[100]{0:T(128)} %param.15, s32[800]{0:T(1024)} %param.16), kind=kLoop, calls=%fused_computation.22 | loop fusion | flops 1024 | bytes 7696 | tf_op jit(solution)/shard_map/reshape | solution.py:475
  10.2 0.4 collective-permute-done.4.other_orbs
  10.5 5.8 %symbols.1 = (s32[8,1024]{1,0:T(8,128)S(1)}, s32[8,1024]{1,0:T(8,128)S(1)}, s32[8,1024]{1,0:T(8,128)S(1)}, s32[4096,128]{1,0:T(8,128)S(1)}, bf16[16,4096]{1,0:T(...) custom-call(s32[8,128]{1,0:T(8,128)S(1)} %fusion.2.labels_ref, ...), custom_call_target="tpu_custom_call" | custom-call | tf_op jit(solution)/shard_map/symbols/pallas_call | solution.py:459
  16.4 0.6 compact.1
  17.0 0.4 collective-permute-start.8
  17.4 0.6 outputs.1.m_ref.refs_8_
  18.0 0.3 collective-permute-done.8
  18.3 0.1 broadcast_in_dim.2
  18.4 26.3 %all_to_all.22.amp_ref = bf16[16,176,256]{2,1,0:T(8,128)(2,1)S(1)} all-to-all(bf16[16,176,256]{2,1,0:T(8,128)(2,1)S(1)} %broadcast_in_dim.2), channel_id=1, replica_groups=mesh['row'=16,'col'=8] {'row'}, dimensions={0} | all-to-all | bytes 2883584 | tf_op jit(solution)/shard_map/all_to_all | solution.py:512
  44.7 4.6 %first.1 = (f32[4,32,1024]{2,1,0:T(8,128)S(1)}, f32[4,32,1024]{2,1,0:T(8,128)S(1)}, bf16[4096,256]{1,0:T(8,128)(2,1)S(1)}, bf16[1024,4096]{1,0:T(8,128)(2,1)S(1)}) custom-call(bf16[16,176,256]{2,1,0:T(8,128)(2,1)S(1)} %all_to_all.22.amp_ref, bf16[1024,4096]{1,0:T(8,128)(2,1)S(1)} %get-tuple-element.404.early, bf16[2048,4096]{1,0:T(8,128)(2,1)} %int_ref.3, ...), custom_call_target="tpu_custom_call" | custom-call | tf_op jit(solution)/shard_map/first/pallas_call | solution.py:459
  49.2 2.4 %collective-permute-start.9 = (f32[4,32,1024]{2,1,0:T(8,128)S(1)}, f32[4,32,1024]{2,1,0:T(8,128)S(1)}, u32[]{:S(2)}, u32[]{:S(2)}) collective-permute-start(f32[4,32,1024]{2,1,0:T(8,128)S(1)} %get-tuple-element.409), channel_id=1, source_target_pairs={{0,1},{1,0},{2,3},{3,2},{4,5},{5,4},{6,7},{7,6},{8,9},{9,8},{10,11... | collective-permute-start | bytes 1572872 | tf_op jit(solution)/shard_map/ppermute | solution.py:534
  51.6 2.4 %second.1 = (f32[4,32,1024]{2,1,0:T(8,128)S(1)}, f32[4,32,1024]{2,1,0:T(8,128)S(1)}) custom-call(bf16[1024,4096]{1,0:T(8,128)(2,1)S(1)} %get-tuple-element.414.int_ref, bf16[4096,256]{1,0:T(8,128)(2,1)S(1)} %get-tuple-element.415.kept_ref, bf16[16,4096]{1,0:T(8,128)(2,1)S(1)} %get-tuple-element.405.k_ref, bf16[2048,128]{1,0:T(8,128)(2,1)S(1)} %outputs.1.m_ref.refs_8_), custom_call_target="tpu_custom_call" | custom-call | flops 2147483648 | bytes 8388608 | tf_op jit(solution)/shard_map/second/pallas_call | solution.py:459
  54.0 0.0 copy-start
  54.0 0.0 copy-start.1
  54.0 0.0 copy-start.4
  54.1 0.1 collective-permute-start.13
  54.2 0.2 share.2
  54.4 0.8 %collective-permute-start.10 = (s16[32,1024]{1,0:T(8,128)(2,1)S(1)}, s16[32,1024]{1,0:T(8,128)(2,1)S(1)}, u32[]{:S(2)}, u32[]{:S(2)}) collective-permute-start(s16[32,1024]{1,0:T(8,128)(2,1)S(1)} %get-tuple-element.411), channel_id=1, source_target_pairs={{0,2},{1,3},{2,4},{3,5},{4,6},{5,7},{6,0},{7,1},{8,10},{9,11},{10,... | collective-permute-start | bytes 196616 | tf_op jit(solution)/shard_map/ppermute | solution.py:541
  55.2 0.2 collective-permute-start.11
  55.4 2.3 %collective-permute-start.12 = (s16[32,1024]{1,0:T(8,128)(2,1)S(1)}, s16[32,1024]{1,0:T(8,128)(2,1)S(1)}, u32[]{:S(2)}, u32[]{:S(2)}) collective-permute-start(s16[32,1024]{1,0:T(8,128)(2,1)S(1)} %get-tuple-element.413), channel_id=1, source_target_pairs={{0,6},{1,7},{2,0},{3,1},{4,2},{5,3},{6,4},{7,5},{8,14},{9,15},{10,... | collective-permute-start | bytes 196616 | tf_op jit(solution)/shard_map/ppermute | solution.py:541
  57.6 0.2 share.3
  57.8 0.3 collective-permute-start.14
  58.1 1.9 %collective-permute-start.15 = (s16[32,1024]{1,0:T(8,128)(2,1)S(1)}, s16[32,1024]{1,0:T(8,128)(2,1)S(1)}, u32[]{:S(2)}, u32[]{:S(2)}) collective-permute-start(s16[32,1024]{1,0:T(8,128)(2,1)S(1)} %get-tuple-element.420), channel_id=1, source_target_pairs={{0,4},{1,5},{2,6},{3,7},{4,0},{5,1},{6,2},{7,3},{8,12},{9,13},{10,... | collective-permute-start | bytes 196616 | tf_op jit(solution)/shard_map/ppermute | solution.py:541
  60.0 1.9 %collective-permute-start.16 = (s16[32,1024]{1,0:T(8,128)(2,1)S(1)}, s16[32,1024]{1,0:T(8,128)(2,1)S(1)}, u32[]{:S(2)}, u32[]{:S(2)}) collective-permute-start(s16[32,1024]{1,0:T(8,128)(2,1)S(1)} %get-tuple-element.421), channel_id=1, source_target_pairs={{0,6},{1,7},{2,0},{3,1},{4,2},{5,3},{6,4},{7,5},{8,14},{9,15},{10,... | collective-permute-start | bytes 196616 | tf_op jit(solution)/shard_map/ppermute | solution.py:541
  62.7 0.5 collective-permute-done.14.refs_5_
  63.1 0.9 %collective-permute-done.16.refs_7_ = s16[32,1024]{1,0:T(8,128)(2,1)S(1)} collective-permute-done((s16[32,1024]{1,0:T(8,128)(2,1)S(1)}, s16[32,1024]{1,0:T(8,128)(2,1)S(1)}, u32[]{:S(2)}, u32[]{:S(2)}) %collective-permute-start.16) | collective-permute-done | bytes 65568 | tf_op jit(solution)/shard_map/ppermute | solution.py:541
  64.0 1.2 %expand.1 = bf16[2048,128]{1,0:T(8,128)(2,1)} custom-call(f32[32,1024]{1,0:T(8,128)S(1)} %get-tuple-element.410.refs_0_, s16[32,1024]{1,0:T(8,128)(2,1)S(1)} %collective-permute-done.10.refs_1_, s16[32,1024]{1,0:T(8,128)(2,1)S(1)} %collective-permute-done.11.refs_2_, s16[32,1024]{1,0:T(8,128)(2,1)S(1)} %collective-permute-done.12.refs_3_, ...), custom_call_target="tpu_custom_call" | custom-call | tf_op jit(solution)/shard_map/expand/pallas_call | solution.py:459
  (22 shorter events, 0.1 us)
Async XLA Ops:
  1.4 15.0 %collective-permute-start.5 = (bf16[64,1024]{1,0:T(8,128)(2,1)S(1)}, bf16[64,1024]{1,0:T(8,128)(2,1)S(1)}, u32[]{:S(2)}, u32[]{:S(2)}) collective-permute-start(bf16[64,1024]{1,0:T(8,128)(2,1)S(1)} %get-tuple-element.392), channel_id=1, source_target_pairs={{0,2},{1,3},{2,4},{3,5},{4,6},{5,7},{6,0},{7,1},{8,10},{9,11},{10,... | collective-permute-start | bytes 393224 | tf_op jit(solution)/shard_map/ppermute | solution.py:470
  3.9 12.4 %collective-permute-start.6 = (bf16[64,1024]{1,0:T(8,128)(2,1)S(1)}, bf16[64,1024]{1,0:T(8,128)(2,1)S(1)}, u32[]{:S(2)}, u32[]{:S(2)}) collective-permute-start(bf16[64,1024]{1,0:T(8,128)(2,1)S(1)} %get-tuple-element.393), channel_id=1, source_target_pairs={{0,4},{1,5},{2,6},{3,7},{4,0},{5,1},{6,2},{7,3},{8,12},{9,13},{10,... | collective-permute-start | bytes 393224 | tf_op jit(solution)/shard_map/ppermute | solution.py:470
  7.2 9.2 %collective-permute-start.7 = (bf16[64,1024]{1,0:T(8,128)(2,1)S(1)}, bf16[64,1024]{1,0:T(8,128)(2,1)S(1)}, u32[]{:S(2)}, u32[]{:S(2)}) collective-permute-start(bf16[64,1024]{1,0:T(8,128)(2,1)S(1)} %get-tuple-element.394), channel_id=1, source_target_pairs={{0,6},{1,7},{2,0},{3,1},{4,2},{5,3},{6,4},{7,5},{8,14},{9,15},{10,... | collective-permute-start | bytes 393224 | tf_op jit(solution)/shard_map/ppermute | solution.py:470
  7.9 2.6 %collective-permute-start.4 = (s32[2,4096]{1,0:T(2,128)}, s32[2,4096]{1,0:T(2,128)S(1)}, u32[]{:S(2)}, u32[]{:S(2)}) collective-permute-start(s32[2,4096]{1,0:T(2,128)} %k_orbs.1), channel_id=1, source_target_pairs={{0,1},{1,0},{2,3},{3,2},{4,5},{5,4},{6,7},{7,6},{8,9},{9,8},{10,11... | collective-permute-start | bytes 98312 | tf_op jit(solution)/shard_map/ppermute | solution.py:472
  10.2 7.2 %copy-start.2 = (s32[2,2048]{1,0:T(2,128)S(1)}, s32[2,2048]{1,0:T(2,128)}, u32[]{:S(2)}) copy-start(s32[2,2048]{1,0:T(2,128)} %m_orbs.1) | copy-start | bytes 49156
  17.0 1.3 %collective-permute-start.8 = (bf16[176,128]{1,0:T(8,128)(2,1)S(1)}, bf16[176,128]{1,0:T(8,128)(2,1)S(1)}, u32[]{:S(2)}, u32[]{:S(2)}) collective-permute-start(bf16[176,128]{1,0:T(8,128)(2,1)S(1)} %get-tuple-element.403), channel_id=1, source_target_pairs={{0,1},{1,0},{2,3},{3,2},{4,5},{5,4},{6,7},{7,6},{8,9},{9,8},{10,11... | collective-permute-start | bytes 135176 | tf_op jit(solution)/shard_map/ppermute | solution.py:507
  49.2 4.9 %collective-permute-start.9 = (f32[4,32,1024]{2,1,0:T(8,128)S(1)}, f32[4,32,1024]{2,1,0:T(8,128)S(1)}, u32[]{:S(2)}, u32[]{:S(2)}) collective-permute-start(f32[4,32,1024]{2,1,0:T(8,128)S(1)} %get-tuple-element.409), channel_id=1, source_target_pairs={{0,1},{1,0},{2,3},{3,2},{4,5},{5,4},{6,7},{7,6},{8,9},{9,8},{10,11... | collective-permute-start | bytes 1572872 | tf_op jit(solution)/shard_map/ppermute | solution.py:534
  54.0 11.2 %copy-start = (bf16[256,1024]{1,0:T(8,128)(2,1)S(1)}, bf16[256,1024]{1,0:T(8,128)(2,1)}, u32[]{:S(2)}) copy-start(bf16[256,1024]{1,0:T(8,128)(2,1)} %amp_ref.1) | copy-start | bytes 1572868
  54.0 11.1 %copy-start.1 = (s32[2,4096]{1,0:T(2,128)S(1)}, s32[2,4096]{1,0:T(2,128)}, u32[]{:S(2)}) copy-start(s32[2,4096]{1,0:T(2,128)} %k_orbs.1) | copy-start | bytes 98308
  54.0 11.1 %copy-start.3 = (s32[2,1024]{1,0:T(2,128)S(1)}, s32[2,1024]{1,0:T(2,128)}, u32[]{:S(2)}) copy-start(s32[2,1024]{1,0:T(2,128)} %occ_orbs.1) | copy-start | bytes 24580
  54.0 11.1 %copy-start.4 = (s32[800]{0:T(1024)S(1)}, s32[800]{0:T(1024)}, u32[]{:S(2)}) copy-start(s32[800]{0:T(1024)} %param.16) | copy-start | bytes 9604
  54.0 11.1 %copy-start.5 = (s32[256]{0:T(256)S(1)}, s32[256]{0:T(256)}, u32[]{:S(2)}) copy-start(s32[256]{0:T(256)} %param.13) | copy-start | bytes 3076
  54.0 11.1 %copy-start.6 = (s32[100]{0:T(128)S(1)}, s32[100]{0:T(128)}, u32[]{:S(2)}) copy-start(s32[100]{0:T(128)} %param.15) | copy-start | bytes 1204
  54.1 3.6 %collective-permute-start.13 = (f32[4,32,1024]{2,1,0:T(8,128)S(1)}, f32[4,32,1024]{2,1,0:T(8,128)S(1)}, u32[]{:S(2)}, u32[]{:S(2)}) collective-permute-start(f32[4,32,1024]{2,1,0:T(8,128)S(1)} %get-tuple-element.417), channel_id=1, source_target_pairs={{0,1},{1,0},{2,3},{3,2},{4,5},{5,4},{6,7},{7,6},{8,9},{9,8},{10,11... | collective-permute-start | bytes 1572872 | tf_op jit(solution)/shard_map/ppermute | solution.py:534
  54.4 5.7 %collective-permute-start.10 = (s16[32,1024]{1,0:T(8,128)(2,1)S(1)}, s16[32,1024]{1,0:T(8,128)(2,1)S(1)}, u32[]{:S(2)}, u32[]{:S(2)}) collective-permute-start(s16[32,1024]{1,0:T(8,128)(2,1)S(1)} %get-tuple-element.411), channel_id=1, source_target_pairs={{0,2},{1,3},{2,4},{3,5},{4,6},{5,7},{6,0},{7,1},{8,10},{9,11},{10,... | collective-permute-start | bytes 196616 | tf_op jit(solution)/shard_map/ppermute | solution.py:541
  55.2 7.5 %collective-permute-start.11 = (s16[32,1024]{1,0:T(8,128)(2,1)S(1)}, s16[32,1024]{1,0:T(8,128)(2,1)S(1)}, u32[]{:S(2)}, u32[]{:S(2)}) collective-permute-start(s16[32,1024]{1,0:T(8,128)(2,1)S(1)} %get-tuple-element.412), channel_id=1, source_target_pairs={{0,4},{1,5},{2,6},{3,7},{4,0},{5,1},{6,2},{7,3},{8,12},{9,13},{10,... | collective-permute-start | bytes 196616 | tf_op jit(solution)/shard_map/ppermute | solution.py:541
  55.4 7.3 %collective-permute-start.12 = (s16[32,1024]{1,0:T(8,128)(2,1)S(1)}, s16[32,1024]{1,0:T(8,128)(2,1)S(1)}, u32[]{:S(2)}, u32[]{:S(2)}) collective-permute-start(s16[32,1024]{1,0:T(8,128)(2,1)S(1)} %get-tuple-element.413), channel_id=1, source_target_pairs={{0,6},{1,7},{2,0},{3,1},{4,2},{5,3},{6,4},{7,5},{8,14},{9,15},{10,... | collective-permute-start | bytes 196616 | tf_op jit(solution)/shard_map/ppermute | solution.py:541
  57.8 5.3 %collective-permute-start.14 = (s16[32,1024]{1,0:T(8,128)(2,1)S(1)}, s16[32,1024]{1,0:T(8,128)(2,1)S(1)}, u32[]{:S(2)}, u32[]{:S(2)}) collective-permute-start(s16[32,1024]{1,0:T(8,128)(2,1)S(1)} %get-tuple-element.419), channel_id=1, source_target_pairs={{0,2},{1,3},{2,4},{3,5},{4,6},{5,7},{6,0},{7,1},{8,10},{9,11},{10,... | collective-permute-start | bytes 196616 | tf_op jit(solution)/shard_map/ppermute | solution.py:541
  58.1 5.0 %collective-permute-start.15 = (s16[32,1024]{1,0:T(8,128)(2,1)S(1)}, s16[32,1024]{1,0:T(8,128)(2,1)S(1)}, u32[]{:S(2)}, u32[]{:S(2)}) collective-permute-start(s16[32,1024]{1,0:T(8,128)(2,1)S(1)} %get-tuple-element.420), channel_id=1, source_target_pairs={{0,4},{1,5},{2,6},{3,7},{4,0},{5,1},{6,2},{7,3},{8,12},{9,13},{10,... | collective-permute-start | bytes 196616 | tf_op jit(solution)/shard_map/ppermute | solution.py:541
  60.0 3.9 %collective-permute-start.16 = (s16[32,1024]{1,0:T(8,128)(2,1)S(1)}, s16[32,1024]{1,0:T(8,128)(2,1)S(1)}, u32[]{:S(2)}, u32[]{:S(2)}) collective-permute-start(s16[32,1024]{1,0:T(8,128)(2,1)S(1)} %get-tuple-element.421), channel_id=1, source_target_pairs={{0,6},{1,7},{2,0},{3,1},{4,2},{5,3},{6,4},{7,5},{8,14},{9,15},{10,... | collective-permute-start | bytes 196616 | tf_op jit(solution)/shard_map/ppermute | solution.py:541
